TPU v7x, 32 devices: a whole 2x2x4 slice. The times are simulated.
32 devices in a mesh: seq: 8 (over z, x), blk: 4 (over y, core).
Axes of the slice: x: 2, y: 2, z: 4, core: 2. Of those that a mesh axis runs over, the one named last changes fastest.
Arguments:
- tokens: bfloat16 [1024, 4, 512], P('seq', 'blk'), may hold values from -6 to 6
- lengths: int32 [4, 8], replicated, may hold values from 0 to 1024, as said below
- norm_gain: float32 [2, 512], replicated, may hold values from 0.5 to 1.5
- in_proj: bfloat16 [2, 512, 2, 384], replicated, may hold values from -0.25 to 0.25
- out_proj: bfloat16 [2, 2, 384, 512], replicated, may hold values from -1.25 to 1.25
- skip_gain: float32 [2, 512], replicated, may hold values from -1 to 1
- glu_weight: bfloat16 [2, 512, 512], replicated, may hold values from -0.25 to 0.25
- glu_bias: float32 [2, 512], replicated, may hold values from -3 to 3
- decay_log: float32 [2, 384], replicated, may hold values from -3.9 to 0
- frequency: float32 [2, 384], replicated, may hold values from -30 to 30
- step_log: float32 [2, 384], replicated, may hold values from -6.9 to -3
- cotangent: bfloat16 [1024, 4, 512], P('seq', 'blk'), may hold values from -6 to 6
Outputs:
- activations: bfloat16 [1024, 4, 512], P('seq', 'blk')
- tokens_grad: float32 [1024, 4, 512], P('seq', 'blk')
- norm_gain_grad: float32 [2, 512], P(None, ('seq', 'blk'))
- in_proj_grad: float32 [2, 512, 2, 384], P(None, ('seq', 'blk'))
- out_proj_grad: float32 [2, 2, 384, 512], P(None, None, None, ('seq', 'blk'))
- skip_gain_grad: float32 [2, 512], P(None, ('seq', 'blk'))
- glu_weight_grad: float32 [2, 512, 512], P(None, ('seq', 'blk'))
- glu_bias_grad: float32 [2, 512], P(None, ('seq', 'blk'))
- decay_log_grad: float32 [2, 384], replicated
- frequency_grad: float32 [2, 384], replicated
- step_log_grad: float32 [2, 384], replicated
Inputs may be any that keep to these rules, and one draw needn't show every extreme that they name: `lengths`: each row sums to 1024. In one row, chosen by the seed, the first item fills the whole stream and the others are empty; every other row holds 8 items of 64 to 192 positions each, in random order.
All inputs are finite; a program needn't handle non-finite values.
Results may differ from a plain program's by a relative error of at most 0.015.
Values may be sent and summed in bfloat16 or wider, within the bound.
A program may use at most 192 MiB of HBM per device.

v0:
```python
import jax
import jax.numpy as jnp
from jax import lax
from jax.sharding import PartitionSpec as P

EPS = 1e-06


def prefix(value, axis, join, neutral, backward):
    count, mine = (lax.axis_size(axis), lax.axis_index(axis))
    pieces = jax.tree.map(lambda part: lax.all_gather(part, axis), value)
    if backward:
        pieces = jax.tree.map(lambda part: part[::-1], pieces)
        mine = count - 1 - mine
    subtotal = jax.tree.map(
        lambda part, zero: jnp.full_like(part, 0) + jnp.asarray(zero, part.dtype), value, neutral
    )

    def step(position, subtotal):
        longer = join(subtotal, jax.tree.map(lambda part: part[position], pieces))
        return jax.tree.map(lambda new, old: jnp.where(position < mine, new, old), longer, subtotal)

    return lax.fori_loop(0, count - 1, step, subtotal)


def combine(earlier, later):
    prior_re, prior_im, prior_sre, prior_sim = earlier
    next_re, next_im, next_sre, next_sim = later
    return (
        next_re * prior_re - next_im * prior_im,
        next_re * prior_im + next_im * prior_re,
        next_re * prior_sre - next_im * prior_sim + next_sre,
        next_re * prior_sim + next_im * prior_sre + next_sim,
    )


def discretize(decay_vec, freq_vec, step_vec):
    lam_re = -jnp.exp(decay_vec)
    step_size = jnp.exp(step_vec)
    rotation = freq_vec * step_size
    shrink = jnp.expm1(lam_re * step_size)
    cosine = jnp.cos(rotation)
    sine_part = jnp.sin(rotation)
    magnitude = shrink + 1.0
    bar_re = magnitude * cosine
    bar_im = magnitude * sine_part
    minus_re = shrink * cosine - 2.0 * jnp.sin(0.5 * rotation) ** 2
    denominator = lam_re * lam_re + freq_vec * freq_vec
    coef_re = (minus_re * lam_re + bar_im * freq_vec) / denominator
    coef_im = (bar_im * lam_re - minus_re * freq_vec) / denominator
    return (bar_re, bar_im, coef_re, coef_im)


def normalize(values, gain_vec):
    inv_scale = lax.rsqrt(jnp.mean(values * values, axis=-1, keepdims=True) + EPS)
    return values * inv_scale * gain_vec


def local_block(vector):
    count = vector.shape[0] // lax.axis_size("blk")
    return lax.dynamic_slice_in_dim(vector, lax.axis_index("blk") * count, count, 0)


def to_states(pair_low):
    moved = lax.all_to_all(pair_low, "blk", split_axis=1, concat_axis=2, tiled=True)
    return moved.reshape(2, moved.shape[1], lax.axis_size("blk"), pair_low.shape[2])


def to_time(state_low):
    flat = state_low.reshape(2, state_low.shape[1], -1)
    return lax.all_to_all(flat, "blk", split_axis=2, concat_axis=1, tiled=True)


def drive(coef_re, coef_im, state_in):
    proj_re = state_in[0].astype(jnp.float32)
    proj_im = state_in[1].astype(jnp.float32)
    scale_re = coef_re[:, None, None]
    scale_im = coef_im[:, None, None]
    return (scale_re * proj_re - scale_im * proj_im, scale_re * proj_im + scale_im * proj_re)


def recurrence(bar_re, bar_im, keep_mask, drive_re, drive_im, backward, carried):
    pieces = (
        bar_re[:, None, None] * keep_mask,
        bar_im[:, None, None] * keep_mask,
        drive_re,
        drive_im,
    )
    if backward:
        pieces = tuple((jnp.flip(piece, 2) for piece in pieces))
    prod_re, prod_im, local_re, local_im = lax.associative_scan(combine, pieces, axis=2)
    if carried is None:
        summary = (prod_re[:, :, -1], prod_im[:, :, -1], local_re[:, :, -1], local_im[:, :, -1])
        blank = jnp.zeros_like(summary[0])
        unit = (jnp.ones_like(summary[0]), blank, blank, blank)
        before = prefix(summary, "seq", combine, unit, backward)
        carried = (before[2], before[3])
    carry_re = carried[0][:, :, None]
    carry_im = carried[1][:, :, None]
    state_re = local_re + prod_re * carry_re - prod_im * carry_im
    state_im = local_im + prod_re * carry_im + prod_im * carry_re
    if backward:
        state_re, state_im = (jnp.flip(state_re, 2), jnp.flip(state_im, 2))
    return (state_re, state_im, carried)


def layer_forward(layer_in, weights, keep_mask, backward):
    (
        gain_vec,
        in_weight,
        out_weight,
        skip_vec,
        glu_matrix,
        glu_shift,
        decay_vec,
        freq_vec,
        step_vec,
    ) = weights
    normed = normalize(layer_in, gain_vec)
    proj_low = jnp.einsum(
        "th,hcp->cpt", normed.astype(jnp.bfloat16), in_weight, preferred_element_type=jnp.float32
    ).astype(jnp.bfloat16)
    state_in = to_states(proj_low)
    bar_re, bar_im, coef_re, coef_im = discretize(
        local_block(decay_vec), local_block(freq_vec), local_block(step_vec)
    )
    drive_re, drive_im = drive(coef_re, coef_im, state_in)
    state_re, state_im, carried = recurrence(
        bar_re, bar_im, keep_mask, drive_re, drive_im, backward, None
    )
    state_low = to_time(jnp.stack([state_re, state_im]).astype(jnp.bfloat16))
    mixed = (
        jnp.einsum("cpt,cph->th", state_low, out_weight, preferred_element_type=jnp.float32)
        + skip_vec * normed
    )
    activated = jax.nn.gelu(mixed)
    gate_pre = (
        jnp.dot(activated.astype(jnp.bfloat16), glu_matrix, preferred_element_type=jnp.float32)
        + glu_shift
    )
    layer_out = layer_in + activated * jax.nn.sigmoid(gate_pre)
    return (layer_out, (state_in, carried, state_low, mixed, gate_pre))


def layer_backward(layer_in, weights, keep_mask, adjoint_mask, backward, saved, out_grad):
    (
        gain_vec,
        in_weight,
        out_weight,
        skip_vec,
        glu_matrix,
        glu_shift,
        decay_vec,
        freq_vec,
        step_vec,
    ) = weights
    state_in, carried, state_low, mixed, gate_pre = saved
    normed, norm_pull = jax.vjp(normalize, layer_in, gain_vec)
    normed_low = normed.astype(jnp.bfloat16)
    activated, gelu_pull = jax.vjp(jax.nn.gelu, mixed)
    gate_open = jax.nn.sigmoid(gate_pre)
    gate_grad = (out_grad * activated * gate_open * (1.0 - gate_open)).astype(jnp.bfloat16)
    glu_bias_grad = jnp.sum(gate_grad.astype(jnp.float32), axis=0)
    glu_weight_grad = jnp.einsum(
        "th,tk->hk", activated.astype(jnp.bfloat16), gate_grad, preferred_element_type=jnp.float32
    )
    act_grad = out_grad * gate_open + jnp.einsum(
        "tk,hk->th", gate_grad, glu_matrix, preferred_element_type=jnp.float32
    )
    mixed_grad = gelu_pull(act_grad)[0].astype(jnp.bfloat16)
    mixed_wide = mixed_grad.astype(jnp.float32)
    skip_grad = jnp.sum(mixed_wide * normed, axis=0)
    out_weight_grad = jnp.einsum(
        "cpt,th->cph", state_low, mixed_grad, preferred_element_type=jnp.float32
    )
    state_grad = to_states(
        jnp.einsum(
            "th,cph->cpt", mixed_grad, out_weight, preferred_element_type=jnp.float32
        ).astype(jnp.bfloat16)
    )

    def discrete(decay_all, freq_all, step_all):
        return discretize(local_block(decay_all), local_block(freq_all), local_block(step_all))

    (bar_re, bar_im, coef_re, coef_im), disc_pull = jax.vjp(discrete, decay_vec, freq_vec, step_vec)
    drive_re, drive_im = drive(coef_re, coef_im, state_in)
    state_re, state_im, unused = recurrence(
        bar_re, bar_im, keep_mask, drive_re, drive_im, backward, carried
    )
    adjoint_re, adjoint_im, unused = recurrence(
        bar_re,
        -bar_im,
        adjoint_mask,
        state_grad[0].astype(jnp.float32),
        state_grad[1].astype(jnp.float32),
        not backward,
        None,
    )
    edge_re = carried[0][:, :, None]
    edge_im = carried[1][:, :, None]
    if backward:
        prev_re = jnp.concatenate([state_re[:, :, 1:], edge_re], axis=2)
        prev_im = jnp.concatenate([state_im[:, :, 1:], edge_im], axis=2)
    else:
        prev_re = jnp.concatenate([edge_re, state_re[:, :, :-1]], axis=2)
        prev_im = jnp.concatenate([edge_im, state_im[:, :, :-1]], axis=2)
    bar_grad_re = jnp.sum(keep_mask * (adjoint_re * prev_re + adjoint_im * prev_im), axis=(1, 2))
    bar_grad_im = jnp.sum(keep_mask * (adjoint_im * prev_re - adjoint_re * prev_im), axis=(1, 2))
    proj_re = state_in[0].astype(jnp.float32)
    proj_im = state_in[1].astype(jnp.float32)
    coef_grad_re = jnp.sum(adjoint_re * proj_re + adjoint_im * proj_im, axis=(1, 2))
    coef_grad_im = jnp.sum(adjoint_im * proj_re - adjoint_re * proj_im, axis=(1, 2))
    decay_grad, freq_grad, step_grad = disc_pull(
        (bar_grad_re, bar_grad_im, coef_grad_re, coef_grad_im)
    )
    scale_re = coef_re[:, None, None]
    scale_im = coef_im[:, None, None]
    drive_grad = jnp.stack(
        [
            scale_re * adjoint_re + scale_im * adjoint_im,
            scale_re * adjoint_im - scale_im * adjoint_re,
        ]
    ).astype(jnp.bfloat16)
    proj_grad = to_time(drive_grad)
    in_weight_grad = jnp.einsum(
        "th,cpt->hcp", normed_low, proj_grad, preferred_element_type=jnp.float32
    )
    normed_grad = (
        jnp.einsum("cpt,hcp->th", proj_grad, in_weight, preferred_element_type=jnp.float32)
        + skip_vec * mixed_wide
    )
    input_grad, gain_grad = norm_pull(normed_grad)
    state_totals = lax.psum((decay_grad, freq_grad, step_grad), ("seq", "blk"))
    weight_totals = (
        lax.psum_scatter(in_weight_grad, ("seq", "blk"), scatter_dimension=0, tiled=True),
        lax.psum_scatter(out_weight_grad, ("seq", "blk"), scatter_dimension=2, tiled=True),
        lax.psum_scatter(glu_weight_grad, ("seq", "blk"), scatter_dimension=0, tiled=True),
        lax.psum_scatter(gain_grad, ("seq", "blk"), scatter_dimension=0, tiled=True),
        lax.psum_scatter(skip_grad, ("seq", "blk"), scatter_dimension=0, tiled=True),
        lax.psum_scatter(glu_bias_grad, ("seq", "blk"), scatter_dimension=0, tiled=True),
    )
    return (out_grad + input_grad, tuple(weight_totals) + tuple(state_totals))


def on_device(
    tokens,
    lengths,
    norm_gain,
    in_proj,
    out_proj,
    skip_gain,
    glu_weight,
    glu_bias,
    decay_log,
    frequency,
    step_log,
    cotangent,
):
    shard_rows = tokens.shape[0]
    position = lax.axis_index("seq") * shard_rows + jnp.arange(shard_rows, dtype=jnp.int32)
    item_ends = jnp.cumsum(lengths, axis=1)
    item_starts = item_ends - lengths
    start_hit = jnp.any(position[None, :, None] == item_starts[:, None, :], axis=2)
    end_hit = jnp.any(position[None, :, None] == (item_ends - 1)[:, None, :], axis=2)
    keep_start = 1.0 - start_hit.astype(jnp.float32)
    keep_end = 1.0 - end_hit.astype(jnp.float32)
    params = (
        norm_gain,
        in_proj,
        out_proj,
        skip_gain,
        glu_weight,
        glu_bias,
        decay_log,
        frequency,
        step_log,
    )
    first_weights = tuple((param[0] for param in params))
    second_weights = tuple((param[1] for param in params))
    layer_in = tokens[:, 0, :].astype(jnp.float32)
    middle, first_saved = layer_forward(layer_in, first_weights, keep_start, False)
    layer_out, second_saved = layer_forward(middle, second_weights, keep_end, True)
    middle_grad, second_grads = layer_backward(
        middle,
        second_weights,
        keep_end,
        keep_start,
        True,
        second_saved,
        cotangent[:, 0, :].astype(jnp.float32),
    )
    input_grad, first_grads = layer_backward(
        layer_in, first_weights, keep_start, keep_end, False, first_saved, middle_grad
    )
    stacked = tuple(
        (
            jnp.stack([first_part, second_part])
            for first_part, second_part in zip(first_grads, second_grads)
        )
    )
    return (
        layer_out[:, None, :].astype(jnp.bfloat16),
        input_grad[:, None, :],
        stacked[3],
        stacked[0],
        stacked[1],
        stacked[4],
        stacked[2],
        stacked[5],
        stacked[6],
        stacked[7],
        stacked[8],
    )


def solution(mesh):
    return jax.shard_map(
        on_device,
        mesh=mesh,
        in_specs=(
            P("seq", "blk", None),
            P(),
            P(),
            P(),
            P(),
            P(),
            P(),
            P(),
            P(),
            P(),
            P(),
            P("seq", "blk", None),
        ),
        out_specs=(
            P("seq", "blk", None),
            P("seq", "blk", None),
            P(None, ("seq", "blk")),
            P(None, ("seq", "blk"), None, None),
            P(None, None, None, ("seq", "blk")),
            P(None, ("seq", "blk")),
            P(None, ("seq", "blk"), None),
            P(None, ("seq", "blk")),
            P(),
            P(),
            P(),
        ),
        check_vma=False,
    )
```

profile of v0, /device:TPU:0, one launch (start us, length us, event | category | flops | bytes accessed | tf_op | source)
XLA Modules:
  0.0 1786.3 jit_solution(14171633769263351071)
XLA Ops:
  158.4 32.2 %all-gather.3 = f32[768,4,1]{1,2,0:T(1,128)S(1)} all-gather(f32[96,4,1]{1,2,0:T(1,128)S(1)} %copy.1134), channel_id=5, replica_groups=mesh['seq'=8,'blk'=4] {'seq'}, dimensions={0}, use_global_device_ids=true | all-gather | bytes 13824 | tf_op jit(solution)/shard_map/all_gather | solution.py:11
  193.2 31.0 %all-gather.2 = f32[768,4,1]{1,2,0:T(1,128)S(1)} all-gather(f32[96,4,1]{1,2,0:T(1,128)S(1)} %copy.1132), channel_id=4, replica_groups=mesh['seq'=8,'blk'=4] {'seq'}, dimensions={0}, use_global_device_ids=true | all-gather | bytes 13824 | tf_op jit(solution)/shard_map/all_gather | solution.py:11
  226.7 22.2 %pad.853 = f32[96,4,128]{0,1,2:T(4,128)S(1)} pad(f32[96,4,64]{0,1,2:T(4,128)} %add.2138, f32[]{:T(128)} %constant.139.clone.1), padding=0_0_0x0_0_0x1_0_1 | pad | bytes 294916 | tf_op jit(solution)/shard_map/pad | solution.py:91
  250.3 31.3 %all-gather.1 = f32[768,4,1]{1,2,0:T(1,128)S(1)} all-gather(f32[96,4,1]{1,2,0:T(1,128)} %copy.1130), channel_id=3, replica_groups=mesh['seq'=8,'blk'=4] {'seq'}, dimensions={0}, use_global_device_ids=true | all-gather | bytes 13824 | tf_op jit(solution)/shard_map/all_gather | solution.py:11
  284.2 19.6 %pad.851 = f32[96,4,128]{0,1,2:T(4,128)} pad(f32[96,4,64]{0,1,2:T(4,128)S(1)} %add.2136, f32[]{:T(128)} %constant.139.clone.1), padding=0_0_0x0_0_0x1_0_1 | pad | bytes 294916 | tf_op jit(solution)/shard_map/pad | solution.py:91
  304.6 31.2 %all-gather = f32[768,4,1]{1,2,0:T(1,128)S(1)} all-gather(f32[96,4,1]{1,2,0:T(1,128)S(1)} %copy.1128), channel_id=2, replica_groups=mesh['seq'=8,'blk'=4] {'seq'}, dimensions={0}, use_global_device_ids=true | all-gather | bytes 13824 | tf_op jit(solution)/shard_map/all_gather | solution.py:11
  507.3 14.8 pad.903
  539.2 21.9 %pad.911 = f32[96,4,128]{0,1,2:T(4,128)S(1)} pad(f32[96,4,64]{0,1,2:T(4,128)} %add.2214, f32[]{:T(128)} %constant.139.clone.1), padding=0_0_0x0_0_0x1_0_1 | pad | bytes 294916 | tf_op jit(solution)/shard_map/pad | solution.py:91
  561.9 31.1 %all-gather.7 = f32[768,4,1]{1,2,0:T(1,128)S(1)} all-gather(f32[96,4,1]{1,2,0:T(1,128)S(1)} %copy.1157), channel_id=9, replica_groups=mesh['seq'=8,'blk'=4] {'seq'}, dimensions={0}, use_global_device_ids=true | all-gather | bytes 13824 | tf_op jit(solution)/shard_map/all_gather | solution.py:11
  595.7 22.2 %pad.880 = f32[96,4,128]{0,1,2:T(4,128)S(1)} pad(f32[96,4,64]{0,1,2:T(4,128)} %pad_maximum_fusion.12, f32[]{:T(128)} %constant.139.clone.1), padding=0_0_0x0_0_0x0_1_1 | pad | bytes 294916 | tf_op jit(solution)/shard_map/pad | solution.py:91
  618.7 31.0 %all-gather.6 = f32[768,4,1]{1,2,0:T(1,128)S(1)} all-gather(f32[96,4,1]{1,2,0:T(1,128)S(1)} %copy.1155), channel_id=8, replica_groups=mesh['seq'=8,'blk'=4] {'seq'}, dimensions={0}, use_global_device_ids=true | all-gather | bytes 13824 | tf_op jit(solution)/shard_map/all_gather | solution.py:11
  652.3 22.0 %pad.909 = f32[96,4,128]{0,1,2:T(4,128)S(1)} pad(f32[96,4,64]{0,1,2:T(4,128)} %add.2234, f32[]{:T(128)} %constant.139.clone.1), padding=0_0_0x0_0_0x1_0_1 | pad | bytes 294916 | tf_op jit(solution)/shard_map/pad | solution.py:91
  675.0 31.0 %all-gather.5 = f32[768,4,1]{1,2,0:T(1,128)S(1)} all-gather(f32[96,4,1]{1,2,0:T(1,128)S(1)} %copy.1153), channel_id=7, replica_groups=mesh['seq'=8,'blk'=4] {'seq'}, dimensions={0}, use_global_device_ids=true | all-gather | bytes 13824 | tf_op jit(solution)/shard_map/all_gather | solution.py:11
  708.6 21.9 %pad.907 = f32[96,4,128]{0,1,2:T(4,128)S(1)} pad(f32[96,4,64]{0,1,2:T(4,128)} %add.2232, f32[]{:T(128)} %constant.139.clone.1), padding=0_0_0x0_0_0x1_0_1 | pad | bytes 294916 | tf_op jit(solution)/shard_map/pad | solution.py:91
  731.3 31.0 %all-gather.4 = f32[768,4,1]{1,2,0:T(1,128)S(1)} all-gather(f32[96,4,1]{1,2,0:T(1,128)S(1)} %copy.1151), channel_id=6, replica_groups=mesh['seq'=8,'blk'=4] {'seq'}, dimensions={0}, use_global_device_ids=true | all-gather | bytes 13824 | tf_op jit(solution)/shard_map/all_gather | solution.py:11
  939.0 14.6 pad.932
  953.5 14.8 pad.933
  1016.2 21.7 %pad.967 = f32[96,4,128]{0,1,2:T(4,128)S(1)} pad(f32[96,4,64]{0,1,2:T(4,128)} %add.2306, f32[]{:T(128)} %constant.139.clone.1), padding=0_0_0x0_0_0x1_0_1 | pad | bytes 294916 | tf_op jit(solution)/shard_map/pad | solution.py:91
  1038.7 31.5 %all-gather.11 = f32[768,4,1]{1,2,0:T(1,128)S(1)} all-gather(f32[96,4,1]{1,2,0:T(1,128)} %copy.1178), channel_id=13, replica_groups=mesh['seq'=8,'blk'=4] {'seq'}, dimensions={0}, use_global_device_ids=true | all-gather | bytes 13824 | tf_op jit(solution)/shard_map/all_gather | solution.py:11
  1073.5 31.0 %all-gather.10 = f32[768,4,1]{1,2,0:T(1,128)S(1)} all-gather(f32[96,4,1]{1,2,0:T(1,128)S(1)} %copy.1176), channel_id=12, replica_groups=mesh['seq'=8,'blk'=4] {'seq'}, dimensions={0}, use_global_device_ids=true | all-gather | bytes 13824 | tf_op jit(solution)/shard_map/all_gather | solution.py:11
  1107.0 21.8 %pad.965 = f32[96,4,128]{0,1,2:T(4,128)S(1)} pad(f32[96,4,64]{0,1,2:T(4,128)} %add.2326, f32[]{:T(128)} %constant.139.clone.1), padding=0_0_0x0_0_0x1_0_1 | pad | bytes 294916 | tf_op jit(solution)/shard_map/pad | solution.py:91
  1129.7 31.1 %all-gather.9 = f32[768,4,1]{1,2,0:T(1,128)S(1)} all-gather(f32[96,4,1]{1,2,0:T(1,128)S(1)} %copy.1174), channel_id=11, replica_groups=mesh['seq'=8,'blk'=4] {'seq'}, dimensions={0}, use_global_device_ids=true | all-gather | bytes 13824 | tf_op jit(solution)/shard_map/all_gather | solution.py:11
  1163.4 21.9 %pad.963 = f32[96,4,128]{0,1,2:T(4,128)S(1)} pad(f32[96,4,64]{0,1,2:T(4,128)} %add.2324, f32[]{:T(128)} %constant.139.clone.1), padding=0_0_0x0_0_0x1_0_1 | pad | bytes 294916 | tf_op jit(solution)/shard_map/pad | solution.py:91
  1186.8 31.0 %all-gather.8 = f32[768,4,1]{1,2,0:T(1,128)S(1)} all-gather(f32[96,4,1]{1,2,0:T(1,128)S(1)} %copy.1172), channel_id=10, replica_groups=mesh['seq'=8,'blk'=4] {'seq'}, dimensions={0}, use_global_device_ids=true | all-gather | bytes 13824 | tf_op jit(solution)/shard_map/all_gather | solution.py:11
  1271.5 31.2 %all-gather.15 = f32[768,4,1]{1,2,0:T(1,128)S(1)} all-gather(f32[96,4,1]{1,2,0:T(1,128)S(1)} %copy.1199), channel_id=17, replica_groups=mesh['seq'=8,'blk'=4] {'seq'}, dimensions={0}, use_global_device_ids=true | all-gather | bytes 13824 | tf_op jit(solution)/shard_map/all_gather | solution.py:11
  1304.7 31.1 %all-gather.14 = f32[768,4,1]{1,2,0:T(1,128)S(1)} all-gather(f32[96,4,1]{1,2,0:T(1,128)S(1)} %copy.1197), channel_id=16, replica_groups=mesh['seq'=8,'blk'=4] {'seq'}, dimensions={0}, use_global_device_ids=true | all-gather | bytes 13824 | tf_op jit(solution)/shard_map/all_gather | solution.py:11
  1337.8 31.0 %all-gather.13 = f32[768,4,1]{1,2,0:T(1,128)S(1)} all-gather(f32[96,4,1]{1,2,0:T(1,128)S(1)} %copy.1195), channel_id=15, replica_groups=mesh['seq'=8,'blk'=4] {'seq'}, dimensions={0}, use_global_device_ids=true | all-gather | bytes 13824 | tf_op jit(solution)/shard_map/all_gather | solution.py:11
  1370.7 31.0 %all-gather.12 = f32[768,4,1]{1,2,0:T(1,128)S(1)} all-gather(f32[96,4,1]{1,2,0:T(1,128)S(1)} %copy.1193), channel_id=14, replica_groups=mesh['seq'=8,'blk'=4] {'seq'}, dimensions={0}, use_global_device_ids=true | all-gather | bytes 13824 | tf_op jit(solution)/shard_map/all_gather | solution.py:11
  1418.6 39.3 %all-reduce.230 = (f32[512]{0:T(512)S(1)}, f32[512]{0:T(512)S(1)}, f32[512]{0:T(512)S(1)}, f32[512]{0:T(512)S(1)}, f32[512]{0:T(512)S(1)}, /*index=5*/f32[512]{0...) all-reduce(f32[512]{0:T(512)S(1)} %copy-done.245, ...), channel_id=19, replica_groups=mesh['seq'=8,'blk'=4] {'seq','blk'}, use_global_device_ids=true, to_apply=%region_18.19.clone | all-reduce | flops 5376 | bytes 43008
  1474.1 101.2 %reduce-scatter.11.cloned.1.call-done = f32[2,384,16]{1,2,0:T(8,128)} async-done(((f32[2,384,512]{1,2,0:T(8,128)}), f32[2,384,16]{1,2,0:T(8,128)}) %reduce-scatter.11.cloned.1.call-update) | async-done | bytes 49168 | tf_op jit(solution)/shard_map/reduce_scatter | solution.py:236
  1576.7 99.7 %reduce-scatter.9.cloned.1.call-done = f32[16,2,384]{2,0,1:T(8,128)} async-done(((f32[512,2,384]{2,0,1:T(8,128)}), f32[16,2,384]{2,0,1:T(8,128)}) %reduce-scatter.9.cloned.1.call-update) | async-done | bytes 49168 | tf_op jit(solution)/shard_map/reduce_scatter | solution.py:235
  1676.4 101.2 %reduce-scatter.7.cloned.1.call-done = f32[16,2,384]{2,0,1:T(8,128)} async-done(((f32[512,2,384]{2,0,1:T(8,128)}), f32[16,2,384]{2,0,1:T(8,128)}) %reduce-scatter.7.cloned.1.call-update) | async-done | bytes 49168 | tf_op jit(solution)/shard_map/reduce_scatter | solution.py:235
  (1364 shorter events, 708.8 us)
Async XLA Ops:
  14.7 14.0 all-to-all-start
  29.4 61.4 %copy-start.47 = (f32[96,4,32]{0,1,2:T(4,128)}, f32[96,4,32]{0,1,2:T(4,128)S(1)}, u32[]{:S(2)}) copy-start(f32[96,4,32]{0,1,2:T(4,128)S(1)} %get-tuple-element.1288) | copy-start | bytes 147460
  157.4 67.4 %copy-start.172 = (f32[96,4,1]{0,1,2:T(4,128)S(1)}, f32[96,4,1]{0,1,2:T(4,128)}, u32[]{:S(2)}) copy-start(f32[96,4,1]{0,1,2:T(4,128)} %slice.2773) | copy-start | bytes 4612
  192.2 90.2 %copy-start.171 = (f32[96,4,1]{0,1,2:T(4,128)S(1)}, f32[96,4,1]{0,1,2:T(4,128)}, u32[]{:S(2)}) copy-start(f32[96,4,1]{0,1,2:T(4,128)} %slice.2734) | copy-start | bytes 4612
  226.7 109.3 %copy-start.113 = (f32[96,4]{0,1:T(4,128)S(1)}, f32[96,4]{0,1:T(4,128)}, u32[]{:S(2)}) copy-start(f32[96,4]{0,1:T(4,128)} %custom-call) | copy-start | bytes 4612
  226.7 109.3 %copy-start.116 = (f32[96,4]{0,1:T(4,128)S(1)}, f32[96,4]{0,1:T(4,128)}, u32[]{:S(2)}) copy-start(f32[96,4]{0,1:T(4,128)} %custom-call.1) | copy-start | bytes 4612
  344.7 9.4 all-to-all-start.1
  358.6 8.8 all-to-all-start.2
  369.9 69.0 %copy-start.50 = (f32[96,4,32]{0,1,2:T(4,128)}, f32[96,4,32]{0,1,2:T(4,128)S(1)}, u32[]{:S(2)}) copy-start(f32[96,4,32]{0,1,2:T(4,128)S(1)} %get-tuple-element.1271) | copy-start | bytes 147460
  407.6 74.1 %copy-start.95 = (f32[96,4,8]{0,1,2:T(4,128)S(1)}, f32[96,4,8]{0,1,2:T(4,128)}, u32[]{:S(2)}) copy-start(f32[96,4,8]{0,1,2:T(4,128)} %copy-done.94) | copy-start | bytes 36868
  539.1 111.3 %copy-start.169 = (f32[96,4,1]{0,1,2:T(4,128)S(1)}, f32[96,4,1]{0,1,2:T(4,128)}, u32[]{:S(2)}) copy-start(f32[96,4,1]{0,1,2:T(4,128)} %slice.2867) | copy-start | bytes 4612
  595.7 111.0 %copy-start.168 = (f32[96,4,1]{0,1,2:T(4,128)S(1)}, f32[96,4,1]{0,1,2:T(4,128)}, u32[]{:S(2)}) copy-start(f32[96,4,1]{0,1,2:T(4,128)} %slice.2828) | copy-start | bytes 4612
  652.3 110.2 %copy-start.107 = (f32[96,4]{0,1:T(4,128)S(1)}, f32[96,4]{0,1:T(4,128)}, u32[]{:S(2)}) copy-start(f32[96,4]{0,1:T(4,128)} %custom-call.2) | copy-start | bytes 4612
  652.3 110.2 %copy-start.110 = (f32[96,4]{0,1:T(4,128)S(1)}, f32[96,4]{0,1:T(4,128)}, u32[]{:S(2)}) copy-start(f32[96,4]{0,1:T(4,128)} %custom-call.3) | copy-start | bytes 4612
  777.3 9.4 all-to-all-start.3
  793.2 8.7 all-to-all-start.4
  796.6 665.3 %reduce-scatter.17.cloned.1.call-start = ((), (), s32[]{:S(2)}) async-start(), calls=%async_computation.19 | async-start | bytes 1081344 | tf_op jit(solution)/shard_map/reduce_scatter | solution.py:237
  798.0 663.9 %reduce-scatter.15.cloned.1.call-start = ((), (), s32[]{:S(2)}) async-start(), calls=%async_computation.18 | async-start | bytes 1081344 | tf_op jit(solution)/shard_map/reduce_scatter | solution.py:237
  803.9 103.2 %copy-start.5 = (f32[96,4,64]{0,1,2:T(4,128)}, f32[96,4,64]{0,1,2:T(4,128)S(1)}, u32[]{:S(2)}) copy-start(f32[96,4,64]{0,1,2:T(4,128)S(1)} %get-tuple-element.1209) | copy-start | bytes 294916
  910.9 62.5 %copy-start.92 = (f32[96,4,8]{0,1,2:T(4,128)S(1)}, f32[96,4,8]{0,1,2:T(4,128)}, u32[]{:S(2)}) copy-start(f32[96,4,8]{0,1,2:T(4,128)} %copy-done.91) | copy-start | bytes 36868
  1107.0 110.9 %copy-start.119 = (f32[96,4]{0,1:T(4,128)S(1)}, f32[96,4]{0,1:T(4,128)}, u32[]{:S(2)}) copy-start(f32[96,4]{0,1:T(4,128)} %custom-call.4) | copy-start | bytes 4612
  1107.0 110.9 %copy-start.120 = (f32[96,4]{0,1:T(4,128)S(1)}, f32[96,4]{0,1:T(4,128)}, u32[]{:S(2)}) copy-start(f32[96,4]{0,1:T(4,128)} %custom-call.5) | copy-start | bytes 4612
  1129.7 93.2 %copy-start.43 = (f32[4,128]{0,1:T(8,128)S(1)}, f32[4,128]{0,1:T(8,128)}, u32[]{:S(2)}) copy-start(f32[4,128]{0,1:T(8,128)} %copy-done.42) | copy-start | bytes 6148
  1129.7 93.2 %copy-start.109 = (f32[96,4]{0,1:T(4,128)S(1)}, f32[96,4]{0,1:T(4,128)}, u32[]{:S(2)}) copy-start(f32[96,4]{0,1:T(4,128)} %copy-done.108) | copy-start | bytes 4612
  1129.7 93.2 %copy-start.112 = (f32[96,4]{0,1:T(4,128)S(1)}, f32[96,4]{0,1:T(4,128)}, u32[]{:S(2)}) copy-start(f32[96,4]{0,1:T(4,128)} %copy-done.111) | copy-start | bytes 4612
  1239.8 234.3 %reduce-scatter.13.cloned.1.call-start = ((), (), s32[]{:S(2)}) async-start(), calls=%async_computation.17 | async-start | bytes 1622016 | tf_op jit(solution)/shard_map/reduce_scatter | solution.py:236
  1241.5 333.7 %reduce-scatter.11.cloned.1.call-start = ((), (), s32[]{:S(2)}) async-start(), calls=%async_computation.16 | async-start | bytes 1622016 | tf_op jit(solution)/shard_map/reduce_scatter | solution.py:236
  1251.8 9.0 all-to-all-start.6
  1255.2 421.2 %reduce-scatter.9.cloned.1.call-start = ((), (), s32[]{:S(2)}) async-start(), calls=%async_computation.15 | async-start | bytes 1622016 | tf_op jit(solution)/shard_map/reduce_scatter | solution.py:235
  1270.6 65.3 %copy-start.170 = (f32[96,4,1]{0,1,2:T(4,128)S(1)}, f32[96,4,1]{0,1,2:T(4,128)}, u32[]{:S(2)}) copy-start(f32[96,4,1]{0,1,2:T(4,128)} %slice.3055) | copy-start | bytes 4612
  1405.2 9.4 all-to-all-start.7
  1408.6 368.9 %reduce-scatter.7.cloned.1.call-start = ((), (), s32[]{:S(2)}) async-start(), calls=%async_computation.14 | async-start | bytes 1622016 | tf_op jit(solution)/shard_map/reduce_scatter | solution.py:235
  (234 other events, 1440.1 us)
Sparse Core Ops, SparseCore 0:
  799.6 136.0 reduce-scatter.16
  1239.9 135.8 reduce-scatter.14
  1381.0 92.9 reduce-scatter.12
  1479.2 96.0 reduce-scatter.10
  1580.3 95.9 reduce-scatter.8
  1681.5 96.0 reduce-scatter.6
where the time goes:
time: 1820 us; the launch traced here: 1790 us
  local copies, waits for them, and re-layouts  670 us (37%)
  blocking collectives  546 us (30%)
  waiting for transfers between devices  337 us (19%)
  other arithmetic  169 us (9%)
  starting transfers between devices  25.4 us (1%)
  matrix products  19.3 us (1%)
  between operations  18.9 us (1%)
    pad x192, local copies, waits for them, and re-layouts, recurrence(): lax.associative_scan(combine, pieces, axis=2)  560 us
    all_gather x16, blocking collectives, prefix(): pieces = jax.tree.map(lambda part: lax.all_gather(part, axis), value)  498 us
    reduce_scatter x2, waiting for transfers between devices, layer_backward(): lax.psum_scatter(in_weight_grad, ('seq', 'blk'), scatter_dimension=0, til...  201 us
    reduce_scatter x2, waiting for transfers between devices, layer_backward(): lax.psum_scatter(out_weight_grad, ('seq', 'blk'), scatter_dimension=2, ti...  112 us
    slice x108, local copies, waits for them, and re-layouts, recurrence(): lax.associative_scan(combine, pieces, axis=2)  49.3 us
    add x112, other arithmetic, recurrence(): lax.associative_scan(combine, pieces, axis=2)  48 us
    concatenate x96, other arithmetic, recurrence(): lax.associative_scan(combine, pieces, axis=2)  45.9 us
    unnamed x1, blocking collectives  39.3 us
  transfers between devices with their start and end apart: 13, of which 10 were waited for; matrix products, arithmetic and copies ran while one was open for 20% of the time, Pallas kernels for 0%

commit v1 on v0

v1 whole, which is shorter than its diff:
```python
import types

import jax
import jax.numpy as jnp
from jax import lax
from jax.experimental import pallas as pl
from jax.experimental.pallas import tpu as pltpu
from jax.sharding import PartitionSpec as P

EPS = 1e-6
F32 = jnp.float32
LOW = jnp.bfloat16
GELU_A = 0.7978845608028654
GELU_B = 0.044715
LANES = 128
SUB = 8
BLOCK = 16
LINKS = 112


def cmul(are, aim, bre, bim):
    return are * bre - aim * bim, are * bim + aim * bre


def expm1(value):
    series = jnp.ones_like(value)
    for order in range(9, 1, -1):
        series = 1.0 + value * series * (1.0 / order)
    return jnp.where(value > -0.35, value * series, jnp.exp(value) - 1.0)


def discretize(decay, freq, step_log):
    lam_re = -jnp.exp(decay)
    step = jnp.exp(step_log)
    rotation = freq * step
    shrink = expm1(lam_re * step)
    cosine, sine = jnp.cos(rotation), jnp.sin(rotation)
    half = jnp.sin(0.5 * rotation)
    bar_re = (shrink + 1.0) * cosine
    bar_im = (shrink + 1.0) * sine
    minus_re = shrink * cosine - 2.0 * half * half
    scale = 1.0 / (lam_re * lam_re + freq * freq)
    coef_re = (minus_re * lam_re + bar_im * freq) * scale
    coef_im = (bar_im * lam_re - minus_re * freq) * scale
    return types.SimpleNamespace(
        lam_re=lam_re, freq=freq, step=step, scale=scale,
        bar_re=bar_re, bar_im=bar_im, coef_re=coef_re, coef_im=coef_im,
    )


def discretize_grad(d, bar_gre, bar_gim, coef_gre, coef_gim):
    over_re, over_im = d.lam_re * d.scale, d.freq * d.scale
    part_re, part_im = cmul(coef_gre, coef_gim, over_re, over_im)
    all_re, all_im = bar_gre + part_re, bar_gim + part_im
    one_re, one_im = cmul(all_re, all_im, d.bar_re, -d.bar_im)
    two_re, two_im = cmul(part_re, part_im, d.coef_re, -d.coef_im)
    lam_gre = one_re * d.step - two_re
    lam_gim = one_im * d.step - two_im
    step_g = one_re * d.lam_re + one_im * d.freq
    return lam_gre * d.lam_re, lam_gim, step_g * d.step


def mm(a, b):
    return jnp.dot(a, b, preferred_element_type=F32)


def mm_nt(a, b):
    return lax.dot_general(a, b, (((1,), (1,)), ((), ())), preferred_element_type=F32)


def wide(mask, width):
    return jnp.concatenate([mask] * (width // LANES), axis=1)


class Wire:
    def __init__(self, send_sems, recv_sems):
        self.send_sems, self.recv_sems = send_sems, recv_sems
        self.count = 0
        self.open = []

    def send(self, src, dst, device):
        at = self.count
        self.count += 1
        copy = pltpu.make_async_remote_copy(
            src_ref=src, dst_ref=dst,
            send_sem=self.send_sems.at[at], recv_sem=self.recv_sems.at[at],
            device_id=device, device_id_type=pl.DeviceIdType.MESH,
        )
        copy.start()
        self.open.append(copy)
        return copy

    def close(self):
        for copy in self.open:
            copy.wait_send()


def make_kernel(names, z):
    T, H, N, S, nseq, nblk, fused = z.T, z.H, z.N, z.S, z.nseq, z.nblk, z.fused
    W = 2 * N
    CE = H + W

    def kernel(*refs):
        r = types.SimpleNamespace(**dict(zip(names, refs, strict=True)))
        seq = lax.axis_index("seq")
        blk = lax.axis_index("blk")
        wire = Wire(r.send_sems, r.recv_sems)
        core, yy = blk % 2, blk // 2
        xx, zz = seq % 2, seq // 2
        nz = nseq // 2
        sibling = {"blk": yy * 2 + (1 - core)}
        y_peer = {"blk": (1 - yy) * 2 + core}
        x_peer = {"seq": zz * 2 + (1 - xx)}

        loads = {}

        def load(name, src, dst):
            copy = pltpu.make_async_copy(src, dst, r.load_sems.at[len(loads)])
            copy.start()
            loads[name] = copy

        load("tok", r.tokens, r.tok)
        load("wi0", r.in_proj.at[0], r.wi.at[0])
        load("wo0", r.out_proj.at[0], r.wo.at[0])
        load("wg0", r.glu_weight.at[0], r.wg.at[0])
        load("wi1", r.in_proj.at[1], r.wi.at[1])
        load("wo1", r.out_proj.at[1], r.wo.at[1])
        load("wg1", r.glu_weight.at[1], r.wg.at[1])
        load("cot", r.cotangent, r.cot)

        barrier = pltpu.get_barrier_semaphore()
        greeted = [{"seq": (seq + o) % nseq} for o in range(1, nseq)]
        if fused:
            greeted += [sibling, y_peer]
        for device in greeted:
            pl.semaphore_signal(barrier, inc=1, device_id=device, device_id_type=pl.DeviceIdType.MESH)

        disc, powers = [], []
        for l in range(2):
            d = discretize(
                r.decay_log[l : l + 1, :], r.frequency[l : l + 1, :], r.step_log[l : l + 1, :]
            )
            disc.append(d)
            chain = [(d.bar_re, d.bar_im)]
            while len(chain) < 12:
                chain.append(cmul(*chain[-1], *chain[-1]))
            powers.append(chain)
        step_bits = S.bit_length() - 1
        seg_bits = T.bit_length() - 1

        def power_rows(l, first, exponent, bits):
            rows = exponent.shape[0]
            out_re = jnp.ones((rows, N), F32)
            out_im = jnp.zeros((rows, N), F32)
            for bit in range(bits):
                use = wide(((exponent >> bit) & 1) == 1, N)
                pre, pim = powers[l][first + bit]
                new_re, new_im = cmul(out_re, out_im, pre, pim)
                out_re = jnp.where(use, new_re, out_re)
                out_im = jnp.where(use, new_im, out_im)
            return out_re, out_im

        ends, starts = [], []
        total = jnp.int32(0)
        for i in range(r.lengths.shape[1]):
            starts.append(total)
            total = total + r.lengths[blk, i]
            ends.append(total - 1)

        def keep(position, marks):
            hit = position == marks[0]
            for mark in marks[1:]:
                hit = hit | (position == mark)
            return jnp.where(hit, 0.0, 1.0).astype(F32)

        row = lax.broadcasted_iota(jnp.int32, (T, LANES), 0)
        here = seq * T + (row % SUB) * S + row // SUB
        r.keep[0] = keep(here, starts)
        r.keep[1] = keep(here, ends)
        offset = lax.broadcasted_iota(jnp.int32, (nseq, T), 0)
        lane = lax.broadcasted_iota(jnp.int32, (nseq, T), 1)
        there = ((seq - offset + nseq) % nseq) * T + lane
        k8 = lax.broadcasted_iota(jnp.int32, (SUB, LANES), 0)
        n_row = lax.broadcasted_iota(jnp.int32, (nseq, LANES), 0)
        for way in range(2):
            chunk = jnp.ones((SUB, LANES), F32)
            for s in range(S):
                chunk = chunk * r.keep[way, s * SUB : (s + 1) * SUB, :]
            for level in range(3):
                delta = 1 << level
                if way == 0:
                    inside, rolled = k8 >= delta, pltpu.roll(chunk, delta, 0)
                else:
                    inside, rolled = k8 < SUB - delta, pltpu.roll(chunk, SUB - delta, 0)
                r.chunk_keep[way, level] = jnp.where(inside, chunk, 0.0)
                chunk = jnp.where(inside, chunk * rolled, chunk)
            if way == 0:
                before = jnp.where(k8 >= 1, pltpu.roll(chunk, 1, 0), 1.0)
                chunks_before = k8
            else:
                before = jnp.where(k8 < SUB - 1, pltpu.roll(chunk, SUB - 1, 0), 1.0)
                chunks_before = SUB - 1 - k8
            whole = jnp.min(keep(there, starts if way == 0 else ends), axis=1, keepdims=True)
            whole = jnp.broadcast_to(whole, (nseq, LANES))
            gates = [None] * nseq
            running = jnp.ones((1, LANES), F32)
            for o in range(1, nseq) if way == 0 else range(nseq - 1, 0, -1):
                gates[o] = running
                running = running * whole[o : o + 1, :]
            gates[0] = jnp.zeros((1, LANES), F32)
            gate = jnp.concatenate(gates, axis=0)
            if way == 0:
                valid = (n_row >= 1) & (n_row <= seq)
                hops = n_row - 1
            else:
                valid = n_row > seq
                hops = nseq - 1 - n_row
            gate = jnp.where(valid, gate, 0.0)
            hops = jnp.where(valid, hops, 0)
            for l in range(2):
                index = (0, 2)[l] if way == 0 else (3, 1)[l]
                sign = 1.0 if index < 2 else -1.0
                pre, pim = power_rows(l, step_bits, chunks_before, 3)
                r.chunk_table[index, :, 0:N] = pre * wide(before, N)
                r.chunk_table[index, :, N:W] = pim * wide(before, N) * sign
                pre, pim = power_rows(l, seg_bits, hops, (nseq - 1).bit_length())
                r.seq_table[index, :, 0:N] = pre * wide(gate, N)
                r.seq_table[index, :, N:W] = pim * wide(gate, N) * sign
        for index in range(4):
            r.carry_in[index, 0] = jnp.zeros((1, W), F32)

        def scan(index, l, way, conj, source, between, sink):
            bre, bim = disc[l].bar_re, disc[l].bar_im
            sign = -1.0 if conj else 1.0
            bre = jnp.broadcast_to(bre, (SUB, N))
            bim = jnp.broadcast_to(bim * sign, (SUB, N))
            order = list(range(S)) if way == 0 else list(range(S - 1, -1, -1))

            def advance(s, yre, yim, dre, dim):
                k = wide(r.keep[way, s * SUB : (s + 1) * SUB, :], N)
                pre, pim = cmul(bre, bim, yre * k, yim * k)
                return pre + dre, pim + dim

            yre = jnp.zeros((SUB, N), F32)
            yim = jnp.zeros((SUB, N), F32)
            for s in order:
                dre, dim = source(s, True)
                yre, yim = advance(s, yre, yim, dre, dim)
            for level in range(3):
                delta = 1 << level
                shift = delta if way == 0 else SUB - delta
                m = wide(r.chunk_keep[way, level], N)
                pre, pim = powers[l][step_bits + level]
                gre, gim = cmul(pre, pim * sign, pltpu.roll(yre, shift, 0) * m, pltpu.roll(yim, shift, 0) * m)
                yre, yim = yre + gre, yim + gim
            last = SUB - 1 if way == 0 else 0
            r.carry_out[index, 0:1, 0:N] = yre[last : last + 1, :]
            r.carry_out[index, 0:1, N:W] = yim[last : last + 1, :]
            if index == 0:
                pl.semaphore_wait(barrier, len(greeted))
            copies = [
                wire.send(r.carry_out.at[index], r.carry_in.at[index, o], {"seq": (seq + o) % nseq})
                for o in range(1, nseq)
            ]
            edge = wide(k8 >= 1 if way == 0 else k8 < SUB - 1, N)
            shift = 1 if way == 0 else SUB - 1
            yre = jnp.where(edge, pltpu.roll(yre, shift, 0), 0.0)
            yim = jnp.where(edge, pltpu.roll(yim, shift, 0), 0.0)
            between()
            for copy in copies:
                copy.wait_recv()
            got = r.carry_in[index, :, 0, :]
            gre, gim = cmul(got[:, 0:N], got[:, N:W], r.seq_table[index, :, 0:N], r.seq_table[index, :, N:W])
            gre = jnp.sum(gre, axis=0, keepdims=True)
            gim = jnp.sum(gim, axis=0, keepdims=True)
            gre, gim = cmul(gre, gim, r.chunk_table[index, :, 0:N], r.chunk_table[index, :, N:W])
            yre, yim = yre + gre, yim + gim
            if not conj:
                r.x_first[l, :, 0:N] = yre
                r.x_first[l, :, N:W] = yim
            held = None
            for s in order:
                dre, dim = source(s, False)
                yre, yim = advance(s, yre, yim, dre, dim)
                out = sink(s, yre, yim)
                if held is None:
                    held = out
                else:
                    pair = (held, out) if way == 0 else (out, held)
                    first = s - 1 if way == 0 else s
                    for c in range(2):
                        both = jnp.concatenate([pair[0][c], pair[1][c]], axis=0).astype(LOW)
                        dest, at = sink.dest
                        dest[l, first * SUB : (first + 2) * SUB, at + c * N : at + (c + 1) * N] = both
                    held = None

        def chunks(body, init=0, unroll=2):
            def step(i, carry):
                return body(pl.ds(pl.multiple_of(i * BLOCK, BLOCK), BLOCK), carry)

            return lax.fori_loop(0, T // BLOCK, step, init, unroll=unroll)

        def turn(l, value_ref, lt, rt):
            for j in range(H // LANES):
                block = value_ref[:, j * LANES : (j + 1) * LANES].T
                lt[l, 4 * j : 4 * j + 4] = block.reshape(4, 2, BLOCK, LANES)
            if fused:
                return wire.send(lt.at[l, :, 1 - core], rt.at[l], sibling)

        def share(l, ref, first, last):
            if fused:
                return wire.send(
                    ref.at[l, 0:T, first:last], ref.at[l, T : 2 * T, first:last], sibling
                )

        def outer(l, lt, rt, right, first, last, dest, waits, at):
            if fused:
                for copy in waits:
                    copy.wait_recv()
                mine = lt[l, :, core].reshape(H // 2, LANES)
                left = jnp.concatenate([mine, rt[l].reshape(H // 2, LANES)], axis=1)
                for c in range(first, last, 256):
                    g = mm(left, right[l, :, c : c + 256]).astype(LOW)
                    dest[l, :, :, :, :, c : c + 256] = g.reshape(nz, 2, 2, BLOCK, 256)
            else:
                left = lt[l].reshape(H, LANES)
                for c in range(first, last, 256):
                    r.matrix_sums[l, :, at + c - first : at + c - first + 256] = mm(
                        left, right[l, 0:T, c : c + 256]
                    )

        def rs_start(l, u):
            half = u.p.shape[-1] // 2
            u.first[l] = (
                wire.send(u.p.at[l, :, 1 - xx, :, :, 0:half], u.r1.at[l, 0], x_peer),
                wire.send(u.p.at[l, :, :, 1 - yy, :, half : 2 * half], u.r1.at[l, 1], y_peer),
            )

        def rs_second(l, u):
            half = u.p.shape[-1] // 2
            u.first[l][0].wait_recv()
            for q in range(nz):
                u.s1[l, 0, q] = u.p[l, q, xx, :, :, 0:half] + u.r1[l, 0, q]
            to_y = wire.send(u.s1.at[l, 0, :, 1 - yy], u.r2.at[l, 0], y_peer)
            u.first[l][1].wait_recv()
            for q in range(nz):
                u.s1[l, 1, q] = u.p[l, q, :, yy, :, half : 2 * half] + u.r1[l, 1, q]
            to_x = wire.send(u.s1.at[l, 1, :, 1 - xx], u.r2.at[l, 1], x_peer)
            u.second[l] = (to_y, to_x)

        def rs_third(l, u):
            u.third[l] = []
            for part, mine in ((0, yy), (1, xx)):
                u.second[l][part].wait_recv()
                u.s2[l, part] = u.s1[l, part, :, mine] + u.r2[l, part]
                for o in range(1, nz):
                    to = (zz + o) % nz
                    u.third[l].append(
                        wire.send(
                            u.s2.at[l, part, to], u.r3.at[l, part, o - 1], {"seq": to * 2 + xx}
                        )
                    )

        def rs_end(l, u):
            for copy in u.third[l]:
                copy.wait_recv()
            halves = []
            for part in range(2):
                value = u.s2[l, part, zz].astype(F32)
                for o in range(1, nz):
                    value = value + u.r3[l, part, o - 1].astype(F32)
                halves.append(value)
            return jnp.concatenate(halves, axis=1)

        def vec_start(l):
            r.vec_copy[l] = wire.send(r.vec.at[l, 0], r.vec_in.at[l, 0], sibling)

        def vec_next(l, stage):
            r.vec_copy[l].wait_recv()
            r.vec[l, stage] = r.vec[l, stage - 1] + r.vec_in[l, stage - 1]
            r.vec_copy[l] = wire.send(
                r.vec.at[l, stage], r.vec_in.at[l, stage], (sibling, x_peer, y_peer)[stage]
            )

        def vec_last(l):
            r.vec_copy[l].wait_recv()
            total = r.vec[l, 2] + r.vec_in[l, 2]
            r.vec_z[l, zz] = total
            r.vec_copy[l] = [
                wire.send(
                    r.vec_z.at[l, zz], r.vec_z.at[l, zz], {"seq": ((zz + o) % nz) * 2 + xx}
                )
                for o in range(1, nz)
            ]

        def vec_end(l):
            for copy in r.vec_copy[l]:
                copy.wait_recv()
            total = r.vec_z[l, 0]
            for o in range(1, nz):
                total = total + r.vec_z[l, o]
            return total

        r.vec_copy = [None, None]
        early = late = None
        if fused:
            early = types.SimpleNamespace(p=r.p_e, r1=r.r1_e, s1=r.s1_e, r2=r.r2_e, s2=r.s2_e, r3=r.r3_e, first={}, second={}, third={})
            late = types.SimpleNamespace(p=r.p_n, r1=r.r1_n, s1=r.s1_n, r2=r.r2_n, s2=r.s2_n, r3=r.r3_n, first={}, second={}, third={})
        waits = {}

        def gain(l):
            return r.norm_gain[l : l + 1, :]

        def skip(l):
            return r.skip_gain[l : l + 1, :]

        def forward_in(l):
            def norm(rows, carry):
                u = r.u[l, rows, :]
                inv = lax.rsqrt(jnp.mean(u * u, axis=1, keepdims=True) + EPS)
                normed = u * inv * gain(l)
                r.inv[l, rows, :] = jnp.broadcast_to(inv, (BLOCK, LANES))
                r.normed[l, rows, :] = normed
                r.normed_low[l, rows, :] = normed.astype(LOW)
                return carry

            chunks(norm)
            loads[f"wi{l}"].wait()
            r.proj[l] = mm(r.normed_low[l], r.wi[l])

        def states(l, between):
            cre = jnp.broadcast_to(disc[l].coef_re, (SUB, N))
            cim = jnp.broadcast_to(disc[l].coef_im, (SUB, N))

            def source(s, first):
                rows = slice(s * SUB, (s + 1) * SUB)
                if first:
                    dre, dim = cmul(cre, cim, r.proj[l, rows, 0:N], r.proj[l, rows, N:W])
                    r.drive[rows, 0:N] = dre
                    r.drive[rows, N:W] = dim
                    return dre, dim
                return r.drive[rows, 0:N], r.drive[rows, N:W]

            def sink(s, yre, yim):
                rows = slice(s * SUB, (s + 1) * SUB)
                r.x[l, rows, 0:N] = yre
                r.x[l, rows, N:W] = yim
                return yre, yim

            sink.dest = (r.right_e, H)
            scan(l, l, l, False, source, between, sink)

        def forward_out(l):
            waits["x", l] = share(l, r.right_e, H, CE)
            loads[f"wo{l}"].wait()
            r.mixed[l] = mm(r.right_e[l, 0:T, H:CE], r.wo[l])

            def gelu(rows, carry):
                mixed = r.mixed[l, rows, :] + skip(l) * r.normed[l, rows, :]
                th = jnp.tanh(GELU_A * (mixed + GELU_B * (mixed * mixed * mixed)))
                r.mixed[l, rows, :] = mixed
                r.th[l, rows, :] = th
                r.act_low[l, rows, :] = (0.5 * mixed * (1.0 + th)).astype(LOW)
                return carry

            chunks(gelu)
            loads[f"wg{l}"].wait()
            r.gate[l] = mm(r.act_low[l], r.wg[l])

            def out(rows, carry):
                gate = jax.nn.sigmoid(r.gate[l, rows, :] + r.glu_bias[l : l + 1, :])
                r.gate[l, rows, :] = gate
                act = 0.5 * r.mixed[l, rows, :] * (1.0 + r.th[l, rows, :])
                value = r.u[l, rows, :] + act * gate
                if l == 0:
                    r.u[1, rows, :] = value
                else:
                    r.act_out[rows, :] = value.astype(LOW)
                return carry

            chunks(out)

        def backward_in(l):
            def glu(rows, bias):
                g = r.og[rows, :]
                gate = r.gate[l, rows, :]
                act = 0.5 * r.mixed[l, rows, :] * (1.0 + r.th[l, rows, :])
                gate_grad = (g * act * gate * (1.0 - gate)).astype(LOW)
                r.right_e[l, rows, 0:H] = gate_grad
                wide_grad = gate_grad.astype(F32)
                return bias + wide_grad[0:SUB] + wide_grad[SUB:BLOCK]

            bias = chunks(glu, jnp.zeros((SUB, H), F32))
            r.vec[l, 0, 2:3, :] = jnp.sum(bias, axis=0, keepdims=True)
            waits["gate", l] = share(l, r.right_e, 0, H)
            r.tmp[...] = mm_nt(r.right_e[l, 0:T, 0:H], r.wg[l])

            def gelu(rows, total):
                act_grad = r.og[rows, :] * r.gate[l, rows, :] + r.tmp[rows, :]
                mixed, th = r.mixed[l, rows, :], r.th[l, rows, :]
                inner = GELU_A * (1.0 + 3.0 * GELU_B * mixed * mixed)
                slope = 0.5 * (1.0 + th) + 0.5 * mixed * (1.0 - th * th) * inner
                low = (act_grad * slope).astype(LOW)
                r.mixed_grad[l, rows, :] = low
                part = low.astype(F32) * r.normed[l, rows, :]
                return total + part[0:SUB] + part[SUB:BLOCK]

            total = chunks(gelu, jnp.zeros((SUB, H), F32))
            r.vec[l, 0, 0:1, :] = jnp.sum(total, axis=0, keepdims=True)
            r.xg[...] = mm_nt(r.mixed_grad[l], r.wo[l])

        def adjoints(l, between):
            d = disc[l]
            cre = jnp.broadcast_to(d.coef_re, (SUB, N))
            cim = jnp.broadcast_to(d.coef_im, (SUB, N))
            way = 1 - l
            sums = [jnp.zeros((SUB, N), F32) for _ in range(4)]

            def source(s, first):
                rows = slice(s * SUB, (s + 1) * SUB)
                return r.xg[rows, 0:N], r.xg[rows, N:W]

            def sink(s, are, aim):
                rows = slice(s * SUB, (s + 1) * SUB)
                at = s - 1 if l == 0 else s + 1
                if 0 <= at < S:
                    old = slice(at * SUB, (at + 1) * SUB)
                    xre, xim = r.x[l, old, 0:N], r.x[l, old, N:W]
                else:
                    xre, xim = r.x_first[l, :, 0:N], r.x_first[l, :, N:W]
                k = wide(r.keep[l, rows, :], N)
                xre, xim = xre * k, xim * k
                pre, pim = r.proj[l, rows, 0:N], r.proj[l, rows, N:W]
                sums[0] = sums[0] + (are * xre + aim * xim)
                sums[1] = sums[1] + (aim * xre - are * xim)
                sums[2] = sums[2] + (are * pre + aim * pim)
                sums[3] = sums[3] + (aim * pre - are * pim)
                return cre * are + cim * aim, cre * aim - cim * are

            sink.dest = (r.right_n, 0)
            scan(3 - l, l, way, True, source, between, sink)
            pad = jnp.zeros((1, H - N), F32)
            for i in range(4):
                value = jnp.sum(sums[i], axis=0, keepdims=True)
                r.vec[l, 0, 3 + i : 4 + i, :] = jnp.concatenate([value, pad], axis=1)

        def backward_out(l):
            waits["pg", l] = share(l, r.right_n, 0, W)
            r.tmp[...] = mm_nt(r.right_n[l, 0:T, :], r.wi[l])

            def norm(rows, total):
                u = r.u[l, rows, :]
                inv = wide(r.inv[l, rows, :], H)
                ng = r.tmp[rows, :] + skip(l) * r.mixed_grad[l, rows, :].astype(F32)
                v = gain(l) * ng
                uv = jnp.mean(u * v, axis=1, keepdims=True)
                out = r.og[rows, :] + inv * v - u * (inv * inv * inv) * uv
                r.og[rows, :] = out
                part = ng * u * inv
                return total + part[0:SUB] + part[SUB:BLOCK]

            total = chunks(norm, jnp.zeros((SUB, H), F32))
            r.vec[l, 0, 1:2, :] = jnp.sum(total, axis=0, keepdims=True)
            r.vec[l, 0, 7:8, :] = jnp.zeros((1, H), F32)

        loads["tok"].wait()
        at = lax.broadcasted_iota(jnp.int32, (T, T), 0)
        of = lax.broadcasted_iota(jnp.int32, (T, T), 1)
        to_rows = jnp.where(of == (at % SUB) * S + at // SUB, 1.0, 0.0).astype(LOW)
        to_time = jnp.where(at == (of % SUB) * S + of // SUB, 1.0, 0.0).astype(LOW)
        r.u[0] = mm(to_rows, r.tok[...])
        forward_in(0)

        def fill0():
            waits["ln", 0] = turn(0, r.normed_low.at[0], r.lt_n, r.rt_n)

        states(0, fill0)
        forward_out(0)

        forward_in(1)

        def fill1():
            waits["lg", 0] = turn(0, r.act_low.at[0], r.lt_g, r.rt_g)
            waits["ln", 1] = turn(1, r.normed_low.at[1], r.lt_n, r.rt_n)
            loads["cot"].wait()
            r.og[...] = mm(to_rows, r.cot[...])

        states(1, fill1)
        forward_out(1)
        backward_in(1)

        def early_products(l):
            outer(l, r.lt_g, r.rt_g, r.right_e, 0, H, early and early.p, (waits["lg", l], waits["gate", l]), 0)
            outer(l, r.lt_o, r.rt_o, r.right_e, H, CE, early and early.p, (waits["lo", l], waits["x", l]), H)
            if fused:
                rs_start(l, early)

        def late_products(l):
            outer(l, r.lt_n, r.rt_n, r.right_n, 0, W, late and late.p, (waits["ln", l], waits["pg", l]), CE)
            if fused:
                rs_start(l, late)

        def fill2():
            waits["lo", 1] = turn(1, r.mixed_grad.at[1], r.lt_o, r.rt_o)
            waits["lg", 1] = turn(1, r.act_low.at[1], r.lt_g, r.rt_g)
            r.activations[...] = mm(to_time, r.act_out[...]).astype(LOW)
            early_products(1)

        adjoints(1, fill2)
        backward_out(1)
        if fused:
            vec_start(1)
        late_products(1)
        backward_in(0)

        def fill3():
            waits["lo", 0] = turn(0, r.mixed_grad.at[0], r.lt_o, r.rt_o)
            if fused:
                rs_second(1, early)
                vec_next(1, 1)
            early_products(0)
            if fused:
                rs_second(1, late)
                vec_next(1, 2)
                rs_third(1, early)

        adjoints(0, fill3)
        backward_out(0)
        if fused:
            vec_start(0)
        late_products(0)

        for s in range(S):
            for j in range(H // LANES):
                r.tokens_grad[pl.ds(s * (H // LANES) + j, SUB, stride=S * (H // LANES)), :] = r.og[
                    s * SUB : (s + 1) * SUB, j * LANES : (j + 1) * LANES
                ]

        if not fused:
            r.vector_sums[...] = r.vec[:, 0]
            wire.close()
            return

        rs_third(1, late)
        vec_last(1)
        rs_second(0, early)
        vec_next(0, 1)
        rs_second(0, late)
        vec_next(0, 2)
        rs_third(0, early)
        rs_third(0, late)
        vec_last(0)
        device = seq * nblk + blk
        for l in (1, 0):
            g = rs_end(l, early)
            r.glu_weight_grad[l] = g[:, 0:H]
            r.out_proj_grad[l, 0] = g[:, H : H + N]
            r.out_proj_grad[l, 1] = g[:, H + N : CE]
            g = rs_end(l, late)
            for c in range(2):
                r.in_proj_grad[l, :, c, :] = g[:, c * N : (c + 1) * N]
            total = vec_end(l)
            mine = pltpu.roll(total, (H - device * BLOCK) % H, 1)[:, 0:BLOCK]
            r.skip_gain_grad[l : l + 1, :] = mine[0:1]
            r.norm_gain_grad[l : l + 1, :] = mine[1:2]
            r.glu_bias_grad[l : l + 1, :] = mine[2:3]
            grads = discretize_grad(disc[l], *(total[3 + i : 4 + i, 0:N] for i in range(4)))
            r.decay_log_grad[l : l + 1, :] = grads[0]
            r.frequency_grad[l : l + 1, :] = grads[1]
            r.step_log_grad[l : l + 1, :] = grads[2]
        wire.close()

    return kernel


def solution(mesh):
    nseq, nblk = mesh.shape["seq"], mesh.shape["blk"]

    def on_device(
        tokens, lengths, norm_gain, in_proj, out_proj, skip_gain,
        glu_weight, glu_bias, decay_log, frequency, step_log, cotangent,
    ):
        T, streams, H = tokens.shape
        N = decay_log.shape[1]
        W = 2 * N
        CE = H + W
        assert streams == 1 and T == LANES and H == 512
        fused = nseq == 8 and nblk == 4
        z = types.SimpleNamespace(T=T, H=H, N=N, S=T // SUB, nseq=nseq, nblk=nblk, fused=fused)
        any_space = pl.BlockSpec(memory_space=pl.ANY)
        vmem = pl.BlockSpec(memory_space=pltpu.VMEM)
        smem = pl.BlockSpec(memory_space=pltpu.SMEM)
        operands = {
            "tokens": (tokens.reshape(T, H), any_space),
            "lengths": (lengths, smem),
            "norm_gain": (norm_gain, vmem),
            "in_proj": (in_proj.reshape(2, H, W), any_space),
            "out_proj": (out_proj.reshape(2, W, H), any_space),
            "skip_gain": (skip_gain, vmem),
            "glu_weight": (glu_weight, any_space),
            "glu_bias": (glu_bias, vmem),
            "decay_log": (decay_log, vmem),
            "frequency": (frequency, vmem),
            "step_log": (step_log, vmem),
            "cotangent": (cotangent.reshape(T, H), any_space),
        }
        results = {
            "activations": ((T, H), LOW),
            "tokens_grad": ((T * H // LANES, LANES), F32),
        }
        if fused:
            results |= {
                "norm_gain_grad": ((2, BLOCK), F32),
                "in_proj_grad": ((2, BLOCK, 2, N), F32),
                "out_proj_grad": ((2, 2, BLOCK, N), F32),
                "skip_gain_grad": ((2, BLOCK), F32),
                "glu_weight_grad": ((2, BLOCK, H), F32),
                "glu_bias_grad": ((2, BLOCK), F32),
                "decay_log_grad": ((2, N), F32),
                "frequency_grad": ((2, N), F32),
                "step_log_grad": ((2, N), F32),
            }
        else:
            results |= {"matrix_sums": ((2, H, CE + W), F32), "vector_sums": ((2, 8, H), F32)}
        dma = pltpu.SemaphoreType.DMA
        scratch = {
            "wi": pltpu.VMEM((2, H, W), LOW),
            "wo": pltpu.VMEM((2, W, H), LOW),
            "wg": pltpu.VMEM((2, H, H), LOW),
            "tok": pltpu.VMEM((T, H), LOW),
            "cot": pltpu.VMEM((T, H), LOW),
            "u": pltpu.VMEM((2, T, H), F32),
            "inv": pltpu.VMEM((2, T, LANES), F32),
            "normed": pltpu.VMEM((2, T, H), F32),
            "normed_low": pltpu.VMEM((2, T, H), LOW),
            "proj": pltpu.VMEM((2, T, W), F32),
            "drive": pltpu.VMEM((T, W), F32),
            "x": pltpu.VMEM((2, T, W), F32),
            "x_first": pltpu.VMEM((2, SUB, W), F32),
            "mixed": pltpu.VMEM((2, T, H), F32),
            "th": pltpu.VMEM((2, T, H), F32),
            "gate": pltpu.VMEM((2, T, H), F32),
            "act_low": pltpu.VMEM((2, T, H), LOW),
            "act_out": pltpu.VMEM((T, H), LOW),
            "og": pltpu.VMEM((T, H), F32),
            "tmp": pltpu.VMEM((T, H), F32),
            "xg": pltpu.VMEM((T, W), F32),
            "mixed_grad": pltpu.VMEM((2, T, H), LOW),
            "right_e": pltpu.VMEM((2, 2 * T, CE), LOW),
            "right_n": pltpu.VMEM((2, 2 * T, W), LOW),
            "keep": pltpu.VMEM((2, T, LANES), F32),
            "chunk_keep": pltpu.VMEM((2, 3, SUB, LANES), F32),
            "chunk_table": pltpu.VMEM((4, SUB, W), F32),
            "seq_table": pltpu.VMEM((4, nseq, W), F32),
            "carry_out": pltpu.VMEM((4, 1, W), F32),
            "carry_in": pltpu.VMEM((4, nseq, 1, W), F32),
            "vec": pltpu.VMEM((2, 3, 8, H), F32),
        }
        for name in "gon":
            scratch[f"lt_{name}"] = pltpu.VMEM((2, H // 32, 2, BLOCK, LANES), LOW)
            scratch[f"rt_{name}"] = pltpu.VMEM((2, H // 32, BLOCK, LANES), LOW)
        if fused:
            nz = nseq // 2
            for name, width in (("e", CE), ("n", W)):
                half = width // 2
                scratch[f"p_{name}"] = pltpu.VMEM((2, nz, 2, 2, BLOCK, width), LOW)
                scratch[f"r1_{name}"] = pltpu.VMEM((2, 2, nz, 2, BLOCK, half), LOW)
                scratch[f"s1_{name}"] = pltpu.VMEM((2, 2, nz, 2, BLOCK, half), LOW)
                scratch[f"r2_{name}"] = pltpu.VMEM((2, 2, nz, BLOCK, half), LOW)
                scratch[f"s2_{name}"] = pltpu.VMEM((2, 2, nz, BLOCK, half), LOW)
                scratch[f"r3_{name}"] = pltpu.VMEM((2, 2, nz - 1, BLOCK, half), LOW)
            scratch["vec_in"] = pltpu.VMEM((2, 3, 8, H), F32)
            scratch["vec_z"] = pltpu.VMEM((2, nz, 8, H), F32)
        links = LINKS if fused else 4 * (nseq - 1)
        scratch["send_sems"] = dma((links,))
        scratch["recv_sems"] = dma((links,))
        scratch["load_sems"] = dma((8,))
        names = list(operands) + list(results) + list(scratch)
        outs = pl.pallas_call(
            make_kernel(names, z),
            out_shape=[jax.ShapeDtypeStruct(*v) for v in results.values()],
            in_specs=[spec for _, spec in operands.values()],
            out_specs=[vmem] * len(results),
            scratch_shapes=list(scratch.values()),
            compiler_params=pltpu.CompilerParams(
                collective_id=0, has_side_effects=True, vmem_limit_bytes=48 * 2**20
            ),
            name="two_layers",
        )(*(value for value, _ in operands.values()))
        o = types.SimpleNamespace(**dict(zip(results, outs)))
        activations = o.activations.reshape(T, 1, H)
        tokens_grad = o.tokens_grad.reshape(T, 1, H)
        if fused:
            return (
                activations, tokens_grad, o.norm_gain_grad, o.in_proj_grad,
                jnp.swapaxes(o.out_proj_grad, 2, 3), o.skip_gain_grad, o.glu_weight_grad,
                o.glu_bias_grad, o.decay_log_grad, o.frequency_grad, o.step_log_grad,
            )
        both = ("seq", "blk")
        sums = lax.psum_scatter(o.matrix_sums, both, scatter_dimension=1, tiled=True)
        rows = sums.shape[1]
        vectors = lax.psum(o.vector_sums, both)
        mine = lax.dynamic_slice_in_dim(vectors, lax.axis_index(both) * rows, rows, 2)
        grads = discretize_grad(
            discretize(decay_log, frequency, step_log), *(vectors[:, 3 + i, 0:N] for i in range(4))
        )
        return (
            activations, tokens_grad, mine[:, 1], sums[:, :, CE:].reshape(2, rows, 2, N),
            jnp.moveaxis(sums[:, :, H:CE].reshape(2, rows, 2, N), 1, 3), mine[:, 0], sums[:, :, 0:H],
            mine[:, 2], *grads,
        )

    split = P("seq", "blk", None)
    owned = ("seq", "blk")
    return jax.shard_map(
        on_device,
        mesh=mesh,
        in_specs=(split,) + (P(),) * 10 + (split,),
        out_specs=(
            split, split, P(None, owned), P(None, owned, None, None), P(None, None, None, owned),
            P(None, owned), P(None, owned, None), P(None, owned), P(), P(), P(),
        ),
        check_vma=False,
    )
```

time: 1820 us -> 63.8 us (0.04); the launches traced: 1790 us -> 63.6 us
  local copies, waits for them, and re-layouts: 670 us -> 12 us
  blocking collectives: 546 us -> 0 us
  waiting for transfers between devices: 337 us -> 0 us
  other arithmetic: 169 us -> 0 us
  Pallas kernels: 0 us -> 50.8 us
  starting transfers between devices: 25.4 us -> 0 us
  matrix products: 19.3 us -> 0 us
    pad x192 -> x0, local copies, waits for them, and re-layouts: 560 us -> none  [recurrence(): lax.associative_scan(combine, pieces, axis=2)]
    all_gather x16 -> x0, blocking collectives: 498 us -> none  [prefix(): pieces = jax.tree.map(lambda part: lax.all_gather(part, axis), value)]
    reduce_scatter x6 -> x0, waiting for transfers between devices: 313 us -> none  [the longest x2 201 us: layer_backward(): lax.psum_scatter(in_weight_grad, ('seq', 'blk'), scatter_dimension=0, til...]
    add x188 -> x0, other arithmetic: 87.3 us -> none  [the longest x112 48 us: recurrence(): lax.associative_scan(combine, pieces, axis=2)]
    slice x137 -> x0, local copies, waits for them, and re-layouts: 62.6 us -> none  [the longest x108 49.3 us: recurrence(): lax.associative_scan(combine, pieces, axis=2)]
    pallas_call x0 -> x1, Pallas kernels: none -> 50.8 us  [on_device(): pl.pallas_call(make_kernel(names, z), out_shape=[jax.ShapeDtypeStruct(*v)...]
    concatenate x96 -> x0, other arithmetic: 45.9 us -> none  [recurrence(): lax.associative_scan(combine, pieces, axis=2)]
    unnamed x1 -> x0, blocking collectives: 39.3 us -> none
  transfers between devices with their start and end apart: 13 -> 0, of which waited for: 10 -> 0; matrix products, arithmetic and copies ran while one was open for 20% -> 0% of each run, Pallas kernels for 0% -> 0%
where the time goes in v1:
time: 63.8 us; the launch traced here: 63.6 us
  Pallas kernels  50.8 us (80%)
  local copies, waits for them, and re-layouts  12 us (19%)
  between operations  0.84 us (1%)
    pallas_call x1, Pallas kernels, on_device(): pl.pallas_call(make_kernel(names, z), out_shape=[jax.ShapeDtypeStruct(*v)...  50.8 us
    unnamed x33, local copies, waits for them, and re-layouts  7.95 us
    reshape x1, local copies, waits for them, and re-layouts, on_device(): in_proj.reshape(2, H, W)  4.03 us

profile of v1, /device:TPU:0, one launch (start us, length us, event | category | flops | bytes accessed | tf_op | source)
XLA Modules:
  0.0 63.6 jit_solution(16120856619907108575)
XLA Ops:
  0.6 0.0 copy-start
  0.7 0.0 copy-start.2
  0.7 0.0 copy-start.3
  0.7 0.0 copy-start.4
  0.7 0.0 copy-start.5
  0.7 0.0 copy-start.6
  0.7 0.0 copy-start.7
  0.7 0.0 copy-start.8
  0.7 0.0 copy-start.9
  0.7 0.0 copy-start.10
  0.7 4.0 %reshape.41.refs_3_ = bf16[2,512,768]{2,1,0:T(8,128)(2,1)S(1)} reshape(bf16[2,512,2,384]{3,2,1,0:T(2,128)(2,1)} %param.15) | data formatting | bytes 3145728 | tf_op jit(solution)/shard_map/reshape | solution.py:697
  4.8 0.0 copy-done
  4.8 0.0 copy-done.2
  4.8 0.0 copy-done.3
  4.8 0.0 copy-done.4
  4.8 0.0 copy-done.5
  4.8 0.0 copy-done.6
  4.8 0.0 copy-done.7
  4.9 0.0 copy-start.1
  4.9 1.2 %copy-done.1 = bf16[2,512,512]{2,1,0:T(8,128)(2,1)S(1)} copy-done((bf16[2,512,512]{2,1,0:T(8,128)(2,1)S(1)}, bf16[2,512,512]{2,1,0:T(8,128)(2,1)}, u32[]{:S(2)}) %copy-start.1) | copy-done | bytes 1048600
  6.1 50.8 %two_layers.1 = (bf16[128,512]{1,0:T(8,128)(2,1)S(1)}, f32[512,128]{1,0:T(8,128)S(1)}, f32[2,16]{1,0:T(2,128)S(1)}, f32[2,16,2,384]{3,2,1,0:T(2,128)S(1)}, f32[2...) custom-call(bf16[128,512]{1,0:T(8,128)(2,1)S(1)} %bitcast.8, ...), custom_call_target="tpu_custom_call" | custom-call | tf_op jit(solution)/shard_map/two_layers/pallas_call | solution.py:779
  56.9 0.7 %copy.35 = bf16[128,1,512]{2,0,1:T(8,128)(2,1)} copy(bf16[128,1,512]{2,0,1:T(8,128)(2,1)S(1)} %bitcast.10) | data formatting | bytes 262144
  57.6 0.7 %copy.36 = f32[128,1,512]{2,1,0:T(1,128)} copy(f32[128,1,512]{2,1,0:T(1,128)S(1)} %bitcast.7) | data formatting | bytes 524288
  58.3 0.6 copy.37
  58.9 0.6 %copy.38 = f32[2,16,2,384]{3,2,1,0:T(2,128)} copy(f32[2,16,2,384]{3,2,1,0:T(2,128)S(1)} %get-tuple-element.58) | data formatting | bytes 196608
  59.5 0.6 %copy.39 = f32[2,2,384,16]{2,3,1,0:T(8,128)} copy(f32[2,2,384,16]{2,3,1,0:T(8,128)S(1)} %bitcast.11) | data formatting | bytes 196608
  60.1 0.6 copy.40
  60.7 0.6 copy.41
  61.3 0.6 copy.42
  61.9 0.6 copy.43
  62.5 0.6 copy.44
  63.0 0.6 copy.45
  (3 shorter events, 0.0 us)
Async XLA Ops:
  0.6 4.1 %copy-start = (bf16[2,2,384,512]{3,2,1,0:T(8,128)(2,1)S(1)}, bf16[2,2,384,512]{3,2,1,0:T(8,128)(2,1)}, u32[]{:S(2)}) copy-start(bf16[2,2,384,512]{3,2,1,0:T(8,128)(2,1)} %param.16) | copy-start | bytes 4718596
  0.7 4.1 %copy-start.2 = (bf16[128,1,512]{2,0,1:T(8,128)(2,1)S(1)}, bf16[128,1,512]{2,0,1:T(8,128)(2,1)}, u32[]{:S(2)}) copy-start(bf16[128,1,512]{2,0,1:T(8,128)(2,1)} %param.12) | copy-start | bytes 393220
  0.7 4.1 %copy-start.3 = (bf16[128,1,512]{2,0,1:T(8,128)(2,1)S(1)}, bf16[128,1,512]{2,0,1:T(8,128)(2,1)}, u32[]{:S(2)}) copy-start(bf16[128,1,512]{2,0,1:T(8,128)(2,1)} %param.23) | copy-start | bytes 393220
  0.7 4.1 %copy-start.4 = (f32[2,512]{1,0:T(2,128)S(1)}, f32[2,512]{1,0:T(2,128)}, u32[]{:S(2)}) copy-start(f32[2,512]{1,0:T(2,128)} %refs_2_.1) | copy-start | bytes 12292
  0.7 4.1 %copy-start.5 = (f32[2,512]{1,0:T(2,128)S(1)}, f32[2,512]{1,0:T(2,128)}, u32[]{:S(2)}) copy-start(f32[2,512]{1,0:T(2,128)} %refs_5_.1) | copy-start | bytes 12292
  0.7 4.1 %copy-start.6 = (f32[2,512]{1,0:T(2,128)S(1)}, f32[2,512]{1,0:T(2,128)}, u32[]{:S(2)}) copy-start(f32[2,512]{1,0:T(2,128)} %refs_7_.1) | copy-start | bytes 12292
  0.7 4.1 %copy-start.7 = (f32[2,384]{1,0:T(2,128)S(1)}, f32[2,384]{1,0:T(2,128)}, u32[]{:S(2)}) copy-start(f32[2,384]{1,0:T(2,128)} %refs_8_.1) | copy-start | bytes 9220
  0.7 4.1 %copy-start.8 = (f32[2,384]{1,0:T(2,128)S(1)}, f32[2,384]{1,0:T(2,128)}, u32[]{:S(2)}) copy-start(f32[2,384]{1,0:T(2,128)} %refs_9_.1) | copy-start | bytes 9220
  0.7 4.1 %copy-start.9 = (f32[2,384]{1,0:T(2,128)S(1)}, f32[2,384]{1,0:T(2,128)}, u32[]{:S(2)}) copy-start(f32[2,384]{1,0:T(2,128)} %refs_10_.1) | copy-start | bytes 9220
  0.7 4.1 %copy-start.10 = (s32[4,8]{1,0:T(4,128)S(1)}, s32[4,8]{1,0:T(4,128)}, u32[]{:S(2)}) copy-start(s32[4,8]{1,0:T(4,128)} %refs_1_.1) | copy-start | bytes 388
  4.9 1.2 %copy-start.1 = (bf16[2,512,512]{2,1,0:T(8,128)(2,1)S(1)}, bf16[2,512,512]{2,1,0:T(8,128)(2,1)}, u32[]{:S(2)}) copy-start(bf16[2,512,512]{2,1,0:T(8,128)(2,1)} %refs_6_.1) | copy-start | bytes 3145732

commit v2 on v1

--- a/solution.py
+++ b/solution.py
@@ -95,6 +95,17 @@
             copy.wait_send()
 
 
+def hand_out(*refs):
+    count = len(refs) // 2
+    copies = [
+        pltpu.make_async_copy(refs[i], refs[count + i], refs[-1].at[i]) for i in range(count)
+    ]
+    for copy in copies:
+        copy.start()
+    for copy in copies:
+        copy.wait()
+
+
 def make_kernel(names, z):
     T, H, N, S, nseq, nblk, fused = z.T, z.H, z.N, z.S, z.nseq, z.nblk, z.fused
     W = 2 * N
@@ -120,10 +131,10 @@
             loads[name] = copy
 
         load("tok", r.tokens, r.tok)
-        load("wi0", r.in_proj.at[0], r.wi.at[0])
+        load("wi0", r.in_proj.at[0], r.wi_raw.at[0])
         load("wo0", r.out_proj.at[0], r.wo.at[0])
         load("wg0", r.glu_weight.at[0], r.wg.at[0])
-        load("wi1", r.in_proj.at[1], r.wi.at[1])
+        load("wi1", r.in_proj.at[1], r.wi_raw.at[1])
         load("wo1", r.out_proj.at[1], r.wo.at[1])
         load("wg1", r.glu_weight.at[1], r.wg.at[1])
         load("cot", r.cotangent, r.cot)
@@ -329,48 +340,84 @@
                         left, right[l, 0:T, c : c + 256]
                     )
 
-        def rs_start(l, u):
-            half = u.p.shape[-1] // 2
-            u.first[l] = (
-                wire.send(u.p.at[l, :, 1 - xx, :, :, 0:half], u.r1.at[l, 0], x_peer),
-                wire.send(u.p.at[l, :, :, 1 - yy, :, half : 2 * half], u.r1.at[l, 1], y_peer),
-            )
-
-        def rs_second(l, u):
-            half = u.p.shape[-1] // 2
-            u.first[l][0].wait_recv()
-            for q in range(nz):
-                u.s1[l, 0, q] = u.p[l, q, xx, :, :, 0:half] + u.r1[l, 0, q]
-            to_y = wire.send(u.s1.at[l, 0, :, 1 - yy], u.r2.at[l, 0], y_peer)
-            u.first[l][1].wait_recv()
-            for q in range(nz):
-                u.s1[l, 1, q] = u.p[l, q, :, yy, :, half : 2 * half] + u.r1[l, 1, q]
-            to_x = wire.send(u.s1.at[l, 1, :, 1 - xx], u.r2.at[l, 1], x_peer)
-            u.second[l] = (to_y, to_x)
-
-        def rs_third(l, u):
-            u.third[l] = []
-            for part, mine in ((0, yy), (1, xx)):
-                u.second[l][part].wait_recv()
-                u.s2[l, part] = u.s1[l, part, :, mine] + u.r2[l, part]
-                for o in range(1, nz):
-                    to = (zz + o) % nz
-                    u.third[l].append(
-                        wire.send(
-                            u.s2.at[l, part, to], u.r3.at[l, part, o - 1], {"seq": to * 2 + xx}
-                        )
+        place = {"z": zz, "x": xx, "y": yy}
+
+        def peers(axis):
+            if axis == "x":
+                return [(1 - xx, x_peer)]
+            if axis == "y":
+                return [(1 - yy, y_peer)]
+            return [((zz + o) % nz, {"seq": ((zz + o) % nz) * 2 + xx}) for o in range(1, nz)]
+
+        class Part:
+            def __init__(self, whole, first, last, order, got, sums):
+                self.ref, self.columns = whole, pl.ds(first, last - first)
+                self.axes, self.order, self.stage = ["z", "x", "y"], order, 0
+                self.got, self.sums = got, sums
+
+            def begin(self):
+                axis = self.order[self.stage]
+                self.where = self.axes.index(axis)
+                rest = len(self.axes) - 1 - self.where
+                self.copies = []
+                for i, (to, device) in enumerate(peers(axis)):
+                    index = (slice(None),) * self.where + (to,) + (slice(None),) * (rest + 1)
+                    self.copies.append(
+                        wire.send(self.ref.at[index + (self.columns,)], self.got[self.stage].at[i], device)
                     )
 
-        def rs_end(l, u):
-            for copy in u.third[l]:
-                copy.wait_recv()
-            halves = []
-            for part in range(2):
-                value = u.s2[l, part, zz].astype(F32)
-                for o in range(1, nz):
-                    value = value + u.r3[l, part, o - 1].astype(F32)
-                halves.append(value)
-            return jnp.concatenate(halves, axis=1)
+            def total(self):
+                for copy in self.copies:
+                    copy.wait_recv()
+                axis, got = self.order[self.stage], self.got[self.stage]
+                mine, wait = place[axis], len(self.copies)
+                rest = [a for a in self.axes if a != axis]
+                if not rest:
+                    value = self.ref[mine, :, self.columns].astype(F32)
+                    for i in range(wait):
+                        value = value + got[i].astype(F32)
+                    return value
+                out = self.sums[self.stage]
+                for q in range(out.shape[0]):
+                    if self.where == 0:
+                        index = (mine, q)
+                    else:
+                        index = (q,) + (slice(None),) * (self.where - 1) + (mine,)
+                    index += (slice(None),) * (len(self.axes) - len(index) + 1) + (self.columns,)
+                    if wait == 1:
+                        out[q] = self.ref[index] + got[0, q]
+                    else:
+                        value = self.ref[index].astype(F32)
+                        for i in range(wait):
+                            value = value + got[i, q].astype(F32)
+                        out[q] = value.astype(LOW)
+                self.ref, self.columns = out, slice(None)
+                self.axes = rest
+                self.stage += 1
+
+            def step(self):
+                self.total()
+                self.begin()
+
+        def parts_of(l, name):
+            whole = getattr(r, f"p_{name}")
+            out = []
+            for i, (first, last, order) in enumerate(z.plan[name]):
+                got = [getattr(r, f"got_{name}{i}{stage}").at[l] for stage in range(3)]
+                sums = [getattr(r, f"sum_{name}{i}{stage}").at[l] for stage in range(2)]
+                out.append(Part(whole.at[l], first, last, order, got, sums))
+            return out
+
+        def rs_start(parts):
+            for part in parts:
+                part.begin()
+
+        def rs_step(parts):
+            for part in parts:
+                part.step()
+
+        def rs_end(parts):
+            return jnp.concatenate([part.total() for part in parts], axis=1)
 
         def vec_start(l):
             r.vec_copy[l] = wire.send(r.vec.at[l, 0], r.vec_in.at[l, 0], sibling)
@@ -402,10 +449,8 @@
             return total
 
         r.vec_copy = [None, None]
-        early = late = None
-        if fused:
-            early = types.SimpleNamespace(p=r.p_e, r1=r.r1_e, s1=r.s1_e, r2=r.r2_e, s2=r.s2_e, r3=r.r3_e, first={}, second={}, third={})
-            late = types.SimpleNamespace(p=r.p_n, r1=r.r1_n, s1=r.s1_n, r2=r.r2_n, s2=r.s2_n, r3=r.r3_n, first={}, second={}, third={})
+        early = [parts_of(l, "e") if fused else None for l in range(2)]
+        late = [parts_of(l, "n") if fused else None for l in range(2)]
         waits = {}
 
         def gain(l):
@@ -413,6 +458,16 @@
 
         def skip(l):
             return r.skip_gain[l : l + 1, :]
+
+        def pack_in(l):
+            loads[f"wi{l}"].wait()
+
+            def step(i, carry):
+                rows = pl.ds(pl.multiple_of(i * BLOCK, BLOCK), BLOCK)
+                r.wi[l, rows, :] = r.wi_raw[l, rows].reshape(BLOCK, W)
+                return carry
+
+            lax.fori_loop(0, H // BLOCK, step, 0, unroll=2)
 
         def forward_in(l):
             def norm(rows, carry):
@@ -425,7 +480,6 @@
                 return carry
 
             chunks(norm)
-            loads[f"wi{l}"].wait()
             r.proj[l] = mm(r.normed_low[l], r.wi[l])
 
         def states(l, between):
@@ -563,15 +617,26 @@
             r.vec[l, 0, 1:2, :] = jnp.sum(total, axis=0, keepdims=True)
             r.vec[l, 0, 7:8, :] = jnp.zeros((1, H), F32)
 
+        def early_products(l):
+            dest = r.p_e if fused else None
+            outer(l, r.lt_g, r.rt_g, r.right_e, 0, H, dest, (waits["lg", l], waits["gate", l]), 0)
+            outer(l, r.lt_o, r.rt_o, r.right_e, H, CE, dest, (waits["lo", l], waits["x", l]), H)
+
+        def late_products(l):
+            dest = r.p_n if fused else None
+            outer(l, r.lt_n, r.rt_n, r.right_n, 0, W, dest, (waits["ln", l], waits["pg", l]), CE)
+
         loads["tok"].wait()
         at = lax.broadcasted_iota(jnp.int32, (T, T), 0)
         of = lax.broadcasted_iota(jnp.int32, (T, T), 1)
         to_rows = jnp.where(of == (at % SUB) * S + at // SUB, 1.0, 0.0).astype(LOW)
         to_time = jnp.where(at == (of % SUB) * S + of // SUB, 1.0, 0.0).astype(LOW)
         r.u[0] = mm(to_rows, r.tok[...])
+        pack_in(0)
         forward_in(0)
 
         def fill0():
+            pack_in(1)
             waits["ln", 0] = turn(0, r.normed_low.at[0], r.lt_n, r.rt_n)
 
         states(0, fill0)
@@ -589,46 +654,39 @@
         forward_out(1)
         backward_in(1)
 
-        def early_products(l):
-            outer(l, r.lt_g, r.rt_g, r.right_e, 0, H, early and early.p, (waits["lg", l], waits["gate", l]), 0)
-            outer(l, r.lt_o, r.rt_o, r.right_e, H, CE, early and early.p, (waits["lo", l], waits["x", l]), H)
-            if fused:
-                rs_start(l, early)
-
-        def late_products(l):
-            outer(l, r.lt_n, r.rt_n, r.right_n, 0, W, late and late.p, (waits["ln", l], waits["pg", l]), CE)
-            if fused:
-                rs_start(l, late)
-
         def fill2():
             waits["lo", 1] = turn(1, r.mixed_grad.at[1], r.lt_o, r.rt_o)
             waits["lg", 1] = turn(1, r.act_low.at[1], r.lt_g, r.rt_g)
             r.activations[...] = mm(to_time, r.act_out[...]).astype(LOW)
             early_products(1)
+            if fused:
+                rs_start(early[1])
 
         adjoints(1, fill2)
         backward_out(1)
-        if fused:
-            vec_start(1)
-        late_products(1)
         backward_in(0)
 
         def fill3():
+            late_products(1)
+            if fused:
+                rs_start(late[1])
+                vec_start(1)
             waits["lo", 0] = turn(0, r.mixed_grad.at[0], r.lt_o, r.rt_o)
             if fused:
-                rs_second(1, early)
-                vec_next(1, 1)
+                rs_step(early[1])
             early_products(0)
             if fused:
-                rs_second(1, late)
-                vec_next(1, 2)
-                rs_third(1, early)
+                rs_start(early[0])
+                vec_next(1, 1)
 
         adjoints(0, fill3)
         backward_out(0)
         if fused:
             vec_start(0)
+            rs_step(late[1])
         late_products(0)
+        if fused:
+            rs_start(late[0])
 
         for s in range(S):
             for j in range(H // LANES):
@@ -641,22 +699,24 @@
             wire.close()
             return
 
-        rs_third(1, late)
+        vec_next(1, 2)
+        rs_step(early[1])
+        vec_next(0, 1)
+        rs_step(early[0])
+        rs_step(late[1])
         vec_last(1)
-        rs_second(0, early)
-        vec_next(0, 1)
-        rs_second(0, late)
+        rs_step(late[0])
         vec_next(0, 2)
-        rs_third(0, early)
-        rs_third(0, late)
+        rs_step(early[0])
         vec_last(0)
+        rs_step(late[0])
         device = seq * nblk + blk
         for l in (1, 0):
-            g = rs_end(l, early)
+            g = rs_end(early[l])
             r.glu_weight_grad[l] = g[:, 0:H]
             r.out_proj_grad[l, 0] = g[:, H : H + N]
             r.out_proj_grad[l, 1] = g[:, H + N : CE]
-            g = rs_end(l, late)
+            g = rs_end(late[l])
             for c in range(2):
                 r.in_proj_grad[l, :, c, :] = g[:, c * N : (c + 1) * N]
             total = vec_end(l)
@@ -686,7 +746,13 @@
         CE = H + W
         assert streams == 1 and T == LANES and H == 512
         fused = nseq == 8 and nblk == 4
-        z = types.SimpleNamespace(T=T, H=H, N=N, S=T // SUB, nseq=nseq, nblk=nblk, fused=fused)
+        plan = {
+            "e": ((0, 384, "xyz"), (384, 896, "yxz"), (896, CE, "zxy")),
+            "n": ((0, N, "xyz"), (N, W, "yxz")),
+        }
+        z = types.SimpleNamespace(
+            T=T, H=H, N=N, S=T // SUB, nseq=nseq, nblk=nblk, fused=fused, plan=plan
+        )
         any_space = pl.BlockSpec(memory_space=pl.ANY)
         vmem = pl.BlockSpec(memory_space=pltpu.VMEM)
         smem = pl.BlockSpec(memory_space=pltpu.SMEM)
@@ -694,7 +760,7 @@
             "tokens": (tokens.reshape(T, H), any_space),
             "lengths": (lengths, smem),
             "norm_gain": (norm_gain, vmem),
-            "in_proj": (in_proj.reshape(2, H, W), any_space),
+            "in_proj": (in_proj, any_space),
             "out_proj": (out_proj.reshape(2, W, H), any_space),
             "skip_gain": (skip_gain, vmem),
             "glu_weight": (glu_weight, any_space),
@@ -724,6 +790,7 @@
             results |= {"matrix_sums": ((2, H, CE + W), F32), "vector_sums": ((2, 8, H), F32)}
         dma = pltpu.SemaphoreType.DMA
         scratch = {
+            "wi_raw": pltpu.VMEM((2, H, 2, N), LOW),
             "wi": pltpu.VMEM((2, H, W), LOW),
             "wo": pltpu.VMEM((2, W, H), LOW),
             "wg": pltpu.VMEM((2, H, H), LOW),
@@ -762,13 +829,15 @@
         if fused:
             nz = nseq // 2
             for name, width in (("e", CE), ("n", W)):
-                half = width // 2
                 scratch[f"p_{name}"] = pltpu.VMEM((2, nz, 2, 2, BLOCK, width), LOW)
-                scratch[f"r1_{name}"] = pltpu.VMEM((2, 2, nz, 2, BLOCK, half), LOW)
-                scratch[f"s1_{name}"] = pltpu.VMEM((2, 2, nz, 2, BLOCK, half), LOW)
-                scratch[f"r2_{name}"] = pltpu.VMEM((2, 2, nz, BLOCK, half), LOW)
-                scratch[f"s2_{name}"] = pltpu.VMEM((2, 2, nz, BLOCK, half), LOW)
-                scratch[f"r3_{name}"] = pltpu.VMEM((2, 2, nz - 1, BLOCK, half), LOW)
+                for i, (first, last, order) in enumerate(z.plan[name]):
+                    left = {"z": nz, "x": 2, "y": 2}
+                    for stage, axis in enumerate(order):
+                        others = left.pop(axis) - 1
+                        shape = tuple(left.values()) + (BLOCK, last - first)
+                        scratch[f"got_{name}{i}{stage}"] = pltpu.VMEM((2, others) + shape, LOW)
+                        if left:
+                            scratch[f"sum_{name}{i}{stage}"] = pltpu.VMEM((2,) + shape, LOW)
             scratch["vec_in"] = pltpu.VMEM((2, 3, 8, H), F32)
             scratch["vec_z"] = pltpu.VMEM((2, nz, 8, H), F32)
         links = LINKS if fused else 4 * (nseq - 1)
@@ -778,7 +847,7 @@
         names = list(operands) + list(results) + list(scratch)
         outs = pl.pallas_call(
             make_kernel(names, z),
-            out_shape=[jax.ShapeDtypeStruct(*v) for v in results.values()],
+            out_shape=[(pltpu.VMEM if fused else jax.ShapeDtypeStruct)(*v) for v in results.values()],
             in_specs=[spec for _, spec in operands.values()],
             out_specs=[vmem] * len(results),
             scratch_shapes=list(scratch.values()),
@@ -786,7 +855,16 @@
                 collective_id=0, has_side_effects=True, vmem_limit_bytes=48 * 2**20
             ),
             name="two_layers",
-        )(*(value for value, _ in operands.values()))
+        )(*(pltpu.with_memory_space_constraint(value, pltpu.HBM) for value, _ in operands.values()))
+        if fused:
+            outs = pl.pallas_call(
+                hand_out,
+                out_shape=[jax.ShapeDtypeStruct(*v) for v in results.values()],
+                in_specs=[vmem] * len(results),
+                out_specs=[any_space] * len(results),
+                scratch_shapes=[dma((len(results),))],
+                name="hand_out",
+            )(*(pltpu.with_memory_space_constraint(out, pltpu.VMEM) for out in outs))
         o = types.SimpleNamespace(**dict(zip(results, outs)))
         activations = o.activations.reshape(T, 1, H)
         tokens_grad = o.tokens_grad.reshape(T, 1, H)

time: 63.8 us -> 50.6 us (0.79)
  local copies, waits for them, and re-layouts: 12 us -> 0 us
  Pallas kernels: 50.8 us -> 49.8 us
    unnamed x33 -> x0, local copies, waits for them, and re-layouts: 7.95 us -> none
    reshape x1 -> x0, local copies, waits for them, and re-layouts: 4.03 us -> none  [on_device(): in_proj.reshape(2, H, W)]
    pallas_call x1 -> x2, Pallas kernels: 50.8 us -> 49.8 us  [the longest x1 48.9 us: on_device(): pl.pallas_call(make_kernel(names, z), out_shape=[(pltpu.VMEM if fused els...]
where the time goes in v2:
time: 50.6 us; the launch traced here: 50.5 us
  Pallas kernels  49.8 us (98%)
  between operations  0.66 us (1%)
    pallas_call x1, Pallas kernels, on_device(): pl.pallas_call(make_kernel(names, z), out_shape=[(pltpu.VMEM if fused els...  48.9 us

profile of v2, /device:TPU:0, one launch (start us, length us, event | category | flops | bytes accessed | tf_op | source)
XLA Modules:
  0.0 50.5 jit_solution(360666596017866070)
XLA Ops:
  0.6 48.9 %two_layers.1 = (bf16[128,512]{1,0:T(8,128)(2,1)S(1)}, f32[512,128]{1,0:T(8,128)S(1)}, f32[2,16]{1,0:T(2,128)S(1)}, f32[2,16,2,384]{3,2,1,0:T(2,128)S(1)}, f32[2...) custom-call(bf16[128,512]{1,0:T(8,128)(2,1)} %bitcast.7, ...), custom_call_target="tpu_custom_call" | custom-call | tf_op jit(solution)/shard_map/two_layers/pallas_call | solution.py:848
  49.5 0.9 %hand_out.1 = (bf16[128,512]{1,0:T(8,128)(2,1)}, f32[512,128]{1,0:T(8,128)}, f32[2,16]{1,0:T(2,128)}, f32[2,16,2,384]{3,2,1,0:T(2,128)}, f32[2,2,16,384]{3,2,1,0...) custom-call(bf16[128,512]{1,0:T(8,128)(2,1)S(1)} %get-tuple-element., ...), custom_call_target="tpu_custom_call" | custom-call | tf_op jit(solution)/shard_map/hand_out/pallas_call | solution.py:860

commit v3 on v2

--- a/solution.py
+++ b/solution.py
@@ -15,7 +15,21 @@
 LANES = 128
 SUB = 8
 BLOCK = 16
-LINKS = 112
+LINKS = 160
+SMALL = ("lengths", "norm_gain", "skip_gain", "glu_bias", "decay_log", "frequency", "step_log")
+
+PLAN = {
+    "e1": ((384, "zxy"), (256, "yzx"), (640, "xyz")),
+    "n1": ((256, "yzx"), (128, "xyz"), (256, "xyz"), (128, "yxz")),
+    "e0": ((384, "xyz"), (512, "yxz"), (384, "zxy")),
+    "n0": ((256, "xyz"), (512, "xyz")),
+}
+SCHEDULE = (
+    "E1 Be10 Be11 Be12",
+    "N1 M0 e11 Bn10 Bn11 Bn12 e12 va E0 Be00 e10 Be01 Be02 n11 n10",
+    "e11 OUT n12 va N0 vb Bn00 e12 Bn01 Bn13 e00 e10 e11 vb e01 e02 n11 n00 n12 n10 va n13 e00 e12 n01 e10 vb"
+    " n00 n11 n12 e01 va e02 n10 n13 e00 n01 vb e02 n00 e01 n13 n01",
+)
 
 
 def cmul(are, aim, bre, bim):
@@ -131,6 +145,9 @@
             loads[name] = copy
 
         load("tok", r.tokens, r.tok)
+        for name in SMALL:
+            load(name, getattr(r, name), getattr(r, name + "_here"))
+            setattr(r, name, getattr(r, name + "_here"))
         load("wi0", r.in_proj.at[0], r.wi_raw.at[0])
         load("wo0", r.out_proj.at[0], r.wo.at[0])
         load("wg0", r.glu_weight.at[0], r.wg.at[0])
@@ -146,6 +163,8 @@
         for device in greeted:
             pl.semaphore_signal(barrier, inc=1, device_id=device, device_id_type=pl.DeviceIdType.MESH)
 
+        for name in SMALL:
+            loads[name].wait()
         disc, powers = [], []
         for l in range(2):
             d = discretize(
@@ -305,7 +324,7 @@
                         dest[l, first * SUB : (first + 2) * SUB, at + c * N : at + (c + 1) * N] = both
                     held = None
 
-        def chunks(body, init=0, unroll=2):
+        def chunks(body, init=0, unroll=T // BLOCK):
             def step(i, carry):
                 return body(pl.ds(pl.multiple_of(i * BLOCK, BLOCK), BLOCK), carry)
 
@@ -396,61 +415,103 @@
                 self.stage += 1
 
             def step(self):
-                self.total()
-                self.begin()
-
-        def parts_of(l, name):
-            whole = getattr(r, f"p_{name}")
-            out = []
-            for i, (first, last, order) in enumerate(z.plan[name]):
-                got = [getattr(r, f"got_{name}{i}{stage}").at[l] for stage in range(3)]
-                sums = [getattr(r, f"sum_{name}{i}{stage}").at[l] for stage in range(2)]
-                out.append(Part(whole.at[l], first, last, order, got, sums))
-            return out
-
-        def rs_start(parts):
-            for part in parts:
-                part.begin()
-
-        def rs_step(parts):
-            for part in parts:
-                part.step()
-
-        def rs_end(parts):
-            return jnp.concatenate([part.total() for part in parts], axis=1)
-
-        def vec_start(l):
-            r.vec_copy[l] = wire.send(r.vec.at[l, 0], r.vec_in.at[l, 0], sibling)
-
-        def vec_next(l, stage):
-            r.vec_copy[l].wait_recv()
-            r.vec[l, stage] = r.vec[l, stage - 1] + r.vec_in[l, stage - 1]
-            r.vec_copy[l] = wire.send(
-                r.vec.at[l, stage], r.vec_in.at[l, stage], (sibling, x_peer, y_peer)[stage]
-            )
-
-        def vec_last(l):
-            r.vec_copy[l].wait_recv()
-            total = r.vec[l, 2] + r.vec_in[l, 2]
-            r.vec_z[l, zz] = total
-            r.vec_copy[l] = [
-                wire.send(
-                    r.vec_z.at[l, zz], r.vec_z.at[l, zz], {"seq": ((zz + o) % nz) * 2 + xx}
-                )
-                for o in range(1, nz)
-            ]
-
-        def vec_end(l):
-            for copy in r.vec_copy[l]:
-                copy.wait_recv()
-            total = r.vec_z[l, 0]
-            for o in range(1, nz):
-                total = total + r.vec_z[l, o]
-            return total
-
-        r.vec_copy = [None, None]
-        early = [parts_of(l, "e") if fused else None for l in range(2)]
-        late = [parts_of(l, "n") if fused else None for l in range(2)]
+                value = self.total()
+                if value is None:
+                    self.begin()
+                else:
+                    self.sink(value)
+
+        along = {}
+
+        def sink_of(l, name, first, last):
+            def early(value):
+                for low, high, out in (
+                    (0, H, r.glu_weight_grad.at[l]),
+                    (H, H + N, r.out_proj_grad.at[l, 0]),
+                    (H + N, CE, r.out_proj_grad.at[l, 1]),
+                ):
+                    a, b = max(low, first), min(high, last)
+                    if a < b:
+                        out[:, a - low : b - low] = value[:, a - first : b - first]
+
+            def late(value):
+                for c in range(2):
+                    a, b = max(c * N, first), min((c + 1) * N, last)
+                    if a < b:
+                        r.in_proj_grad[l, :, c, a - c * N : b - c * N] = value[:, a - first : b - first]
+                weights = r.wi[l, own_rows, first:last].astype(F32)
+                along.setdefault(l, []).append(jnp.sum(value * weights, axis=1, keepdims=True))
+
+            return early if name == "e" else late
+
+        parts = {}
+        for l, name in z.plan:
+            for i, (first, last, order) in enumerate(z.plan[l, name]):
+                label = f"{name}{l}{i}"
+                got = [getattr(r, f"got_{label}_{stage}") for stage in range(3)]
+                sums = [getattr(r, f"sum_{label}_{stage}") for stage in range(2)]
+                part = Part(getattr(r, f"p_{name}").at[l], first, last, order, got, sums)
+                part.sink = sink_of(l, name, first, last)
+                parts[label] = part
+
+        device = seq * nblk + blk
+        own_rows = pl.ds(pl.multiple_of(device * BLOCK, BLOCK), BLOCK)
+
+        def owned(value):
+            return pltpu.roll(value, (H - device * BLOCK) % H, 1)[:, 0:BLOCK]
+
+        def out_vectors(l, totals):
+            grads = discretize_grad(disc[l], *totals)
+            r.decay_log_grad[l : l + 1, :] = grads[0]
+            r.frequency_grad[l : l + 1, :] = grads[1]
+            r.step_log_grad[l : l + 1, :] = grads[2]
+
+        class Vector:
+            def __init__(self, own, got, last):
+                self.own, self.got, self.last, self.stage = own, got, last, 0
+
+            def begin(self):
+                device = (sibling, x_peer, y_peer)[self.stage]
+                self.copy = wire.send(self.own.at[self.stage], self.got.at[self.stage], device)
+
+            def step(self):
+                if self.stage == 3:
+                    return self.sink(self.total())
+                self.copy.wait_recv()
+                total = self.own[self.stage] + self.got[self.stage]
+                self.stage += 1
+                if self.stage < 3:
+                    self.own[self.stage] = total
+                    return self.begin()
+                self.last[zz] = total
+                self.copies = [
+                    wire.send(self.last.at[zz], self.last.at[zz], {"seq": ((zz + o) % nz) * 2 + xx})
+                    for o in range(1, nz)
+                ]
+
+            def total(self):
+                for copy in self.copies:
+                    copy.wait_recv()
+                value = self.last[0]
+                for o in range(1, nz):
+                    value = value + self.last[o]
+                return value
+
+        if fused:
+            first_vector = Vector(r.vec_a, r.vec_a_in, r.vec_a_z)
+            last_vector = Vector(r.vec_b, r.vec_b_in, r.vec_b_z)
+
+            def first_sink(sums):
+                mine["sums"] = owned(sums)
+                for l, at in ((1, 0), (0, 6)):
+                    r.skip_gain_grad[l : l + 1, :] = mine["sums"][at : at + 1]
+                    r.glu_bias_grad[l : l + 1, :] = mine["sums"][at + 1 : at + 2]
+                out_vectors(1, [sums[2 + i : 3 + i, 0:N] for i in range(4)])
+
+            mine = {}
+            first_vector.sink = first_sink
+            last_vector.sink = lambda sums: out_vectors(0, [sums[i : i + 1] for i in range(4)])
+            parts["va"], parts["vb"] = first_vector, last_vector
         waits = {}
 
         def gain(l):
@@ -467,7 +528,7 @@
                 r.wi[l, rows, :] = r.wi_raw[l, rows].reshape(BLOCK, W)
                 return carry
 
-            lax.fori_loop(0, H // BLOCK, step, 0, unroll=2)
+            lax.fori_loop(0, H // BLOCK, step, 0, unroll=4)
 
         def forward_in(l):
             def norm(rows, carry):
@@ -545,7 +606,7 @@
                 return bias + wide_grad[0:SUB] + wide_grad[SUB:BLOCK]
 
             bias = chunks(glu, jnp.zeros((SUB, H), F32))
-            r.vec[l, 0, 2:3, :] = jnp.sum(bias, axis=0, keepdims=True)
+            r.vec_a[0, 1 if l == 1 else 7, :] = jnp.sum(bias, axis=0)
             waits["gate", l] = share(l, r.right_e, 0, H)
             r.tmp[...] = mm_nt(r.right_e[l, 0:T, 0:H], r.wg[l])
 
@@ -560,7 +621,7 @@
                 return total + part[0:SUB] + part[SUB:BLOCK]
 
             total = chunks(gelu, jnp.zeros((SUB, H), F32))
-            r.vec[l, 0, 0:1, :] = jnp.sum(total, axis=0, keepdims=True)
+            r.vec_a[0, 0 if l == 1 else 6, :] = jnp.sum(total, axis=0)
             r.xg[...] = mm_nt(r.mixed_grad[l], r.wo[l])
 
         def adjoints(l, between):
@@ -596,13 +657,15 @@
             pad = jnp.zeros((1, H - N), F32)
             for i in range(4):
                 value = jnp.sum(sums[i], axis=0, keepdims=True)
-                r.vec[l, 0, 3 + i : 4 + i, :] = jnp.concatenate([value, pad], axis=1)
+                if l == 1:
+                    r.vec_a[0, 2 + i : 3 + i, :] = jnp.concatenate([value, pad], axis=1)
+                else:
+                    r.vec_b[0, i : i + 1, :] = value
 
         def backward_out(l):
-            waits["pg", l] = share(l, r.right_n, 0, W)
             r.tmp[...] = mm_nt(r.right_n[l, 0:T, :], r.wi[l])
 
-            def norm(rows, total):
+            def norm(rows, carry):
                 u = r.u[l, rows, :]
                 inv = wide(r.inv[l, rows, :], H)
                 ng = r.tmp[rows, :] + skip(l) * r.mixed_grad[l, rows, :].astype(F32)
@@ -610,12 +673,9 @@
                 uv = jnp.mean(u * v, axis=1, keepdims=True)
                 out = r.og[rows, :] + inv * v - u * (inv * inv * inv) * uv
                 r.og[rows, :] = out
-                part = ng * u * inv
-                return total + part[0:SUB] + part[SUB:BLOCK]
-
-            total = chunks(norm, jnp.zeros((SUB, H), F32))
-            r.vec[l, 0, 1:2, :] = jnp.sum(total, axis=0, keepdims=True)
-            r.vec[l, 0, 7:8, :] = jnp.zeros((1, H), F32)
+                return carry
+
+            chunks(norm)
 
         def early_products(l):
             dest = r.p_e if fused else None
@@ -654,80 +714,65 @@
         forward_out(1)
         backward_in(1)
 
+        def run(tokens):
+            for token in tokens:
+                if token in tasks:
+                    tasks[token]()
+                elif fused and token[0] == "B":
+                    parts[token[1:]].begin()
+                elif fused:
+                    parts[token].step()
+
+        def task_n1():
+            late_products(1)
+            if fused:
+                first_vector.begin()
+
+        def task_m0():
+            waits["lo", 0] = turn(0, r.mixed_grad.at[0], r.lt_o, r.rt_o)
+
+        def task_out():
+            backward_out(0)
+            for s in range(S):
+                for j in range(H // LANES):
+                    into = pl.ds(s * (H // LANES) + j, SUB, stride=S * (H // LANES))
+                    r.tokens_grad[into, :] = r.og[s * SUB : (s + 1) * SUB, j * LANES : (j + 1) * LANES]
+
+        tasks = {
+            "N1": task_n1, "M0": task_m0, "E0": lambda: early_products(0),
+            "N0": lambda: late_products(0), "OUT": task_out, "E1": lambda: early_products(1),
+        }
+
         def fill2():
             waits["lo", 1] = turn(1, r.mixed_grad.at[1], r.lt_o, r.rt_o)
             waits["lg", 1] = turn(1, r.act_low.at[1], r.lt_g, r.rt_g)
             r.activations[...] = mm(to_time, r.act_out[...]).astype(LOW)
-            early_products(1)
-            if fused:
-                rs_start(early[1])
+            run(z.schedule[0])
 
         adjoints(1, fill2)
+        waits["pg", 1] = share(1, r.right_n, 0, W)
         backward_out(1)
         backward_in(0)
-
-        def fill3():
-            late_products(1)
-            if fused:
-                rs_start(late[1])
-                vec_start(1)
-            waits["lo", 0] = turn(0, r.mixed_grad.at[0], r.lt_o, r.rt_o)
-            if fused:
-                rs_step(early[1])
-            early_products(0)
-            if fused:
-                rs_start(early[0])
-                vec_next(1, 1)
-
-        adjoints(0, fill3)
-        backward_out(0)
+        adjoints(0, lambda: run(z.schedule[1]))
+        waits["pg", 0] = share(0, r.right_n, 0, W)
         if fused:
-            vec_start(0)
-            rs_step(late[1])
-        late_products(0)
-        if fused:
-            rs_start(late[0])
-
-        for s in range(S):
-            for j in range(H // LANES):
-                r.tokens_grad[pl.ds(s * (H // LANES) + j, SUB, stride=S * (H // LANES)), :] = r.og[
-                    s * SUB : (s + 1) * SUB, j * LANES : (j + 1) * LANES
-                ]
+            last_vector.begin()
+        run(z.schedule[2])
 
         if not fused:
-            r.vector_sums[...] = r.vec[:, 0]
+            r.vector_sums[...] = r.vec_a[0]
+            r.last_vector_sums[...] = r.vec_b[0]
             wire.close()
             return
 
-        vec_next(1, 2)
-        rs_step(early[1])
-        vec_next(0, 1)
-        rs_step(early[0])
-        rs_step(late[1])
-        vec_last(1)
-        rs_step(late[0])
-        vec_next(0, 2)
-        rs_step(early[0])
-        vec_last(0)
-        rs_step(late[0])
-        device = seq * nblk + blk
-        for l in (1, 0):
-            g = rs_end(early[l])
-            r.glu_weight_grad[l] = g[:, 0:H]
-            r.out_proj_grad[l, 0] = g[:, H : H + N]
-            r.out_proj_grad[l, 1] = g[:, H + N : CE]
-            g = rs_end(late[l])
-            for c in range(2):
-                r.in_proj_grad[l, :, c, :] = g[:, c * N : (c + 1) * N]
-            total = vec_end(l)
-            mine = pltpu.roll(total, (H - device * BLOCK) % H, 1)[:, 0:BLOCK]
-            r.skip_gain_grad[l : l + 1, :] = mine[0:1]
-            r.norm_gain_grad[l : l + 1, :] = mine[1:2]
-            r.glu_bias_grad[l : l + 1, :] = mine[2:3]
-            grads = discretize_grad(disc[l], *(total[3 + i : 4 + i, 0:N] for i in range(4)))
-            r.decay_log_grad[l : l + 1, :] = grads[0]
-            r.frequency_grad[l : l + 1, :] = grads[1]
-            r.step_log_grad[l : l + 1, :] = grads[2]
+        gains = owned(jnp.concatenate([r.norm_gain[...], r.skip_gain[...], jnp.zeros((4, H), F32)], axis=0))
+        diagonal = lax.broadcasted_iota(jnp.int32, (BLOCK, BLOCK), 0) == lax.broadcasted_iota(
+            jnp.int32, (BLOCK, BLOCK), 1
+        )
+        for l, at in ((1, 0), (0, 6)):
+            total = jnp.sum(jnp.where(diagonal, sum(along[l]), 0.0), axis=0, keepdims=True)
+            total = total + gains[2 + l : 3 + l] * mine["sums"][at : at + 1]
+            r.norm_gain_grad[l : l + 1, :] = total / gains[l : l + 1]
         wire.close()
 
     return kernel
@@ -746,28 +791,33 @@
         CE = H + W
         assert streams == 1 and T == LANES and H == 512
         fused = nseq == 8 and nblk == 4
-        plan = {
-            "e": ((0, 384, "xyz"), (384, 896, "yxz"), (896, CE, "zxy")),
-            "n": ((0, N, "xyz"), (N, W, "yxz")),
-        }
+        plan = {}
+        for unit, pieces in PLAN.items():
+            first = 0
+            cuts = []
+            for width, order in pieces:
+                cuts.append((first, first + width, order))
+                first += width
+            assert first == (CE if unit[0] == "e" else W)
+            plan[int(unit[1]), unit[0]] = cuts
         z = types.SimpleNamespace(
-            T=T, H=H, N=N, S=T // SUB, nseq=nseq, nblk=nblk, fused=fused, plan=plan
+            T=T, H=H, N=N, S=T // SUB, nseq=nseq, nblk=nblk, fused=fused, plan=plan if fused else {},
+            schedule=[line.split() for line in SCHEDULE],
         )
         any_space = pl.BlockSpec(memory_space=pl.ANY)
         vmem = pl.BlockSpec(memory_space=pltpu.VMEM)
-        smem = pl.BlockSpec(memory_space=pltpu.SMEM)
         operands = {
             "tokens": (tokens.reshape(T, H), any_space),
-            "lengths": (lengths, smem),
-            "norm_gain": (norm_gain, vmem),
+            "lengths": (lengths, any_space),
+            "norm_gain": (norm_gain, any_space),
             "in_proj": (in_proj, any_space),
             "out_proj": (out_proj.reshape(2, W, H), any_space),
-            "skip_gain": (skip_gain, vmem),
+            "skip_gain": (skip_gain, any_space),
             "glu_weight": (glu_weight, any_space),
-            "glu_bias": (glu_bias, vmem),
-            "decay_log": (decay_log, vmem),
-            "frequency": (frequency, vmem),
-            "step_log": (step_log, vmem),
+            "glu_bias": (glu_bias, any_space),
+            "decay_log": (decay_log, any_space),
+            "frequency": (frequency, any_space),
+            "step_log": (step_log, any_space),
             "cotangent": (cotangent.reshape(T, H), any_space),
         }
         results = {
@@ -787,7 +837,11 @@
                 "step_log_grad": ((2, N), F32),
             }
         else:
-            results |= {"matrix_sums": ((2, H, CE + W), F32), "vector_sums": ((2, 8, H), F32)}
+            results |= {
+                "matrix_sums": ((2, H, CE + W), F32),
+                "vector_sums": ((8, H), F32),
+                "last_vector_sums": ((4, N), F32),
+            }
         dma = pltpu.SemaphoreType.DMA
         scratch = {
             "wi_raw": pltpu.VMEM((2, H, 2, N), LOW),
@@ -821,7 +875,8 @@
             "seq_table": pltpu.VMEM((4, nseq, W), F32),
             "carry_out": pltpu.VMEM((4, 1, W), F32),
             "carry_in": pltpu.VMEM((4, nseq, 1, W), F32),
-            "vec": pltpu.VMEM((2, 3, 8, H), F32),
+            "vec_a": pltpu.VMEM((3, 8, H), F32),
+            "vec_b": pltpu.VMEM((3, 4, N), F32),
         }
         for name in "gon":
             scratch[f"lt_{name}"] = pltpu.VMEM((2, H // 32, 2, BLOCK, LANES), LOW)
@@ -830,20 +885,26 @@
             nz = nseq // 2
             for name, width in (("e", CE), ("n", W)):
                 scratch[f"p_{name}"] = pltpu.VMEM((2, nz, 2, 2, BLOCK, width), LOW)
-                for i, (first, last, order) in enumerate(z.plan[name]):
+            for l, name in plan:
+                for i, (first, last, order) in enumerate(plan[l, name]):
                     left = {"z": nz, "x": 2, "y": 2}
                     for stage, axis in enumerate(order):
                         others = left.pop(axis) - 1
                         shape = tuple(left.values()) + (BLOCK, last - first)
-                        scratch[f"got_{name}{i}{stage}"] = pltpu.VMEM((2, others) + shape, LOW)
+                        scratch[f"got_{name}{l}{i}_{stage}"] = pltpu.VMEM((others,) + shape, LOW)
                         if left:
-                            scratch[f"sum_{name}{i}{stage}"] = pltpu.VMEM((2,) + shape, LOW)
-            scratch["vec_in"] = pltpu.VMEM((2, 3, 8, H), F32)
-            scratch["vec_z"] = pltpu.VMEM((2, nz, 8, H), F32)
+                            scratch[f"sum_{name}{l}{i}_{stage}"] = pltpu.VMEM(shape, LOW)
+            for name, shape in (("a", (8, H)), ("b", (4, N))):
+                scratch[f"vec_{name}_in"] = pltpu.VMEM((3,) + shape, F32)
+                scratch[f"vec_{name}_z"] = pltpu.VMEM((nz,) + shape, F32)
         links = LINKS if fused else 4 * (nseq - 1)
         scratch["send_sems"] = dma((links,))
         scratch["recv_sems"] = dma((links,))
-        scratch["load_sems"] = dma((8,))
+        scratch["load_sems"] = dma((8 + len(SMALL),))
+        for name in SMALL:
+            value = operands[name][0]
+            space = pltpu.SMEM if name == "lengths" else pltpu.VMEM
+            scratch[name + "_here"] = space(value.shape, value.dtype)
         names = list(operands) + list(results) + list(scratch)
         outs = pl.pallas_call(
             make_kernel(names, z),
@@ -877,15 +938,24 @@
         both = ("seq", "blk")
         sums = lax.psum_scatter(o.matrix_sums, both, scatter_dimension=1, tiled=True)
         rows = sums.shape[1]
-        vectors = lax.psum(o.vector_sums, both)
-        mine = lax.dynamic_slice_in_dim(vectors, lax.axis_index(both) * rows, rows, 2)
-        grads = discretize_grad(
-            discretize(decay_log, frequency, step_log), *(vectors[:, 3 + i, 0:N] for i in range(4))
-        )
+        vectors, last = lax.psum((o.vector_sums, o.last_vector_sums), both)
+        start = lax.axis_index(both) * rows
+
+        def owned(value, axis):
+            return lax.dynamic_slice_in_dim(value, start, rows, axis)
+
+        mine = owned(vectors, 1)
+        skip_grad = jnp.stack([mine[6], mine[0]])
+        bias_grad = jnp.stack([mine[7], mine[1]])
+        totals = [jnp.stack([last[i], vectors[2 + i, 0:N]]) for i in range(4)]
+        grads = discretize_grad(discretize(decay_log, frequency, step_log), *totals)
+        in_grad = sums[:, :, CE:].reshape(2, rows, 2, N)
+        along = jnp.sum(in_grad * owned(in_proj, 1).astype(F32), axis=(2, 3))
+        gain_grad = (along + owned(skip_gain, 1) * skip_grad) / owned(norm_gain, 1)
         return (
-            activations, tokens_grad, mine[:, 1], sums[:, :, CE:].reshape(2, rows, 2, N),
-            jnp.moveaxis(sums[:, :, H:CE].reshape(2, rows, 2, N), 1, 3), mine[:, 0], sums[:, :, 0:H],
-            mine[:, 2], *grads,
+            activations, tokens_grad, gain_grad, in_grad,
+            jnp.moveaxis(sums[:, :, H:CE].reshape(2, rows, 2, N), 1, 3), skip_grad, sums[:, :, 0:H],
+            bias_grad, *grads,
         )
 
     split = P("seq", "blk", None)

time: 50.6 us -> 47.5 us (0.939)
  Pallas kernels: 49.8 us -> 46.7 us
    pallas_call x1, Pallas kernels: 48.9 us -> 45.7 us  [on_device(): pl.pallas_call(make_kernel(names, z), out_shape=[(pltpu.VMEM if fused els...]
where the time goes in v3:
time: 47.5 us; the launch traced here: 47.3 us
  Pallas kernels  46.7 us (98%)
  between operations  0.66 us (1%)
    pallas_call x1, Pallas kernels, on_device(): pl.pallas_call(make_kernel(names, z), out_shape=[(pltpu.VMEM if fused els...  45.7 us

profile of v3, /device:TPU:0, one launch (start us, length us, event | category | flops | bytes accessed | tf_op | source)
XLA Modules:
  0.0 47.3 jit_solution(16334365543978061081)
XLA Ops:
  0.6 45.7 %two_layers.1 = (bf16[128,512]{1,0:T(8,128)(2,1)S(1)}, f32[512,128]{1,0:T(8,128)S(1)}, f32[2,16]{1,0:T(2,128)S(1)}, f32[2,16,2,384]{3,2,1,0:T(2,128)S(1)}, f32[2...) custom-call(bf16[128,512]{1,0:T(8,128)(2,1)} %bitcast.7, ...), custom_call_target="tpu_custom_call" | custom-call | tf_op jit(solution)/shard_map/two_layers/pallas_call | solution.py:909
  46.4 0.9 %hand_out.1 = (bf16[128,512]{1,0:T(8,128)(2,1)}, f32[512,128]{1,0:T(8,128)}, f32[2,16]{1,0:T(2,128)}, f32[2,16,2,384]{3,2,1,0:T(2,128)}, f32[2,2,16,384]{3,2,1,0...) custom-call(bf16[128,512]{1,0:T(8,128)(2,1)S(1)} %get-tuple-element., ...), custom_call_target="tpu_custom_call" | custom-call | tf_op jit(solution)/shard_map/hand_out/pallas_call | solution.py:921

commit v4 on v3

--- a/solution.py
+++ b/solution.py
@@ -19,16 +19,20 @@
 SMALL = ("lengths", "norm_gain", "skip_gain", "glu_bias", "decay_log", "frequency", "step_log")
 
 PLAN = {
-    "e1": ((384, "zxy"), (256, "yzx"), (640, "xyz")),
-    "n1": ((256, "yzx"), (128, "xyz"), (256, "xyz"), (128, "yxz")),
-    "e0": ((384, "xyz"), (512, "yxz"), (384, "zxy")),
-    "n0": ((256, "xyz"), (512, "xyz")),
+    "e1": ((384, "ylhx"), (256, "lyxh"), (384, "ylhx"), (256, "zyx"),),
+    "n1": ((128, "xhly"), (384, "hlxy"), (128, "yxz"), (128, "xhly"),),
+    "e0": ((128, "lhyx"), (512, "xylh"), (384, "ylhx"), (256, "yxz"),),
+    "n0": ((256, "yxz"), (256, "xyz"), (256, "xyz"),),
 }
 SCHEDULE = (
-    "E1 Be10 Be11 Be12",
-    "N1 M0 e11 Bn10 Bn11 Bn12 e12 va E0 Be00 e10 Be01 Be02 n11 n10",
-    "e11 OUT n12 va N0 vb Bn00 e12 Bn01 Bn13 e00 e10 e11 vb e01 e02 n11 n00 n12 n10 va n13 e00 e12 n01 e10 vb"
-    " n00 n11 n12 e01 va e02 n10 n13 e00 n01 vb e02 n00 e01 n13 n01",
+    ("E1", "Be10", "Be11", "Be12", "Be13",),
+    ("N1", "V", "M0", "Bn12", "Bn11", "e11", "e10", "Bn10", "Bn13", "va", "E0", "Be02", "Be03", "Be00",)
+    + ("Be01", "e13", "e12", "n12", "n10", "e11",),
+    ("n13", "OUT", "va", "N0", "Bn00", "vb", "Bn01", "e10", "Bn02", "e02", "e00", "n11", "e01", "e03",)
+    + ("e12", "n12", "e13", "e11", "va", "vb", "n10", "n13", "n01", "n00", "e10", "e02", "n02", "e01",)
+    + ("e00", "n11", "vb", "e03", "e13", "n01", "e12", "n00", "e10", "e11", "n10", "n12", "n13", "n02",)
+    + ("va", "n11", "e02", "e00", "e01", "va", "e12", "vb", "n10", "e03", "n13", "n01", "n11", "vb",)
+    + ("e02", "n00", "e00", "n02", "e01",),
 )
 
 
@@ -324,11 +328,9 @@
                         dest[l, first * SUB : (first + 2) * SUB, at + c * N : at + (c + 1) * N] = both
                     held = None
 
-        def chunks(body, init=0, unroll=T // BLOCK):
-            def step(i, carry):
-                return body(pl.ds(pl.multiple_of(i * BLOCK, BLOCK), BLOCK), carry)
-
-            return lax.fori_loop(0, T // BLOCK, step, init, unroll=unroll)
+        def each(body):
+            for first in range(0, T, BLOCK):
+                body(slice(first, first + BLOCK))
 
         def turn(l, value_ref, lt, rt):
             for j in range(H // LANES):
@@ -351,7 +353,7 @@
                 left = jnp.concatenate([mine, rt[l].reshape(H // 2, LANES)], axis=1)
                 for c in range(first, last, 256):
                     g = mm(left, right[l, :, c : c + 256]).astype(LOW)
-                    dest[l, :, :, :, :, c : c + 256] = g.reshape(nz, 2, 2, BLOCK, 256)
+                    dest[l, :, :, :, :, :, c : c + 256] = g.reshape(2, 2, 2, 2, BLOCK, 256)
             else:
                 left = lt[l].reshape(H, LANES)
                 for c in range(first, last, 256):
@@ -359,59 +361,59 @@
                         left, right[l, 0:T, c : c + 256]
                     )
 
-        place = {"z": zz, "x": xx, "y": yy}
+        hh, ll = zz // 2, zz % 2
+        place = {"h": hh, "l": ll, "x": xx, "y": yy}
+
+        def z_peer(at):
+            return {"seq": at * 2 + xx}
 
         def peers(axis):
-            if axis == "x":
-                return [(1 - xx, x_peer)]
-            if axis == "y":
-                return [(1 - yy, y_peer)]
-            return [((zz + o) % nz, {"seq": ((zz + o) % nz) * 2 + xx}) for o in range(1, nz)]
+            if axis == "z":
+                others = [(zz + o) % nz for o in range(1, nz)]
+                return [({"h": to // 2, "l": to % 2}, z_peer(to)) for to in others]
+            device = {
+                "x": x_peer, "y": y_peer, "l": z_peer(hh * 2 + 1 - ll), "h": z_peer((1 - hh) * 2 + ll),
+            }
+            return [({axis: 1 - place[axis]}, device[axis])]
 
         class Part:
             def __init__(self, whole, first, last, order, got, sums):
                 self.ref, self.columns = whole, pl.ds(first, last - first)
-                self.axes, self.order, self.stage = ["z", "x", "y"], order, 0
+                self.axes, self.order, self.stage = "hlxy", order, 0
                 self.got, self.sums = got, sums
 
+            def index(self, at):
+                return tuple(at.get(a, slice(None)) for a in self.axes) + (slice(None), self.columns)
+
             def begin(self):
-                axis = self.order[self.stage]
-                self.where = self.axes.index(axis)
-                rest = len(self.axes) - 1 - self.where
-                self.copies = []
-                for i, (to, device) in enumerate(peers(axis)):
-                    index = (slice(None),) * self.where + (to,) + (slice(None),) * (rest + 1)
-                    self.copies.append(
-                        wire.send(self.ref.at[index + (self.columns,)], self.got[self.stage].at[i], device)
-                    )
+                self.copies = [
+                    wire.send(self.ref.at[self.index(at)], self.got[self.stage].at[i], device)
+                    for i, (at, device) in enumerate(peers(self.order[self.stage]))
+                ]
 
             def total(self):
                 for copy in self.copies:
                     copy.wait_recv()
                 axis, got = self.order[self.stage], self.got[self.stage]
-                mine, wait = place[axis], len(self.copies)
-                rest = [a for a in self.axes if a != axis]
+                gone = "hl" if axis == "z" else axis
+                mine = {a: place[a] for a in gone}
+                rest = "".join(a for a in self.axes if a not in gone)
                 if not rest:
-                    value = self.ref[mine, :, self.columns].astype(F32)
-                    for i in range(wait):
+                    value = self.ref[self.index(mine)].astype(F32)
+                    for i in range(len(self.copies)):
                         value = value + got[i].astype(F32)
                     return value
                 out = self.sums[self.stage]
-                for q in range(out.shape[0]):
-                    if self.where == 0:
-                        index = (mine, q)
+                for q in range(2):
+                    here = self.ref[self.index(mine | {rest[0]: q})]
+                    if len(self.copies) == 1:
+                        out[q] = here + got[0, q]
                     else:
-                        index = (q,) + (slice(None),) * (self.where - 1) + (mine,)
-                    index += (slice(None),) * (len(self.axes) - len(index) + 1) + (self.columns,)
-                    if wait == 1:
-                        out[q] = self.ref[index] + got[0, q]
-                    else:
-                        value = self.ref[index].astype(F32)
-                        for i in range(wait):
+                        value = here.astype(F32)
+                        for i in range(len(self.copies)):
                             value = value + got[i, q].astype(F32)
                         out[q] = value.astype(LOW)
-                self.ref, self.columns = out, slice(None)
-                self.axes = rest
+                self.ref, self.columns, self.axes = out, slice(None), rest
                 self.stage += 1
 
             def step(self):
@@ -448,8 +450,8 @@
         for l, name in z.plan:
             for i, (first, last, order) in enumerate(z.plan[l, name]):
                 label = f"{name}{l}{i}"
-                got = [getattr(r, f"got_{label}_{stage}") for stage in range(3)]
-                sums = [getattr(r, f"sum_{label}_{stage}") for stage in range(2)]
+                got = [getattr(r, f"got_{label}_{stage}") for stage in range(len(order))]
+                sums = [getattr(r, f"sum_{label}_{stage}") for stage in range(len(order) - 1)]
                 part = Part(getattr(r, f"p_{name}").at[l], first, last, order, got, sums)
                 part.sink = sink_of(l, name, first, last)
                 parts[label] = part
@@ -467,39 +469,44 @@
             r.step_log_grad[l : l + 1, :] = grads[2]
 
         class Vector:
-            def __init__(self, own, got, last):
-                self.own, self.got, self.last, self.stage = own, got, last, 0
+            def __init__(self, name):
+                self.own, self.got = getattr(r, name), getattr(r, name + "_in")
+                self.mid, self.mid_got = getattr(r, name + "_mid"), getattr(r, name + "_mid_in")
+                self.last, self.full = getattr(r, name + "_z"), getattr(r, name + "_full")
+                self.stage = 0
 
             def begin(self):
-                device = (sibling, x_peer, y_peer)[self.stage]
-                self.copy = wire.send(self.own.at[self.stage], self.got.at[self.stage], device)
+                self.copies = [wire.send(self.own, self.got, sibling)]
 
             def step(self):
-                if self.stage == 3:
-                    return self.sink(self.total())
-                self.copy.wait_recv()
-                total = self.own[self.stage] + self.got[self.stage]
-                self.stage += 1
-                if self.stage < 3:
-                    self.own[self.stage] = total
-                    return self.begin()
-                self.last[zz] = total
-                self.copies = [
-                    wire.send(self.last.at[zz], self.last.at[zz], {"seq": ((zz + o) % nz) * 2 + xx})
-                    for o in range(1, nz)
-                ]
-
-            def total(self):
                 for copy in self.copies:
                     copy.wait_recv()
-                value = self.last[0]
-                for o in range(1, nz):
-                    value = value + self.last[o]
-                return value
+                stage = self.stage
+                self.stage += 1
+                if stage == 0:
+                    self.mid[0] = self.own[core] + self.got[core]
+                    self.copies = [wire.send(self.mid.at[0], self.mid_got.at[0], x_peer)]
+                elif stage == 1:
+                    self.mid[1] = self.mid[0] + self.mid_got[0]
+                    self.copies = [wire.send(self.mid.at[1], self.mid_got.at[1], y_peer)]
+                elif stage == 2:
+                    self.last[zz] = self.mid[1] + self.mid_got[1]
+                    mine = self.last.at[zz]
+                    self.copies = [
+                        wire.send(mine, mine, z_peer((zz + o) % nz)) for o in range(1, nz)
+                    ]
+                elif stage == 3:
+                    total = self.last[0]
+                    for o in range(1, nz):
+                        total = total + self.last[o]
+                    self.full[core] = total
+                    mine = self.full.at[core]
+                    self.copies = [wire.send(mine, mine, sibling)]
+                else:
+                    self.sink(jnp.concatenate([self.full[0], self.full[1]], axis=0))
 
         if fused:
-            first_vector = Vector(r.vec_a, r.vec_a_in, r.vec_a_z)
-            last_vector = Vector(r.vec_b, r.vec_b_in, r.vec_b_z)
+            first_vector, last_vector = Vector("vec_a"), Vector("vec_b")
 
             def first_sink(sums):
                 mine["sums"] = owned(sums)
@@ -530,18 +537,13 @@
 
             lax.fori_loop(0, H // BLOCK, step, 0, unroll=4)
 
-        def forward_in(l):
-            def norm(rows, carry):
-                u = r.u[l, rows, :]
-                inv = lax.rsqrt(jnp.mean(u * u, axis=1, keepdims=True) + EPS)
-                normed = u * inv * gain(l)
-                r.inv[l, rows, :] = jnp.broadcast_to(inv, (BLOCK, LANES))
-                r.normed[l, rows, :] = normed
-                r.normed_low[l, rows, :] = normed.astype(LOW)
-                return carry
-
-            chunks(norm)
-            r.proj[l] = mm(r.normed_low[l], r.wi[l])
+        def normalize(l, rows, u):
+            inv = lax.rsqrt(jnp.mean(u * u, axis=1, keepdims=True) + EPS)
+            unit = u * inv
+            r.u[l, rows, :] = u
+            r.inv[l, rows, :] = jnp.broadcast_to(inv, (BLOCK, LANES))
+            r.unit[l, rows, :] = unit
+            r.normed_low[l, rows, :] = (unit * gain(l)).astype(LOW)
 
         def states(l, between):
             cre = jnp.broadcast_to(disc[l].coef_re, (SUB, N))
@@ -565,64 +567,63 @@
             sink.dest = (r.right_e, H)
             scan(l, l, l, False, source, between, sink)
 
-        def forward_out(l):
+        def sigmoid(value):
+            return 0.5 + 0.5 * jnp.tanh(0.5 * value)
+
+        def mix(l):
             waits["x", l] = share(l, r.right_e, H, CE)
             loads[f"wo{l}"].wait()
-            r.mixed[l] = mm(r.right_e[l, 0:T, H:CE], r.wo[l])
-
-            def gelu(rows, carry):
-                mixed = r.mixed[l, rows, :] + skip(l) * r.normed[l, rows, :]
-                th = jnp.tanh(GELU_A * (mixed + GELU_B * (mixed * mixed * mixed)))
+            r.tmp[...] = mm(r.right_e[l, 0:T, H:CE], r.wo[l])
+            through = skip(l) * gain(l)
+
+            def gelu(rows):
+                mixed = r.tmp[rows, :] + through * r.unit[l, rows, :]
+                th = jnp.tanh(mixed * (GELU_A + (GELU_A * GELU_B) * (mixed * mixed)))
+                half = 0.5 * mixed
+                act = half + half * th
                 r.mixed[l, rows, :] = mixed
                 r.th[l, rows, :] = th
-                r.act_low[l, rows, :] = (0.5 * mixed * (1.0 + th)).astype(LOW)
-                return carry
-
-            chunks(gelu)
+                r.act[l, rows, :] = act
+                r.act_low[l, rows, :] = act.astype(LOW)
+
+            each(gelu)
             loads[f"wg{l}"].wait()
-            r.gate[l] = mm(r.act_low[l], r.wg[l])
-
-            def out(rows, carry):
-                gate = jax.nn.sigmoid(r.gate[l, rows, :] + r.glu_bias[l : l + 1, :])
-                r.gate[l, rows, :] = gate
-                act = 0.5 * r.mixed[l, rows, :] * (1.0 + r.th[l, rows, :])
-                value = r.u[l, rows, :] + act * gate
-                if l == 0:
-                    r.u[1, rows, :] = value
-                else:
-                    r.act_out[rows, :] = value.astype(LOW)
-                return carry
-
-            chunks(out)
-
-        def backward_in(l):
-            def glu(rows, bias):
-                g = r.og[rows, :]
-                gate = r.gate[l, rows, :]
-                act = 0.5 * r.mixed[l, rows, :] * (1.0 + r.th[l, rows, :])
-                gate_grad = (g * act * gate * (1.0 - gate)).astype(LOW)
-                r.right_e[l, rows, 0:H] = gate_grad
-                wide_grad = gate_grad.astype(F32)
-                return bias + wide_grad[0:SUB] + wide_grad[SUB:BLOCK]
-
-            bias = chunks(glu, jnp.zeros((SUB, H), F32))
-            r.vec_a[0, 1 if l == 1 else 7, :] = jnp.sum(bias, axis=0)
+            r.tmp[...] = mm(r.act_low[l], r.wg[l])
+
+        def slope(l):
+            def gelu_slope(rows):
+                mixed, th = r.mixed[l, rows, :], r.th[l, rows, :]
+                inner = mixed * (0.5 * GELU_A + (1.5 * GELU_A * GELU_B) * (mixed * mixed))
+                r.slope[l, rows, :] = 0.5 + 0.5 * th + (1.0 - th * th) * inner
+
+            each(gelu_slope)
+
+        def adjoint_in(l):
             waits["gate", l] = share(l, r.right_e, 0, H)
             r.tmp[...] = mm_nt(r.right_e[l, 0:T, 0:H], r.wg[l])
 
-            def gelu(rows, total):
+            def gelu(rows):
                 act_grad = r.og[rows, :] * r.gate[l, rows, :] + r.tmp[rows, :]
-                mixed, th = r.mixed[l, rows, :], r.th[l, rows, :]
-                inner = GELU_A * (1.0 + 3.0 * GELU_B * mixed * mixed)
-                slope = 0.5 * (1.0 + th) + 0.5 * mixed * (1.0 - th * th) * inner
-                low = (act_grad * slope).astype(LOW)
-                r.mixed_grad[l, rows, :] = low
-                part = low.astype(F32) * r.normed[l, rows, :]
-                return total + part[0:SUB] + part[SUB:BLOCK]
-
-            total = chunks(gelu, jnp.zeros((SUB, H), F32))
-            r.vec_a[0, 0 if l == 1 else 6, :] = jnp.sum(total, axis=0)
+                r.mixed_grad[l, rows, :] = (act_grad * r.slope[l, rows, :]).astype(LOW)
+
+            each(gelu)
             r.xg[...] = mm_nt(r.mixed_grad[l], r.wo[l])
+
+        def beside_adjoint(l):
+            sums = [jnp.zeros((SUB, H), F32), jnp.zeros((SUB, H), F32)]
+
+            def add(rows):
+                grad = r.mixed_grad[l, rows, :].astype(F32)
+                r.mixed_skip[rows, :] = grad * (gain(l) * skip(l))
+                grad = grad * r.unit[l, rows, :]
+                gate_grad = r.right_e[l, rows, 0:H].astype(F32)
+                sums[0] = sums[0] + grad[0:SUB] + grad[SUB:BLOCK]
+                sums[1] = sums[1] + gate_grad[0:SUB] + gate_grad[SUB:BLOCK]
+
+            each(add)
+            at = 0 if l == 1 else 6
+            r.vec_a[at // 4, at % 4, :] = jnp.sum(sums[0], axis=0) * r.norm_gain[l, :]
+            r.vec_a[at // 4, at % 4 + 1, :] = jnp.sum(sums[1], axis=0)
 
         def adjoints(l, between):
             d = disc[l]
@@ -658,24 +659,18 @@
             for i in range(4):
                 value = jnp.sum(sums[i], axis=0, keepdims=True)
                 if l == 1:
-                    r.vec_a[0, 2 + i : 3 + i, :] = jnp.concatenate([value, pad], axis=1)
+                    row = (2 + i) % 4
+                    r.vec_a[(2 + i) // 4, row : row + 1, :] = jnp.concatenate([value, pad], axis=1)
                 else:
-                    r.vec_b[0, i : i + 1, :] = value
-
-        def backward_out(l):
-            r.tmp[...] = mm_nt(r.right_n[l, 0:T, :], r.wi[l])
-
-            def norm(rows, carry):
-                u = r.u[l, rows, :]
-                inv = wide(r.inv[l, rows, :], H)
-                ng = r.tmp[rows, :] + skip(l) * r.mixed_grad[l, rows, :].astype(F32)
-                v = gain(l) * ng
-                uv = jnp.mean(u * v, axis=1, keepdims=True)
-                out = r.og[rows, :] + inv * v - u * (inv * inv * inv) * uv
-                r.og[rows, :] = out
-                return carry
-
-            chunks(norm)
+                    r.vec_b[i // 2, i % 2 : i % 2 + 1, :] = value
+
+        def input_grad(l, rows):
+            v = gain(l) * r.tmp[rows, :] + r.mixed_skip[rows, :]
+            unit = r.unit[l, rows, :]
+            along = jnp.mean(unit * v, axis=1, keepdims=True)
+            out = r.og[rows, :] + wide(r.inv[l, rows, :], H) * (v - unit * along)
+            r.og[rows, :] = out
+            return out
 
         def early_products(l):
             dest = r.p_e if fused else None
@@ -691,28 +686,53 @@
         of = lax.broadcasted_iota(jnp.int32, (T, T), 1)
         to_rows = jnp.where(of == (at % SUB) * S + at // SUB, 1.0, 0.0).astype(LOW)
         to_time = jnp.where(at == (of % SUB) * S + of // SUB, 1.0, 0.0).astype(LOW)
-        r.u[0] = mm(to_rows, r.tok[...])
+        r.tmp[...] = mm(to_rows, r.tok[...])
+        each(lambda rows: normalize(0, rows, r.tmp[rows, :]))
         pack_in(0)
-        forward_in(0)
+        r.proj[0] = mm(r.normed_low[0], r.wi[0])
 
         def fill0():
             pack_in(1)
             waits["ln", 0] = turn(0, r.normed_low.at[0], r.lt_n, r.rt_n)
 
         states(0, fill0)
-        forward_out(0)
-
-        forward_in(1)
+        mix(0)
+
+        def between_layers(rows):
+            gate = sigmoid(r.tmp[rows, :] + r.glu_bias[0:1, :])
+            r.gate[0, rows, :] = gate
+            normalize(1, rows, r.u[0, rows, :] + r.act[0, rows, :] * gate)
+
+        each(between_layers)
+        r.proj[1] = mm(r.normed_low[1], r.wi[1])
 
         def fill1():
             waits["lg", 0] = turn(0, r.act_low.at[0], r.lt_g, r.rt_g)
             waits["ln", 1] = turn(1, r.normed_low.at[1], r.lt_n, r.rt_n)
             loads["cot"].wait()
             r.og[...] = mm(to_rows, r.cot[...])
+            for j in range(W // LANES):
+                r.wi_t[j * LANES : (j + 1) * LANES, :] = r.wi[1, :, j * LANES : (j + 1) * LANES].T
+            slope(0)
+
+            def gate_slope(rows):
+                gate = r.gate[0, rows, :]
+                r.gate_slope[rows, :] = r.act[0, rows, :] * (gate * (1.0 - gate))
+
+            each(gate_slope)
 
         states(1, fill1)
-        forward_out(1)
-        backward_in(1)
+        mix(1)
+        slope(1)
+
+        def last_gate(rows):
+            gate = sigmoid(r.tmp[rows, :] + r.glu_bias[1:2, :])
+            r.gate[1, rows, :] = gate
+            grad = r.og[rows, :] * (r.act[1, rows, :] * (gate * (1.0 - gate)))
+            r.right_e[1, rows, 0:H] = grad.astype(LOW)
+
+        each(last_gate)
+        adjoint_in(1)
 
         def run(tokens):
             for token in tokens:
@@ -723,8 +743,8 @@
                 elif fused:
                     parts[token].step()
 
-        def task_n1():
-            late_products(1)
+        def task_vec():
+            beside_adjoint(0)
             if fused:
                 first_vector.begin()
 
@@ -732,27 +752,41 @@
             waits["lo", 0] = turn(0, r.mixed_grad.at[0], r.lt_o, r.rt_o)
 
         def task_out():
-            backward_out(0)
+            r.tmp[...] = mm_nt(r.right_n[0, 0:T, :], r.wi[0])
+            each(lambda rows: input_grad(0, rows))
             for s in range(S):
                 for j in range(H // LANES):
                     into = pl.ds(s * (H // LANES) + j, SUB, stride=S * (H // LANES))
                     r.tokens_grad[into, :] = r.og[s * SUB : (s + 1) * SUB, j * LANES : (j + 1) * LANES]
 
         tasks = {
-            "N1": task_n1, "M0": task_m0, "E0": lambda: early_products(0),
+            "N1": lambda: late_products(1), "V": task_vec, "M0": task_m0, "E0": lambda: early_products(0),
             "N0": lambda: late_products(0), "OUT": task_out, "E1": lambda: early_products(1),
         }
 
         def fill2():
             waits["lo", 1] = turn(1, r.mixed_grad.at[1], r.lt_o, r.rt_o)
             waits["lg", 1] = turn(1, r.act_low.at[1], r.lt_g, r.rt_g)
+
+            def result(rows):
+                out = r.u[1, rows, :] + r.act[1, rows, :] * r.gate[1, rows, :]
+                r.act_out[rows, :] = out.astype(LOW)
+
+            each(result)
+            beside_adjoint(1)
+            run(z.schedule[0])
             r.activations[...] = mm(to_time, r.act_out[...]).astype(LOW)
-            run(z.schedule[0])
 
         adjoints(1, fill2)
         waits["pg", 1] = share(1, r.right_n, 0, W)
-        backward_out(1)
-        backward_in(0)
+        r.tmp[...] = mm(r.right_n[1, 0:T, :], r.wi_t[...])
+
+        def between_adjoints(rows):
+            grad = input_grad(1, rows)
+            r.right_e[0, rows, 0:H] = (grad * r.gate_slope[rows, :]).astype(LOW)
+
+        each(between_adjoints)
+        adjoint_in(0)
         adjoints(0, lambda: run(z.schedule[1]))
         waits["pg", 0] = share(0, r.right_n, 0, W)
         if fused:
@@ -760,8 +794,8 @@
         run(z.schedule[2])
 
         if not fused:
-            r.vector_sums[...] = r.vec_a[0]
-            r.last_vector_sums[...] = r.vec_b[0]
+            r.vector_sums[...] = r.vec_a[...]
+            r.last_vector_sums[...] = r.vec_b[...]
             wire.close()
             return
 
@@ -802,7 +836,7 @@
             plan[int(unit[1]), unit[0]] = cuts
         z = types.SimpleNamespace(
             T=T, H=H, N=N, S=T // SUB, nseq=nseq, nblk=nblk, fused=fused, plan=plan if fused else {},
-            schedule=[line.split() for line in SCHEDULE],
+            schedule=SCHEDULE,
         )
         any_space = pl.BlockSpec(memory_space=pl.ANY)
         vmem = pl.BlockSpec(memory_space=pltpu.VMEM)
@@ -839,20 +873,25 @@
         else:
             results |= {
                 "matrix_sums": ((2, H, CE + W), F32),
-                "vector_sums": ((8, H), F32),
-                "last_vector_sums": ((4, N), F32),
+                "vector_sums": ((2, 4, H), F32),
+                "last_vector_sums": ((2, 2, N), F32),
             }
         dma = pltpu.SemaphoreType.DMA
         scratch = {
             "wi_raw": pltpu.VMEM((2, H, 2, N), LOW),
             "wi": pltpu.VMEM((2, H, W), LOW),
+            "wi_t": pltpu.VMEM((W, H), LOW),
             "wo": pltpu.VMEM((2, W, H), LOW),
             "wg": pltpu.VMEM((2, H, H), LOW),
             "tok": pltpu.VMEM((T, H), LOW),
             "cot": pltpu.VMEM((T, H), LOW),
             "u": pltpu.VMEM((2, T, H), F32),
             "inv": pltpu.VMEM((2, T, LANES), F32),
-            "normed": pltpu.VMEM((2, T, H), F32),
+            "unit": pltpu.VMEM((2, T, H), F32),
+            "act": pltpu.VMEM((2, T, H), F32),
+            "slope": pltpu.VMEM((2, T, H), F32),
+            "gate_slope": pltpu.VMEM((T, H), F32),
+            "mixed_skip": pltpu.VMEM((T, H), F32),
             "normed_low": pltpu.VMEM((2, T, H), LOW),
             "proj": pltpu.VMEM((2, T, W), F32),
             "drive": pltpu.VMEM((T, W), F32),
@@ -875,8 +914,8 @@
             "seq_table": pltpu.VMEM((4, nseq, W), F32),
             "carry_out": pltpu.VMEM((4, 1, W), F32),
             "carry_in": pltpu.VMEM((4, nseq, 1, W), F32),
-            "vec_a": pltpu.VMEM((3, 8, H), F32),
-            "vec_b": pltpu.VMEM((3, 4, N), F32),
+            "vec_a": pltpu.VMEM((2, 4, H), F32),
+            "vec_b": pltpu.VMEM((2, 2, N), F32),
         }
         for name in "gon":
             scratch[f"lt_{name}"] = pltpu.VMEM((2, H // 32, 2, BLOCK, LANES), LOW)
@@ -884,19 +923,23 @@
         if fused:
             nz = nseq // 2
             for name, width in (("e", CE), ("n", W)):
-                scratch[f"p_{name}"] = pltpu.VMEM((2, nz, 2, 2, BLOCK, width), LOW)
+                scratch[f"p_{name}"] = pltpu.VMEM((2, 2, 2, 2, 2, BLOCK, width), LOW)
             for l, name in plan:
                 for i, (first, last, order) in enumerate(plan[l, name]):
-                    left = {"z": nz, "x": 2, "y": 2}
+                    left = 4
                     for stage, axis in enumerate(order):
-                        others = left.pop(axis) - 1
-                        shape = tuple(left.values()) + (BLOCK, last - first)
+                        others = 3 if axis == "z" else 1
+                        left -= 2 if axis == "z" else 1
+                        shape = (2,) * left + (BLOCK, last - first)
                         scratch[f"got_{name}{l}{i}_{stage}"] = pltpu.VMEM((others,) + shape, LOW)
                         if left:
                             scratch[f"sum_{name}{l}{i}_{stage}"] = pltpu.VMEM(shape, LOW)
-            for name, shape in (("a", (8, H)), ("b", (4, N))):
-                scratch[f"vec_{name}_in"] = pltpu.VMEM((3,) + shape, F32)
-                scratch[f"vec_{name}_z"] = pltpu.VMEM((nz,) + shape, F32)
+            for name, shape in (("vec_a", (4, H)), ("vec_b", (2, N))):
+                scratch[name + "_in"] = pltpu.VMEM((2,) + shape, F32)
+                scratch[name + "_mid"] = pltpu.VMEM((2,) + shape, F32)
+                scratch[name + "_mid_in"] = pltpu.VMEM((2,) + shape, F32)
+                scratch[name + "_z"] = pltpu.VMEM((nz,) + shape, F32)
+                scratch[name + "_full"] = pltpu.VMEM((2,) + shape, F32)
         links = LINKS if fused else 4 * (nseq - 1)
         scratch["send_sems"] = dma((links,))
         scratch["recv_sems"] = dma((links,))
@@ -938,7 +981,7 @@
         both = ("seq", "blk")
         sums = lax.psum_scatter(o.matrix_sums, both, scatter_dimension=1, tiled=True)
         rows = sums.shape[1]
-        vectors, last = lax.psum((o.vector_sums, o.last_vector_sums), both)
+        vectors, last = lax.psum((o.vector_sums.reshape(8, H), o.last_vector_sums.reshape(4, N)), both)
         start = lax.axis_index(both) * rows
 
         def owned(value, axis):

time: 47.5 us -> 45.4 us (0.956)
  Pallas kernels: 46.7 us -> 44.6 us
    pallas_call x1, Pallas kernels: 45.7 us -> 43.7 us  [on_device(): pl.pallas_call(make_kernel(names, z), out_shape=[(pltpu.VMEM if fused els...]
where the time goes in v4:
time: 45.4 us; the launch traced here: 45.3 us
  Pallas kernels  44.6 us (98%)
  between operations  0.66 us (1%)
    pallas_call x1, Pallas kernels, on_device(): pl.pallas_call(make_kernel(names, z), out_shape=[(pltpu.VMEM if fused els...  43.7 us
    pallas_call x1, Pallas kernels, on_device(): pl.pallas_call(hand_out, out_shape=[jax.ShapeDtypeStruct(*v) for v in res...  0.95 us

profile of v4, /device:TPU:0, one launch (start us, length us, event | category | flops | bytes accessed | tf_op | source)
XLA Modules:
  0.0 45.3 jit_solution(5599353300144670318)
XLA Ops:
  0.6 43.7 %two_layers.1 = (bf16[128,512]{1,0:T(8,128)(2,1)S(1)}, f32[512,128]{1,0:T(8,128)S(1)}, f32[2,16]{1,0:T(2,128)S(1)}, f32[2,16,2,384]{3,2,1,0:T(2,128)S(1)}, f32[2...) custom-call(bf16[128,512]{1,0:T(8,128)(2,1)} %bitcast.7, ...), custom_call_target="tpu_custom_call" | custom-call | tf_op jit(solution)/shard_map/two_layers/pallas_call | solution.py:952
  44.3 0.9 %hand_out.1 = (bf16[128,512]{1,0:T(8,128)(2,1)}, f32[512,128]{1,0:T(8,128)}, f32[2,16]{1,0:T(2,128)}, f32[2,16,2,384]{3,2,1,0:T(2,128)}, f32[2,2,16,384]{3,2,1,0...) custom-call(bf16[128,512]{1,0:T(8,128)(2,1)S(1)} %get-tuple-element., ...), custom_call_target="tpu_custom_call" | custom-call | tf_op jit(solution)/shard_map/hand_out/pallas_call | solution.py:964

commit v5 on v4

--- a/solution.py
+++ b/solution.py
@@ -18,21 +18,21 @@
 LINKS = 160
 SMALL = ("lengths", "norm_gain", "skip_gain", "glu_bias", "decay_log", "frequency", "step_log")
 
-PLAN = {
-    "e1": ((384, "ylhx"), (256, "lyxh"), (384, "ylhx"), (256, "zyx"),),
-    "n1": ((128, "xhly"), (384, "hlxy"), (128, "yxz"), (128, "xhly"),),
-    "e0": ((128, "lhyx"), (512, "xylh"), (384, "ylhx"), (256, "yxz"),),
-    "n0": ((256, "yxz"), (256, "xyz"), (256, "xyz"),),
-}
+E1, N1, E0, N0, SIDE0, OUT, VECTORS, VA, VB, LOCAL = range(10)
+SEND = 100
+PLAN = (
+    ((384, "ylhx"), (256, "lyxh"), (384, "ylhx"), (256, "zyx"),),
+    ((128, "xhly"), (384, "hlxy"), (128, "yxz"), (128, "xhly"),),
+    ((128, "lhyx"), (512, "xylh"), (384, "ylhx"), (256, "yxz"),),
+    ((256, "yxz"), (256, "xyz"), (256, "xyz"),),
+)
 SCHEDULE = (
-    ("E1", "Be10", "Be11", "Be12", "Be13",),
-    ("N1", "V", "M0", "Bn12", "Bn11", "e11", "e10", "Bn10", "Bn13", "va", "E0", "Be02", "Be03", "Be00",)
-    + ("Be01", "e13", "e12", "n12", "n10", "e11",),
-    ("n13", "OUT", "va", "N0", "Bn00", "vb", "Bn01", "e10", "Bn02", "e02", "e00", "n11", "e01", "e03",)
-    + ("e12", "n12", "e13", "e11", "va", "vb", "n10", "n13", "n01", "n00", "e10", "e02", "n02", "e01",)
-    + ("e00", "n11", "vb", "e03", "e13", "n01", "e12", "n00", "e10", "e11", "n10", "n12", "n13", "n02",)
-    + ("va", "n11", "e02", "e00", "e01", "va", "e12", "vb", "n10", "e03", "n13", "n01", "n11", "vb",)
-    + ("e02", "n00", "e00", "n02", "e01",),
+    (E1, SEND + 10, SEND + 11, SEND + 12, SEND + 13,),
+    (N1, VECTORS, SIDE0, SEND + 22, SEND + 21, 11, 10, SEND + 20, SEND + 23, VA, E0, SEND + 32, SEND + 33, SEND + 30,
+     SEND + 31, LOCAL, 13, 12, 22, 20, 11,),
+    (23, OUT, VA, N0, SEND + 40, VB, SEND + 41, 10, SEND + 42, 32, 30, 21, 31, 33, 12, 22, 13, 11, VA, VB, 20, 23, 41,
+     40, 10, 32, 42, 31, 30, 21, VB, 33, 13, 41, 12, 40, 10, 11, 20, 22, 23, 42, VA, 21, 32, 30, 31, VA, 12, VB, 20,
+     33, 23, 41, 21, VB, 32, 40, 30, 42, 31,),
 )
 
 
@@ -263,7 +263,7 @@
         for index in range(4):
             r.carry_in[index, 0] = jnp.zeros((1, W), F32)
 
-        def scan(index, l, way, conj, source, between, sink):
+        def scan(index, l, way, conj, source, between, finish):
             bre, bim = disc[l].bar_re, disc[l].bar_im
             sign = -1.0 if conj else 1.0
             bre = jnp.broadcast_to(bre, (SUB, N))
@@ -298,35 +298,51 @@
             ]
             edge = wide(k8 >= 1 if way == 0 else k8 < SUB - 1, N)
             shift = 1 if way == 0 else SUB - 1
-            yre = jnp.where(edge, pltpu.roll(yre, shift, 0), 0.0)
-            yim = jnp.where(edge, pltpu.roll(yim, shift, 0), 0.0)
-            between()
+            r.shifted[index, :, 0:N] = jnp.where(edge, pltpu.roll(yre, shift, 0), 0.0)
+            r.shifted[index, :, N:W] = jnp.where(edge, pltpu.roll(yim, shift, 0), 0.0)
+
+            def local():
+                yre, yim = r.shifted[index, :, 0:N], r.shifted[index, :, N:W]
+                qre, qim = r.chunk_table[index, :, 0:N], r.chunk_table[index, :, N:W]
+                for s in order:
+                    rows = slice(s * SUB, (s + 1) * SUB)
+                    dre, dim = source(s, False)
+                    yre, yim = advance(s, yre, yim, dre, dim)
+                    qre, qim = advance(s, qre, qim, 0.0, 0.0)
+                    for ref, re, im in ((r.local, yre, yim), (r.factor, qre, qim)):
+                        ref[index, rows, 0:N] = re
+                        ref[index, rows, N:W] = im
+                    if conj:
+                        cre, cim = disc[l].coef_re, -disc[l].coef_im
+                        for ref, pair in ((r.proj_local, (yre, yim)), (r.proj_factor, (qre, qim))):
+                            re, im = cmul(*pair, cre, cim)
+                            ref[rows, 0:N] = re
+                            ref[rows, N:W] = im
+
+            between(local)
             for copy in copies:
                 copy.wait_recv()
             got = r.carry_in[index, :, 0, :]
             gre, gim = cmul(got[:, 0:N], got[:, N:W], r.seq_table[index, :, 0:N], r.seq_table[index, :, N:W])
             gre = jnp.sum(gre, axis=0, keepdims=True)
             gim = jnp.sum(gim, axis=0, keepdims=True)
-            gre, gim = cmul(gre, gim, r.chunk_table[index, :, 0:N], r.chunk_table[index, :, N:W])
-            yre, yim = yre + gre, yim + gim
-            if not conj:
-                r.x_first[l, :, 0:N] = yre
-                r.x_first[l, :, N:W] = yim
-            held = None
-            for s in order:
-                dre, dim = source(s, False)
-                yre, yim = advance(s, yre, yim, dre, dim)
-                out = sink(s, yre, yim)
-                if held is None:
-                    held = out
-                else:
-                    pair = (held, out) if way == 0 else (out, held)
-                    first = s - 1 if way == 0 else s
-                    for c in range(2):
-                        both = jnp.concatenate([pair[0][c], pair[1][c]], axis=0).astype(LOW)
-                        dest, at = sink.dest
-                        dest[l, first * SUB : (first + 2) * SUB, at + c * N : at + (c + 1) * N] = both
-                    held = None
+            r.entered[index, :, 0:N] = gre
+            r.entered[index, :, N:W] = gim
+            base, factor, out, at = finish
+
+            def add(rows):
+                re, im = cmul(factor[rows, 0:N], factor[rows, N:W], gre, gim)
+                out[l, rows, at : at + N] = (base[rows, 0:N] + re).astype(LOW)
+                out[l, rows, at + N : at + W] = (base[rows, N:W] + im).astype(LOW)
+
+            each(add)
+
+        def state_at(index, rows):
+            re, im = cmul(
+                r.factor[index, rows, 0:N], r.factor[index, rows, N:W],
+                r.entered[index, :, 0:N], r.entered[index, :, N:W],
+            )
+            return r.local[index, rows, 0:N] + re, r.local[index, rows, N:W] + im
 
         def each(body):
             for first in range(0, T, BLOCK):
@@ -425,7 +441,7 @@
 
         along = {}
 
-        def sink_of(l, name, first, last):
+        def sink_of(l, whole, first, last):
             def early(value):
                 for low, high, out in (
                     (0, H, r.glu_weight_grad.at[l]),
@@ -444,17 +460,15 @@
                 weights = r.wi[l, own_rows, first:last].astype(F32)
                 along.setdefault(l, []).append(jnp.sum(value * weights, axis=1, keepdims=True))
 
-            return early if name == "e" else late
+            return early if whole == "p_e" else late
 
         parts = {}
-        for l, name in z.plan:
-            for i, (first, last, order) in enumerate(z.plan[l, name]):
-                label = f"{name}{l}{i}"
-                got = [getattr(r, f"got_{label}_{stage}") for stage in range(len(order))]
-                sums = [getattr(r, f"sum_{label}_{stage}") for stage in range(len(order) - 1)]
-                part = Part(getattr(r, f"p_{name}").at[l], first, last, order, got, sums)
-                part.sink = sink_of(l, name, first, last)
-                parts[label] = part
+        for l, whole, label, first, last, order in z.plan:
+            got = [getattr(r, f"got_{label}_{stage}") for stage in range(len(order))]
+            sums = [getattr(r, f"sum_{label}_{stage}") for stage in range(len(order) - 1)]
+            part = Part(getattr(r, whole).at[l], first, last, order, got, sums)
+            part.sink = sink_of(l, whole, first, last)
+            parts[label] = part
 
         device = seq * nblk + blk
         own_rows = pl.ds(pl.multiple_of(device * BLOCK, BLOCK), BLOCK)
@@ -518,7 +532,7 @@
             mine = {}
             first_vector.sink = first_sink
             last_vector.sink = lambda sums: out_vectors(0, [sums[i : i + 1] for i in range(4)])
-            parts["va"], parts["vb"] = first_vector, last_vector
+            parts[VA], parts[VB] = first_vector, last_vector
         waits = {}
 
         def gain(l):
@@ -558,14 +572,7 @@
                     return dre, dim
                 return r.drive[rows, 0:N], r.drive[rows, N:W]
 
-            def sink(s, yre, yim):
-                rows = slice(s * SUB, (s + 1) * SUB)
-                r.x[l, rows, 0:N] = yre
-                r.x[l, rows, N:W] = yim
-                return yre, yim
-
-            sink.dest = (r.right_e, H)
-            scan(l, l, l, False, source, between, sink)
+            scan(l, l, l, False, source, between, (r.local.at[l], r.factor.at[l], r.right_e, H))
 
         def sigmoid(value):
             return 0.5 + 0.5 * jnp.tanh(0.5 * value)
@@ -607,7 +614,7 @@
                 r.mixed_grad[l, rows, :] = (act_grad * r.slope[l, rows, :]).astype(LOW)
 
             each(gelu)
-            r.xg[...] = mm_nt(r.mixed_grad[l], r.wo[l])
+            r.xg[l] = mm_nt(r.mixed_grad[l], r.wo[l])
 
         def beside_adjoint(l):
             sums = [jnp.zeros((SUB, H), F32), jnp.zeros((SUB, H), F32)]
@@ -626,24 +633,22 @@
             r.vec_a[at // 4, at % 4 + 1, :] = jnp.sum(sums[1], axis=0)
 
         def adjoints(l, between):
-            d = disc[l]
-            cre = jnp.broadcast_to(d.coef_re, (SUB, N))
-            cim = jnp.broadcast_to(d.coef_im, (SUB, N))
-            way = 1 - l
-            sums = [jnp.zeros((SUB, N), F32) for _ in range(4)]
-
             def source(s, first):
                 rows = slice(s * SUB, (s + 1) * SUB)
-                return r.xg[rows, 0:N], r.xg[rows, N:W]
-
-            def sink(s, are, aim):
+                return r.xg[l, rows, 0:N], r.xg[l, rows, N:W]
+
+            scan(3 - l, l, 1 - l, True, source, between, (r.proj_local, r.proj_factor, r.right_n, 0))
+
+        def recurrence_sums(l):
+            sums = [jnp.zeros((SUB, N), F32) for _ in range(4)]
+            re, im = cmul(
+                r.chunk_table[l, :, 0:N], r.chunk_table[l, :, N:W],
+                r.entered[l, :, 0:N], r.entered[l, :, N:W],
+            )
+            xre, xim = r.shifted[l, :, 0:N] + re, r.shifted[l, :, N:W] + im
+            for s in range(S) if l == 0 else range(S - 1, -1, -1):
                 rows = slice(s * SUB, (s + 1) * SUB)
-                at = s - 1 if l == 0 else s + 1
-                if 0 <= at < S:
-                    old = slice(at * SUB, (at + 1) * SUB)
-                    xre, xim = r.x[l, old, 0:N], r.x[l, old, N:W]
-                else:
-                    xre, xim = r.x_first[l, :, 0:N], r.x_first[l, :, N:W]
+                are, aim = state_at(3 - l, rows)
                 k = wide(r.keep[l, rows, :], N)
                 xre, xim = xre * k, xim * k
                 pre, pim = r.proj[l, rows, 0:N], r.proj[l, rows, N:W]
@@ -651,10 +656,7 @@
                 sums[1] = sums[1] + (aim * xre - are * xim)
                 sums[2] = sums[2] + (are * pre + aim * pim)
                 sums[3] = sums[3] + (aim * pre - are * pim)
-                return cre * are + cim * aim, cre * aim - cim * are
-
-            sink.dest = (r.right_n, 0)
-            scan(3 - l, l, way, True, source, between, sink)
+                xre, xim = state_at(l, rows)
             pad = jnp.zeros((1, H - N), F32)
             for i in range(4):
                 value = jnp.sum(sums[i], axis=0, keepdims=True)
@@ -691,7 +693,8 @@
         pack_in(0)
         r.proj[0] = mm(r.normed_low[0], r.wi[0])
 
-        def fill0():
+        def fill0(local):
+            local()
             pack_in(1)
             waits["ln", 0] = turn(0, r.normed_low.at[0], r.lt_n, r.rt_n)
 
@@ -706,7 +709,8 @@
         each(between_layers)
         r.proj[1] = mm(r.normed_low[1], r.wi[1])
 
-        def fill1():
+        def fill1(local):
+            local()
             waits["lg", 0] = turn(0, r.act_low.at[0], r.lt_g, r.rt_g)
             waits["ln", 1] = turn(1, r.normed_low.at[1], r.lt_n, r.rt_n)
             loads["cot"].wait()
@@ -738,13 +742,14 @@
             for token in tokens:
                 if token in tasks:
                     tasks[token]()
-                elif fused and token[0] == "B":
-                    parts[token[1:]].begin()
+                elif fused and token >= SEND:
+                    parts[token - SEND].begin()
                 elif fused:
                     parts[token].step()
 
         def task_vec():
             beside_adjoint(0)
+            recurrence_sums(1)
             if fused:
                 first_vector.begin()
 
@@ -760,11 +765,11 @@
                     r.tokens_grad[into, :] = r.og[s * SUB : (s + 1) * SUB, j * LANES : (j + 1) * LANES]
 
         tasks = {
-            "N1": lambda: late_products(1), "V": task_vec, "M0": task_m0, "E0": lambda: early_products(0),
-            "N0": lambda: late_products(0), "OUT": task_out, "E1": lambda: early_products(1),
+            N1: lambda: late_products(1), VECTORS: task_vec, SIDE0: task_m0, E0: lambda: early_products(0),
+            N0: lambda: late_products(0), OUT: task_out, E1: lambda: early_products(1),
         }
 
-        def fill2():
+        def fill2(local):
             waits["lo", 1] = turn(1, r.mixed_grad.at[1], r.lt_o, r.rt_o)
             waits["lg", 1] = turn(1, r.act_low.at[1], r.lt_g, r.rt_g)
 
@@ -775,6 +780,7 @@
             each(result)
             beside_adjoint(1)
             run(z.schedule[0])
+            local()
             r.activations[...] = mm(to_time, r.act_out[...]).astype(LOW)
 
         adjoints(1, fill2)
@@ -787,8 +793,14 @@
 
         each(between_adjoints)
         adjoint_in(0)
-        adjoints(0, lambda: run(z.schedule[1]))
+
+        def fill3(local):
+            tasks[LOCAL] = local
+            run(z.schedule[1])
+
+        adjoints(0, fill3)
         waits["pg", 0] = share(0, r.right_n, 0, W)
+        recurrence_sums(0)
         if fused:
             last_vector.begin()
         run(z.schedule[2])
@@ -825,98 +837,101 @@
         CE = H + W
         assert streams == 1 and T == LANES and H == 512
         fused = nseq == 8 and nblk == 4
-        plan = {}
-        for unit, pieces in PLAN.items():
+        plan = []
+        for unit, pieces in enumerate(PLAN if fused else ()):
             first = 0
-            cuts = []
-            for width, order in pieces:
-                cuts.append((first, first + width, order))
+            for i, (width, order) in enumerate(pieces):
+                whole = ("p_e", "p_n")[unit % 2]
+                plan.append((1 - unit // 2, whole, 10 * (unit + 1) + i, first, first + width, order))
                 first += width
-            assert first == (CE if unit[0] == "e" else W)
-            plan[int(unit[1]), unit[0]] = cuts
+            assert first == (CE, W)[unit % 2]
         z = types.SimpleNamespace(
-            T=T, H=H, N=N, S=T // SUB, nseq=nseq, nblk=nblk, fused=fused, plan=plan if fused else {},
+            T=T, H=H, N=N, S=T // SUB, nseq=nseq, nblk=nblk, fused=fused, plan=plan,
             schedule=SCHEDULE,
         )
         any_space = pl.BlockSpec(memory_space=pl.ANY)
         vmem = pl.BlockSpec(memory_space=pltpu.VMEM)
-        operands = {
-            "tokens": (tokens.reshape(T, H), any_space),
-            "lengths": (lengths, any_space),
-            "norm_gain": (norm_gain, any_space),
-            "in_proj": (in_proj, any_space),
-            "out_proj": (out_proj.reshape(2, W, H), any_space),
-            "skip_gain": (skip_gain, any_space),
-            "glu_weight": (glu_weight, any_space),
-            "glu_bias": (glu_bias, any_space),
-            "decay_log": (decay_log, any_space),
-            "frequency": (frequency, any_space),
-            "step_log": (step_log, any_space),
-            "cotangent": (cotangent.reshape(T, H), any_space),
-        }
-        results = {
-            "activations": ((T, H), LOW),
-            "tokens_grad": ((T * H // LANES, LANES), F32),
-        }
+        operands = dict(
+            tokens=(tokens.reshape(T, H), any_space),
+            lengths=(lengths, any_space),
+            norm_gain=(norm_gain, any_space),
+            in_proj=(in_proj, any_space),
+            out_proj=(out_proj.reshape(2, W, H), any_space),
+            skip_gain=(skip_gain, any_space),
+            glu_weight=(glu_weight, any_space),
+            glu_bias=(glu_bias, any_space),
+            decay_log=(decay_log, any_space),
+            frequency=(frequency, any_space),
+            step_log=(step_log, any_space),
+            cotangent=(cotangent.reshape(T, H), any_space),
+        )
+        results = dict(
+            activations=((T, H), LOW),
+            tokens_grad=((T * H // LANES, LANES), F32),
+        )
         if fused:
-            results |= {
-                "norm_gain_grad": ((2, BLOCK), F32),
-                "in_proj_grad": ((2, BLOCK, 2, N), F32),
-                "out_proj_grad": ((2, 2, BLOCK, N), F32),
-                "skip_gain_grad": ((2, BLOCK), F32),
-                "glu_weight_grad": ((2, BLOCK, H), F32),
-                "glu_bias_grad": ((2, BLOCK), F32),
-                "decay_log_grad": ((2, N), F32),
-                "frequency_grad": ((2, N), F32),
-                "step_log_grad": ((2, N), F32),
-            }
+            results |= dict(
+                norm_gain_grad=((2, BLOCK), F32),
+                in_proj_grad=((2, BLOCK, 2, N), F32),
+                out_proj_grad=((2, 2, BLOCK, N), F32),
+                skip_gain_grad=((2, BLOCK), F32),
+                glu_weight_grad=((2, BLOCK, H), F32),
+                glu_bias_grad=((2, BLOCK), F32),
+                decay_log_grad=((2, N), F32),
+                frequency_grad=((2, N), F32),
+                step_log_grad=((2, N), F32),
+            )
         else:
-            results |= {
-                "matrix_sums": ((2, H, CE + W), F32),
-                "vector_sums": ((2, 4, H), F32),
-                "last_vector_sums": ((2, 2, N), F32),
-            }
+            results |= dict(
+                matrix_sums=((2, H, CE + W), F32),
+                vector_sums=((2, 4, H), F32),
+                last_vector_sums=((2, 2, N), F32),
+            )
         dma = pltpu.SemaphoreType.DMA
-        scratch = {
-            "wi_raw": pltpu.VMEM((2, H, 2, N), LOW),
-            "wi": pltpu.VMEM((2, H, W), LOW),
-            "wi_t": pltpu.VMEM((W, H), LOW),
-            "wo": pltpu.VMEM((2, W, H), LOW),
-            "wg": pltpu.VMEM((2, H, H), LOW),
-            "tok": pltpu.VMEM((T, H), LOW),
-            "cot": pltpu.VMEM((T, H), LOW),
-            "u": pltpu.VMEM((2, T, H), F32),
-            "inv": pltpu.VMEM((2, T, LANES), F32),
-            "unit": pltpu.VMEM((2, T, H), F32),
-            "act": pltpu.VMEM((2, T, H), F32),
-            "slope": pltpu.VMEM((2, T, H), F32),
-            "gate_slope": pltpu.VMEM((T, H), F32),
-            "mixed_skip": pltpu.VMEM((T, H), F32),
-            "normed_low": pltpu.VMEM((2, T, H), LOW),
-            "proj": pltpu.VMEM((2, T, W), F32),
-            "drive": pltpu.VMEM((T, W), F32),
-            "x": pltpu.VMEM((2, T, W), F32),
-            "x_first": pltpu.VMEM((2, SUB, W), F32),
-            "mixed": pltpu.VMEM((2, T, H), F32),
-            "th": pltpu.VMEM((2, T, H), F32),
-            "gate": pltpu.VMEM((2, T, H), F32),
-            "act_low": pltpu.VMEM((2, T, H), LOW),
-            "act_out": pltpu.VMEM((T, H), LOW),
-            "og": pltpu.VMEM((T, H), F32),
-            "tmp": pltpu.VMEM((T, H), F32),
-            "xg": pltpu.VMEM((T, W), F32),
-            "mixed_grad": pltpu.VMEM((2, T, H), LOW),
-            "right_e": pltpu.VMEM((2, 2 * T, CE), LOW),
-            "right_n": pltpu.VMEM((2, 2 * T, W), LOW),
-            "keep": pltpu.VMEM((2, T, LANES), F32),
-            "chunk_keep": pltpu.VMEM((2, 3, SUB, LANES), F32),
-            "chunk_table": pltpu.VMEM((4, SUB, W), F32),
-            "seq_table": pltpu.VMEM((4, nseq, W), F32),
-            "carry_out": pltpu.VMEM((4, 1, W), F32),
-            "carry_in": pltpu.VMEM((4, nseq, 1, W), F32),
-            "vec_a": pltpu.VMEM((2, 4, H), F32),
-            "vec_b": pltpu.VMEM((2, 2, N), F32),
-        }
+        scratch = dict(
+            wi_raw=pltpu.VMEM((2, H, 2, N), LOW),
+            wi=pltpu.VMEM((2, H, W), LOW),
+            wi_t=pltpu.VMEM((W, H), LOW),
+            wo=pltpu.VMEM((2, W, H), LOW),
+            wg=pltpu.VMEM((2, H, H), LOW),
+            tok=pltpu.VMEM((T, H), LOW),
+            cot=pltpu.VMEM((T, H), LOW),
+            u=pltpu.VMEM((2, T, H), F32),
+            inv=pltpu.VMEM((2, T, LANES), F32),
+            unit=pltpu.VMEM((2, T, H), F32),
+            act=pltpu.VMEM((2, T, H), F32),
+            slope=pltpu.VMEM((2, T, H), F32),
+            gate_slope=pltpu.VMEM((T, H), F32),
+            mixed_skip=pltpu.VMEM((T, H), F32),
+            normed_low=pltpu.VMEM((2, T, H), LOW),
+            proj=pltpu.VMEM((2, T, W), F32),
+            drive=pltpu.VMEM((T, W), F32),
+            shifted=pltpu.VMEM((4, SUB, W), F32),
+            local=pltpu.VMEM((4, T, W), F32),
+            factor=pltpu.VMEM((4, T, W), F32),
+            entered=pltpu.VMEM((4, 1, W), F32),
+            proj_local=pltpu.VMEM((T, W), F32),
+            proj_factor=pltpu.VMEM((T, W), F32),
+            mixed=pltpu.VMEM((2, T, H), F32),
+            th=pltpu.VMEM((2, T, H), F32),
+            gate=pltpu.VMEM((2, T, H), F32),
+            act_low=pltpu.VMEM((2, T, H), LOW),
+            act_out=pltpu.VMEM((T, H), LOW),
+            og=pltpu.VMEM((T, H), F32),
+            tmp=pltpu.VMEM((T, H), F32),
+            xg=pltpu.VMEM((2, T, W), F32),
+            mixed_grad=pltpu.VMEM((2, T, H), LOW),
+            right_e=pltpu.VMEM((2, 2 * T, CE), LOW),
+            right_n=pltpu.VMEM((2, 2 * T, W), LOW),
+            keep=pltpu.VMEM((2, T, LANES), F32),
+            chunk_keep=pltpu.VMEM((2, 3, SUB, LANES), F32),
+            chunk_table=pltpu.VMEM((4, SUB, W), F32),
+            seq_table=pltpu.VMEM((4, nseq, W), F32),
+            carry_out=pltpu.VMEM((4, 1, W), F32),
+            carry_in=pltpu.VMEM((4, nseq, 1, W), F32),
+            vec_a=pltpu.VMEM((2, 4, H), F32),
+            vec_b=pltpu.VMEM((2, 2, N), F32),
+        )
         for name in "gon":
             scratch[f"lt_{name}"] = pltpu.VMEM((2, H // 32, 2, BLOCK, LANES), LOW)
             scratch[f"rt_{name}"] = pltpu.VMEM((2, H // 32, BLOCK, LANES), LOW)
@@ -924,16 +939,15 @@
             nz = nseq // 2
             for name, width in (("e", CE), ("n", W)):
                 scratch[f"p_{name}"] = pltpu.VMEM((2, 2, 2, 2, 2, BLOCK, width), LOW)
-            for l, name in plan:
-                for i, (first, last, order) in enumerate(plan[l, name]):
-                    left = 4
-                    for stage, axis in enumerate(order):
-                        others = 3 if axis == "z" else 1
-                        left -= 2 if axis == "z" else 1
-                        shape = (2,) * left + (BLOCK, last - first)
-                        scratch[f"got_{name}{l}{i}_{stage}"] = pltpu.VMEM((others,) + shape, LOW)
-                        if left:
-                            scratch[f"sum_{name}{l}{i}_{stage}"] = pltpu.VMEM(shape, LOW)
+            for _, _, label, first, last, order in plan:
+                left = 4
+                for stage, axis in enumerate(order):
+                    others = 3 if axis == "z" else 1
+                    left -= 2 if axis == "z" else 1
+                    shape = (2,) * left + (BLOCK, last - first)
+                    scratch[f"got_{label}_{stage}"] = pltpu.VMEM((others,) + shape, LOW)
+                    if left:
+                        scratch[f"sum_{label}_{stage}"] = pltpu.VMEM(shape, LOW)
             for name, shape in (("vec_a", (4, H)), ("vec_b", (2, N))):
                 scratch[name + "_in"] = pltpu.VMEM((2,) + shape, F32)
                 scratch[name + "_mid"] = pltpu.VMEM((2,) + shape, F32)

time: 45.4 us -> 45.5 us (level)
  no operation moved by 1% of the time
where the time goes in v5:
time: 45.5 us; the launch traced here: 45.3 us
  Pallas kernels  44.7 us (98%)
  between operations  0.66 us (1%)
    pallas_call x1, Pallas kernels, on_device(): pl.pallas_call(make_kernel(names, z), out_shape=[(pltpu.VMEM if fused els...  43.7 us
    pallas_call x1, Pallas kernels, on_device(): pl.pallas_call(hand_out, out_shape=[jax.ShapeDtypeStruct(*v) for v in res...  0.95 us

profile of v5, /device:TPU:0, one launch (start us, length us, event | category | flops | bytes accessed | tf_op | source)
XLA Modules:
  0.0 45.3 jit_solution(4179446494961716652)
XLA Ops:
  0.6 43.7 %two_layers.1 = (bf16[128,512]{1,0:T(8,128)(2,1)S(1)}, f32[512,128]{1,0:T(8,128)S(1)}, f32[2,16]{1,0:T(2,128)S(1)}, f32[2,16,2,384]{3,2,1,0:T(2,128)S(1)}, f32[2...) custom-call(bf16[128,512]{1,0:T(8,128)(2,1)} %bitcast.7, ...), custom_call_target="tpu_custom_call" | custom-call | tf_op jit(solution)/shard_map/two_layers/pallas_call | solution.py:966
  44.4 0.9 %hand_out.1 = (bf16[128,512]{1,0:T(8,128)(2,1)}, f32[512,128]{1,0:T(8,128)}, f32[2,16]{1,0:T(2,128)}, f32[2,16,2,384]{3,2,1,0:T(2,128)}, f32[2,2,16,384]{3,2,1,0...) custom-call(bf16[128,512]{1,0:T(8,128)(2,1)S(1)} %get-tuple-element., ...), custom_call_target="tpu_custom_call" | custom-call | tf_op jit(solution)/shard_map/hand_out/pallas_call | solution.py:978

commit v6 on v5

--- a/solution.py
+++ b/solution.py
@@ -18,21 +18,21 @@
 LINKS = 160
 SMALL = ("lengths", "norm_gain", "skip_gain", "glu_bias", "decay_log", "frequency", "step_log")
 
-E1, N1, E0, N0, SIDE0, OUT, VECTORS, VA, VB, LOCAL = range(10)
+E1, N1, E0, N0, SIDE0, OUT, VECTORS, VA, VB, LOCAL, O0 = range(11)
 SEND = 100
 PLAN = (
-    ((384, "ylhx"), (256, "lyxh"), (384, "ylhx"), (256, "zyx"),),
-    ((128, "xhly"), (384, "hlxy"), (128, "yxz"), (128, "xhly"),),
-    ((128, "lhyx"), (512, "xylh"), (384, "ylhx"), (256, "yxz"),),
-    ((256, "yxz"), (256, "xyz"), (256, "xyz"),),
+    ((384, "xlhy"), (256, "zyx"), (256, "lyxh"), (384, "yxlh"),),
+    ((384, "zyx"), (384, "yhlx"),),
+    ((512, "xlyh"),),
+    ((256, "yxz"), (256, "xyz"), (128, "yxz"), (128, "xzy"),),
+    ((128, "lxh"), (128, "xlh"), (128, "lxh"), (384, "xz"),),
 )
 SCHEDULE = (
-    (E1, SEND + 10, SEND + 11, SEND + 12, SEND + 13,),
-    (N1, VECTORS, SIDE0, SEND + 22, SEND + 21, 11, 10, SEND + 20, SEND + 23, VA, E0, SEND + 32, SEND + 33, SEND + 30,
-     SEND + 31, LOCAL, 13, 12, 22, 20, 11,),
-    (23, OUT, VA, N0, SEND + 40, VB, SEND + 41, 10, SEND + 42, 32, 30, 21, 31, 33, 12, 22, 13, 11, VA, VB, 20, 23, 41,
-     40, 10, 32, 42, 31, 30, 21, VB, 33, 13, 41, 12, 40, 10, 11, 20, 22, 23, 42, VA, 21, 32, 30, 31, VA, 12, VB, 20,
-     33, 23, 41, 21, VB, 32, 40, 30, 42, 31,),
+    (E1, SEND + 20, SEND + 21, SEND + 22, SEND + 23,),
+    (N1, VECTORS, SIDE0, SEND + 31, 20, SEND + 30, 23, VA, 21, E0, SEND + 40, LOCAL, 22, 20, 23, O0,),
+    (SEND + 61, SEND + 63, VA, SEND + 60, SEND + 62, OUT, N0, VB, SEND + 51, SEND + 53, 31, SEND + 52, SEND + 50, 21,
+     40, 22, 30, 61, VA, 23, 20, 63, 60, VB, 62, 52, 51, 53, 50, 31, 21, 30, 40, 22, 60, 20, 62, 61, VB, 52, 51, 23,
+     VA, 50, 63, VA, 30, 31, 40, 53, 22, 60, 62, 61, VB, 52, 51, 31, VB, 50, 53, 40,),
 )
 
 
@@ -139,6 +139,7 @@
         nz = nseq // 2
         sibling = {"blk": yy * 2 + (1 - core)}
         y_peer = {"blk": (1 - yy) * 2 + core}
+        across = {"blk": (1 - yy) * 2 + (1 - core)}
         x_peer = {"seq": zz * 2 + (1 - xx)}
 
         loads = {}
@@ -163,7 +164,7 @@
         barrier = pltpu.get_barrier_semaphore()
         greeted = [{"seq": (seq + o) % nseq} for o in range(1, nseq)]
         if fused:
-            greeted += [sibling, y_peer]
+            greeted += [sibling, y_peer, across]
         for device in greeted:
             pl.semaphore_signal(barrier, inc=1, device_id=device, device_id_type=pl.DeviceIdType.MESH)
 
@@ -332,8 +333,8 @@
 
             def add(rows):
                 re, im = cmul(factor[rows, 0:N], factor[rows, N:W], gre, gim)
-                out[l, rows, at : at + N] = (base[rows, 0:N] + re).astype(LOW)
-                out[l, rows, at + N : at + W] = (base[rows, N:W] + im).astype(LOW)
+                out[rows, at : at + N] = (base[rows, 0:N] + re).astype(LOW)
+                out[rows, at + N : at + W] = (base[rows, N:W] + im).astype(LOW)
 
             each(add)
 
@@ -360,6 +361,39 @@
                 return wire.send(
                     ref.at[l, 0:T, first:last], ref.at[l, T : 2 * T, first:last], sibling
                 )
+
+        four = (sibling, y_peer, across)
+        block_of = ((yy, 1 - core), (1 - yy, core), (1 - yy, 1 - core))
+
+        def share_four(ref):
+            if fused:
+                return [wire.send(ref.at[0], ref.at[m + 1], device) for m, device in enumerate(four)]
+
+        def turn_four(value_ref):
+            for j in range(H // LANES):
+                block = value_ref[:, j * LANES : (j + 1) * LANES].T
+                r.lt_y[2 * j : 2 * j + 2] = block.reshape(2, 2, 2, BLOCK, LANES)
+            if fused:
+                return [
+                    wire.send(r.lt_y.at[:, block_of[m][0], block_of[m][1]], r.rt_y.at[m], device)
+                    for m, device in enumerate(four)
+                ]
+
+        def outer_four():
+            if fused:
+                for copy in waits["lo", 0] + waits["x", 0]:
+                    copy.wait_recv()
+                rows = H // 4
+                left = [r.lt_y[:, yy, core].reshape(rows, LANES)]
+                left += [r.rt_y[m].reshape(rows, LANES) for m in range(3)]
+                left = jnp.concatenate(left, axis=1)
+                for c in range(0, W, 256):
+                    g = mm(left, r.right_o[:, :, c : c + 256].reshape(4 * T, 256)).astype(LOW)
+                    r.p_o[0, :, :, :, :, c : c + 256] = g.reshape(2, 2, 2, BLOCK, 256)
+            else:
+                left = r.lt_y[...].reshape(H, LANES)
+                for c in range(0, W, 256):
+                    r.matrix_sums[0, :, H + c : H + c + 256] = mm(left, r.right_o[0, :, c : c + 256])
 
         def outer(l, lt, rt, right, first, last, dest, waits, at):
             if fused:
@@ -393,9 +427,9 @@
             return [({axis: 1 - place[axis]}, device[axis])]
 
         class Part:
-            def __init__(self, whole, first, last, order, got, sums):
+            def __init__(self, whole, axes, first, last, order, got, sums):
                 self.ref, self.columns = whole, pl.ds(first, last - first)
-                self.axes, self.order, self.stage = "hlxy", order, 0
+                self.axes, self.order, self.stage = axes, order, 0
                 self.got, self.sums = got, sums
 
             def index(self, at):
@@ -460,13 +494,15 @@
                 weights = r.wi[l, own_rows, first:last].astype(F32)
                 along.setdefault(l, []).append(jnp.sum(value * weights, axis=1, keepdims=True))
 
-            return early if whole == "p_e" else late
+            if whole == "p_o":
+                first, last = first + H, last + H
+            return late if whole == "p_n" else early
 
         parts = {}
         for l, whole, label, first, last, order in z.plan:
             got = [getattr(r, f"got_{label}_{stage}") for stage in range(len(order))]
             sums = [getattr(r, f"sum_{label}_{stage}") for stage in range(len(order) - 1)]
-            part = Part(getattr(r, whole).at[l], first, last, order, got, sums)
+            part = Part(getattr(r, whole).at[l], "hlx" if whole == "p_o" else "hlxy", first, last, order, got, sums)
             part.sink = sink_of(l, whole, first, last)
             parts[label] = part
 
@@ -559,6 +595,9 @@
             r.unit[l, rows, :] = unit
             r.normed_low[l, rows, :] = (unit * gain(l)).astype(LOW)
 
+        def low_states(l):
+            return (r.right_o.at[0], 0) if l == 0 else (r.right_e.at[l], H)
+
         def states(l, between):
             cre = jnp.broadcast_to(disc[l].coef_re, (SUB, N))
             cim = jnp.broadcast_to(disc[l].coef_im, (SUB, N))
@@ -572,15 +611,17 @@
                     return dre, dim
                 return r.drive[rows, 0:N], r.drive[rows, N:W]
 
-            scan(l, l, l, False, source, between, (r.local.at[l], r.factor.at[l], r.right_e, H))
+            scan(l, l, l, False, source, between, (r.local.at[l], r.factor.at[l], *low_states(l)))
 
         def sigmoid(value):
             return 0.5 + 0.5 * jnp.tanh(0.5 * value)
 
         def mix(l):
-            waits["x", l] = share(l, r.right_e, H, CE)
-            loads[f"wo{l}"].wait()
-            r.tmp[...] = mm(r.right_e[l, 0:T, H:CE], r.wo[l])
+            waits["x", l] = share(l, r.right_e, H, CE) if l == 1 else share_four(r.right_o)
+            if loads[f"wo{l}"] is not None:
+                loads[f"wo{l}"].wait()
+            x_low, at = low_states(l)
+            r.tmp[...] = mm(x_low[0:T, at : at + W], r.wo[l])
             through = skip(l) * gain(l)
 
             def gelu(rows):
@@ -614,7 +655,7 @@
                 r.mixed_grad[l, rows, :] = (act_grad * r.slope[l, rows, :]).astype(LOW)
 
             each(gelu)
-            r.xg[l] = mm_nt(r.mixed_grad[l], r.wo[l])
+            r.xg[l] = mm(r.mixed_grad[l], r.wo_t[l])
 
         def beside_adjoint(l):
             sums = [jnp.zeros((SUB, H), F32), jnp.zeros((SUB, H), F32)]
@@ -637,7 +678,7 @@
                 rows = slice(s * SUB, (s + 1) * SUB)
                 return r.xg[l, rows, 0:N], r.xg[l, rows, N:W]
 
-            scan(3 - l, l, 1 - l, True, source, between, (r.proj_local, r.proj_factor, r.right_n, 0))
+            scan(3 - l, l, 1 - l, True, source, between, (r.proj_local, r.proj_factor, r.right_n.at[l], 0))
 
         def recurrence_sums(l):
             sums = [jnp.zeros((SUB, N), F32) for _ in range(4)]
@@ -677,7 +718,8 @@
         def early_products(l):
             dest = r.p_e if fused else None
             outer(l, r.lt_g, r.rt_g, r.right_e, 0, H, dest, (waits["lg", l], waits["gate", l]), 0)
-            outer(l, r.lt_o, r.rt_o, r.right_e, H, CE, dest, (waits["lo", l], waits["x", l]), H)
+            if l == 1:
+                outer(l, r.lt_o, r.rt_o, r.right_e, H, CE, dest, (waits["lo", l], waits["x", l]), H)
 
         def late_products(l):
             dest = r.p_n if fused else None
@@ -718,6 +760,11 @@
             for j in range(W // LANES):
                 r.wi_t[j * LANES : (j + 1) * LANES, :] = r.wi[1, :, j * LANES : (j + 1) * LANES].T
             slope(0)
+            loads["wo1"].wait()
+            loads["wo1"] = None
+            for l in range(2):
+                for j in range(W // LANES):
+                    r.wo_t[l, :, j * LANES : (j + 1) * LANES] = r.wo[l, j * LANES : (j + 1) * LANES, :].T
 
             def gate_slope(rows):
                 gate = r.gate[0, rows, :]
@@ -754,7 +801,7 @@
                 first_vector.begin()
 
         def task_m0():
-            waits["lo", 0] = turn(0, r.mixed_grad.at[0], r.lt_o, r.rt_o)
+            waits["lo", 0] = turn_four(r.mixed_grad.at[0])
 
         def task_out():
             r.tmp[...] = mm_nt(r.right_n[0, 0:T, :], r.wi[0])
@@ -766,7 +813,7 @@
 
         tasks = {
             N1: lambda: late_products(1), VECTORS: task_vec, SIDE0: task_m0, E0: lambda: early_products(0),
-            N0: lambda: late_products(0), OUT: task_out, E1: lambda: early_products(1),
+            N0: lambda: late_products(0), OUT: task_out, O0: outer_four, E1: lambda: early_products(1),
         }
 
         def fill2(local):
@@ -841,10 +888,10 @@
         for unit, pieces in enumerate(PLAN if fused else ()):
             first = 0
             for i, (width, order) in enumerate(pieces):
-                whole = ("p_e", "p_n")[unit % 2]
-                plan.append((1 - unit // 2, whole, 10 * (unit + 1) + i, first, first + width, order))
+                whole = ("p_e", "p_n", "p_e", "p_n", "p_o")[unit]
+                plan.append((int(unit < 2), whole, 10 * (unit + 2) + i, first, first + width, order))
                 first += width
-            assert first == (CE, W)[unit % 2]
+            assert first == (CE, W, H, W, W)[unit]
         z = types.SimpleNamespace(
             T=T, H=H, N=N, S=T // SUB, nseq=nseq, nblk=nblk, fused=fused, plan=plan,
             schedule=SCHEDULE,
@@ -892,6 +939,7 @@
             wi_raw=pltpu.VMEM((2, H, 2, N), LOW),
             wi=pltpu.VMEM((2, H, W), LOW),
             wi_t=pltpu.VMEM((W, H), LOW),
+            wo_t=pltpu.VMEM((2, H, W), LOW),
             wo=pltpu.VMEM((2, W, H), LOW),
             wg=pltpu.VMEM((2, H, H), LOW),
             tok=pltpu.VMEM((T, H), LOW),
@@ -923,6 +971,9 @@
             mixed_grad=pltpu.VMEM((2, T, H), LOW),
             right_e=pltpu.VMEM((2, 2 * T, CE), LOW),
             right_n=pltpu.VMEM((2, 2 * T, W), LOW),
+            right_o=pltpu.VMEM((4, T, W), LOW),
+            lt_y=pltpu.VMEM((H // 64, 2, 2, BLOCK, LANES), LOW),
+            rt_y=pltpu.VMEM((3, H // 64, BLOCK, LANES), LOW),
             keep=pltpu.VMEM((2, T, LANES), F32),
             chunk_keep=pltpu.VMEM((2, 3, SUB, LANES), F32),
             chunk_table=pltpu.VMEM((4, SUB, W), F32),
@@ -937,10 +988,11 @@
             scratch[f"rt_{name}"] = pltpu.VMEM((2, H // 32, BLOCK, LANES), LOW)
         if fused:
             nz = nseq // 2
+            scratch["p_o"] = pltpu.VMEM((1, 2, 2, 2, BLOCK, W), LOW)
             for name, width in (("e", CE), ("n", W)):
                 scratch[f"p_{name}"] = pltpu.VMEM((2, 2, 2, 2, 2, BLOCK, width), LOW)
             for _, _, label, first, last, order in plan:
-                left = 4
+                left = len(order) + order.count("z")
                 for stage, axis in enumerate(order):
                     others = 3 if axis == "z" else 1
                     left -= 2 if axis == "z" else 1

time: 45.5 us -> 45.2 us (level)
  no operation moved by 1% of the time
where the time goes in v6:
time: 45.2 us; the launch traced here: 45.1 us
  Pallas kernels  44.4 us (98%)
  between operations  0.66 us (1%)
    pallas_call x1, Pallas kernels, on_device(): pl.pallas_call(make_kernel(names, z), out_shape=[(pltpu.VMEM if fused els...  43.5 us
    pallas_call x1, Pallas kernels, on_device(): pl.pallas_call(hand_out, out_shape=[jax.ShapeDtypeStruct(*v) for v in res...  0.95 us

profile of v6, /device:TPU:0, one launch (start us, length us, event | category | flops | bytes accessed | tf_op | source)
XLA Modules:
  0.0 45.1 jit_solution(5712769033445184210)
XLA Ops:
  0.6 43.5 %two_layers.1 = (bf16[128,512]{1,0:T(8,128)(2,1)S(1)}, f32[512,128]{1,0:T(8,128)S(1)}, f32[2,16]{1,0:T(2,128)S(1)}, f32[2,16,2,384]{3,2,1,0:T(2,128)S(1)}, f32[2...) custom-call(bf16[128,512]{1,0:T(8,128)(2,1)} %bitcast.7, ...), custom_call_target="tpu_custom_call" | custom-call | tf_op jit(solution)/shard_map/two_layers/pallas_call | solution.py:1018
  44.1 0.9 %hand_out.1 = (bf16[128,512]{1,0:T(8,128)(2,1)}, f32[512,128]{1,0:T(8,128)}, f32[2,16]{1,0:T(2,128)}, f32[2,16,2,384]{3,2,1,0:T(2,128)}, f32[2,2,16,384]{3,2,1,0...) custom-call(bf16[128,512]{1,0:T(8,128)(2,1)S(1)} %get-tuple-element., ...), custom_call_target="tpu_custom_call" | custom-call | tf_op jit(solution)/shard_map/hand_out/pallas_call | solution.py:1030

commit v7 on v6

--- a/solution.py
+++ b/solution.py
@@ -785,6 +785,15 @@
         each(last_gate)
         adjoint_in(1)
 
+        def out_gain(l, at):
+            gains = owned(jnp.concatenate([r.norm_gain[...], r.skip_gain[...], jnp.zeros((4, H), F32)], axis=0))
+            diagonal = lax.broadcasted_iota(jnp.int32, (BLOCK, BLOCK), 0) == lax.broadcasted_iota(
+                jnp.int32, (BLOCK, BLOCK), 1
+            )
+            total = jnp.sum(jnp.where(diagonal, sum(along[l]), 0.0), axis=0, keepdims=True)
+            total = total + gains[2 + l : 3 + l] * mine["sums"][at : at + 1]
+            r.norm_gain_grad[l : l + 1, :] = total / gains[l : l + 1]
+
         def run(tokens):
             for token in tokens:
                 if token in tasks:
@@ -850,7 +859,10 @@
         recurrence_sums(0)
         if fused:
             last_vector.begin()
-        run(z.schedule[2])
+        run(z.schedule[2][:-1])
+        if fused:
+            out_gain(1, 0)
+        run(z.schedule[2][-1:])
 
         if not fused:
             r.vector_sums[...] = r.vec_a[...]
@@ -858,14 +870,7 @@
             wire.close()
             return
 
-        gains = owned(jnp.concatenate([r.norm_gain[...], r.skip_gain[...], jnp.zeros((4, H), F32)], axis=0))
-        diagonal = lax.broadcasted_iota(jnp.int32, (BLOCK, BLOCK), 0) == lax.broadcasted_iota(
-            jnp.int32, (BLOCK, BLOCK), 1
-        )
-        for l, at in ((1, 0), (0, 6)):
-            total = jnp.sum(jnp.where(diagonal, sum(along[l]), 0.0), axis=0, keepdims=True)
-            total = total + gains[2 + l : 3 + l] * mine["sums"][at : at + 1]
-            r.norm_gain_grad[l : l + 1, :] = total / gains[l : l + 1]
+        out_gain(0, 6)
         wire.close()
 
     return kernel

time: 45.2 us -> 45.2 us (level)
  no operation moved by 1% of the time
where the time goes in v7:
time: 45.2 us; the launch traced here: 45.1 us
  Pallas kernels  44.4 us (98%)
  between operations  0.66 us (1%)
    pallas_call x1, Pallas kernels, on_device(): pl.pallas_call(make_kernel(names, z), out_shape=[(pltpu.VMEM if fused els...  43.5 us
    pallas_call x1, Pallas kernels, on_device(): pl.pallas_call(hand_out, out_shape=[jax.ShapeDtypeStruct(*v) for v in res...  0.95 us

profile of v7, /device:TPU:0, one launch (start us, length us, event | category | flops | bytes accessed | tf_op | source)
XLA Modules:
  0.0 45.1 jit_solution(1950166996204988830)
XLA Ops:
  0.6 43.5 %two_layers.1 = (bf16[128,512]{1,0:T(8,128)(2,1)S(1)}, f32[512,128]{1,0:T(8,128)S(1)}, f32[2,16]{1,0:T(2,128)S(1)}, f32[2,16,2,384]{3,2,1,0:T(2,128)S(1)}, f32[2...) custom-call(bf16[128,512]{1,0:T(8,128)(2,1)} %bitcast.7, ...), custom_call_target="tpu_custom_call" | custom-call | tf_op jit(solution)/shard_map/two_layers/pallas_call | solution.py:1023
  44.1 0.9 %hand_out.1 = (bf16[128,512]{1,0:T(8,128)(2,1)}, f32[512,128]{1,0:T(8,128)}, f32[2,16]{1,0:T(2,128)}, f32[2,16,2,384]{3,2,1,0:T(2,128)}, f32[2,2,16,384]{3,2,1,0...) custom-call(bf16[128,512]{1,0:T(8,128)(2,1)S(1)} %get-tuple-element., ...), custom_call_target="tpu_custom_call" | custom-call | tf_op jit(solution)/shard_map/hand_out/pallas_call | solution.py:1035
